TPU v7x, 256 devices: a whole 4x4x8 slice. The times are simulated.
256 devices in a mesh: dir: 2 (over y_lo), loop: 32 (over x, z), pb: 4 (over y_hi, core).
Axes of the slice: x: 4, y: 4 (y_hi: 2, y_lo: 2; y = y_hi * 2 + y_lo), z: 8, core: 2. Of those that a mesh axis runs over, the one named last changes fastest.
Arguments:
- embeddings: bfloat16 [2, 49152, 1024], P('dir', ('loop', 'pb')), may hold values from -24 to 24
- block_mask: int32 [32, 32], replicated, may hold values from 0 to 1, as said below
Outputs:
- soft_neighbour: bfloat16 [2, 49152, 1024], P('dir', ('loop', 'pb'))
- margin: float32 [2, 49152], P('dir', ('loop', 'pb'))
Inputs may be any that keep to these rules, and one draw needn't show every extreme that they name: block_mask[i, i] is 1; block_mask[i, j] is 0 where the cyclic distance between i and j, min((i - j) mod 32, (j - i) mod 32), exceeds 2; the number of scored blocks differs from row to row, and some row scores all 5 blocks of its band.
All inputs are finite; a program needn't handle non-finite values.
Results may differ from a plain program's by a relative error of at most 0.0045.
Values may be sent and summed in bfloat16 or wider, within the bound.
No kernel may reach another device: no remote copies, remote signals or barrier semaphores. Data moves between devices by JAX's collectives and lax.ppermute only.
A program may use at most 128 MiB of HBM per device.

v0:
```python
import math

import jax
import jax.numpy as jnp
from jax import lax
from jax.sharding import PartitionSpec as P

sharpness = 3.0


def shifted(value, axis, steps):
    count = lax.axis_size(axis)
    pairs = [(source, (source + steps) % count) for source in range(count)]
    return lax.ppermute(value, axis, pairs)


def partner(value, axis, apart):
    mask = 2**apart
    pairs = [(source, source ^ mask) for source in range(lax.axis_size(axis))]
    return lax.ppermute(value, axis, pairs)


def band_offsets(reach_blocks):
    offsets = [0]
    for stride in range(1, reach_blocks + 1):
        offsets = offsets + [stride, -stride]
    return offsets


def neighbours(source_rows, reach_blocks):
    fetched = {0: source_rows}
    for offset in band_offsets(reach_blocks)[1:]:
        fetched[offset] = shifted(source_rows, "loop", -offset)
    return [fetched[offset] for offset in band_offsets(reach_blocks)]


def absorb(softmax_state, own_rows, keys_here, scored, score_scale):
    running_max, denominator, weighted = softmax_state
    scores = (
        jnp.einsum("qd,kd->qk", own_rows, keys_here, preferred_element_type=jnp.float32)
        * score_scale
    )
    masked = jnp.where(scored, scores, -jnp.inf)
    new_max = jnp.maximum(running_max, jnp.max(masked, axis=1))
    weights = jnp.exp(masked - new_max[:, None])
    correction = jnp.exp(running_max - new_max)
    denominator = denominator * correction + jnp.sum(weights, axis=1)
    weighted = weighted * correction[:, None] + jnp.dot(
        weights.astype(jnp.bfloat16), keys_here, preferred_element_type=jnp.float32
    )
    return (new_max, denominator, weighted)


def shards(embeddings, block_mask):
    own_rows = embeddings[0]
    counterpart = partner(own_rows, "dir", 0)
    side_index = lax.axis_index("dir")
    loop_index = lax.axis_index("loop")
    loop_count = lax.axis_size("loop")
    reach_blocks = min(2, (loop_count - 1) // 2)
    offsets = band_offsets(reach_blocks)
    key_block = lax.all_gather(counterpart, "pb", axis=0, tiled=True)
    key_blocks = neighbours(key_block, reach_blocks)
    mask_line = jnp.where(
        side_index == 0,
        lax.dynamic_index_in_dim(block_mask, loop_index, 0, False),
        lax.dynamic_index_in_dim(block_mask, loop_index, 1, False),
    )
    block_ids = jnp.arange(loop_count, dtype=jnp.int32)
    query_count, feature_count = own_rows.shape
    score_scale = sharpness / math.sqrt(feature_count)
    softmax_state = (
        jnp.full((query_count,), -1e30, jnp.float32),
        jnp.zeros((query_count,), jnp.float32),
        jnp.zeros((query_count, feature_count), jnp.float32),
    )
    for position, offset in enumerate(offsets):
        target = (loop_index + offset) % loop_count
        tile_flag = jnp.sum(jnp.where(block_ids == target, mask_line, 0))
        keys_here = key_blocks[position]
        softmax_state = absorb(softmax_state, own_rows, keys_here, tile_flag > 0, score_scale)
    running_max, denominator, weighted = softmax_state
    blended = (weighted / denominator[:, None]).astype(jnp.bfloat16)
    own_lse = running_max + jnp.log(denominator)
    partner_lse = partner(own_lse, "dir", 0)
    pair_score = (
        jnp.sum(own_rows.astype(jnp.float32) * counterpart.astype(jnp.float32), axis=1)
        * score_scale
    )
    margin = pair_score - 0.5 * (own_lse + partner_lse)
    return (blended[None], margin[None])


def solution(mesh):
    placed = (P("dir", ("loop", "pb"), None), P())
    return jax.shard_map(
        shards,
        mesh=mesh,
        in_specs=placed,
        out_specs=(P("dir", ("loop", "pb"), None), P("dir", ("loop", "pb"))),
        check_vma=False,
    )
```

profile of v0, /device:TPU:1, one launch (start us, length us, event | category | flops | bytes accessed | tf_op | source)
XLA Modules:
  0.0 310.2 jit_solution(2487731769207991873)
XLA Ops:
  7.2 0.0 copy-start.1
  7.2 0.0 all-gather.2.cloned.1.call-start
  7.2 2.2 collective-permute-start
  9.4 16.3 %collective-permute-done = bf16[384,1024]{1,0:T(8,128)(2,1)S(1)} collective-permute-done((bf16[384,1024]{1,0:T(8,128)(2,1)}, bf16[384,1024]{1,0:T(8,128)(2,1)S(1)}, u32[]{:S(2)}, u32[]{:S(2)}) %collective-permute-start) | collective-permute-done | bytes 786464 | tf_op jit(solution)/shard_map/ppermute | solution.py:20
  25.8 0.0 copy-start
  25.8 0.9 copy-done
  26.6 0.0 all-gather.2.cloned.1.call-update
  26.7 40.5 %all-gather.2.cloned.1.call-done = bf16[1536,1024]{1,0:T(8,128)(2,1)} async-done(((bf16[384,1024]{1,0:T(8,128)(2,1)}), bf16[1536,1024]{1,0:T(8,128)(2,1)}) %all-gather.2.cloned.1.call-update) | async-done | bytes 3145744 | tf_op jit(solution)/shard_map/all_gather | solution.py:62
  67.2 2.3 collective-permute-start.4
  69.5 3.7 %collective-permute-start.3 = (bf16[1536,1024]{1,0:T(8,128)(2,1)}, bf16[1536,1024]{1,0:T(8,128)(2,1)}, u32[]{:S(2)}, u32[]{:S(2)}) collective-permute-start(bf16[1536,1024]{1,0:T(8,128)(2,1)} %all-gather.2.cloned.1.call-done), channel_id=1, source_target_pairs={{0,120},{4,124},{8,0},{12,4},{16,8},{20,12},{24,16},{28,20},{32,24... | collective-permute-start | bytes 9437192 | tf_op jit(solution)/shard_map/ppermute | solution.py:14
  73.2 1.0 collective-permute-start.2
  74.2 3.8 %collective-permute-start.1 = (bf16[1536,1024]{1,0:T(8,128)(2,1)}, bf16[1536,1024]{1,0:T(8,128)(2,1)}, u32[]{:S(2)}, u32[]{:S(2)}) collective-permute-start(bf16[1536,1024]{1,0:T(8,128)(2,1)} %all-gather.2.cloned.1.call-done), channel_id=1, source_target_pairs={{0,124},{4,0},{8,4},{12,8},{16,12},{20,16},{24,20},{28,24},{32,28}... | collective-permute-start | bytes 9437192 | tf_op jit(solution)/shard_map/ppermute | solution.py:14
  78.0 0.9 dynamic-slice_reduce_fusion
  78.9 1.4 fusion.34
  83.4 1.7 multiply_reduce_fusion
  85.1 0.0 copy-done.1
  85.1 3.4 %fusion.48 = (f32[384]{0:T(512)S(1)}, f32[384,1536]{1,0:T(8,128)S(1)}) fusion(bf16[1536,1024]{1,0:T(8,128)(2,1)} %all-gather.2.cloned.1.call-done, bf16[1,384,1024]{2,1,0:T(8,128)(2,1)S(1)} %copy-done.1, pred[]{:T(512)S(6)} %gt.15), kind=kOutput, calls=%fused_computation.70 | convolution fusion | flops 1209728640 | bytes 6292993 | tf_op jit(solution)/shard_map/qd,kd->qk/dot_general | solution.py:40
  88.5 121.9 %collective-permute-done.4 = bf16[1536,1024]{1,0:T(8,128)(2,1)} collective-permute-done((bf16[1536,1024]{1,0:T(8,128)(2,1)}, bf16[1536,1024]{1,0:T(8,128)(2,1)}, u32[]{:S(2)}, u32[]{:S(2)}) %collective-permute-start.4) | collective-permute-done | bytes 3145760 | tf_op jit(solution)/shard_map/ppermute | solution.py:14
  210.4 3.4 %fusion.44 = (f32[384]{0:T(512)S(1)}, f32[384,1536]{1,0:T(8,128)S(1)}) fusion(bf16[1536,1024]{1,0:T(8,128)(2,1)} %collective-permute-done.4, bf16[1,384,1024]{2,1,0:T(8,128)(2,1)S(1)} %copy-done.1, pred[]{:T(512)S(6)} %gt.19), kind=kOutput, calls=%fused_computation.66 | convolution fusion | flops 1209728640 | bytes 6292993 | tf_op jit(solution)/shard_map/qd,kd->qk/dot_general | solution.py:40
  213.8 0.0 collective-permute-done.3
  213.8 3.4 %fusion.45 = (f32[384]{0:T(512)S(1)}, f32[384,1536]{1,0:T(8,128)S(1)}) fusion(bf16[1536,1024]{1,0:T(8,128)(2,1)} %collective-permute-done.3, bf16[1,384,1024]{2,1,0:T(8,128)(2,1)S(1)} %copy-done.1, pred[]{:T(512)S(6)} %gt.18), kind=kOutput, calls=%fused_computation.67 | convolution fusion | flops 1209728640 | bytes 6292993 | tf_op jit(solution)/shard_map/qd,kd->qk/dot_general | solution.py:40
  217.2 59.3 %collective-permute-done.2 = bf16[1536,1024]{1,0:T(8,128)(2,1)} collective-permute-done((bf16[1536,1024]{1,0:T(8,128)(2,1)}, bf16[1536,1024]{1,0:T(8,128)(2,1)}, u32[]{:S(2)}, u32[]{:S(2)}) %collective-permute-start.2) | collective-permute-done | bytes 3145760 | tf_op jit(solution)/shard_map/ppermute | solution.py:14
  276.5 3.4 %fusion.46 = (f32[384]{0:T(512)S(1)}, f32[384,1536]{1,0:T(8,128)S(1)}) fusion(bf16[1536,1024]{1,0:T(8,128)(2,1)} %collective-permute-done.2, bf16[1,384,1024]{2,1,0:T(8,128)(2,1)S(1)} %copy-done.1, pred[]{:T(512)S(6)} %gt.17), kind=kOutput, calls=%fused_computation.68 | convolution fusion | flops 1209728640 | bytes 6292993 | tf_op jit(solution)/shard_map/qd,kd->qk/dot_general | solution.py:40
  279.9 0.0 collective-permute-done.1
  279.9 3.4 %fusion.47 = (f32[384]{0:T(512)S(1)}, f32[384,1536]{1,0:T(8,128)S(1)}) fusion(bf16[1536,1024]{1,0:T(8,128)(2,1)} %collective-permute-done.1, bf16[1,384,1024]{2,1,0:T(8,128)(2,1)S(1)} %copy-done.1, pred[]{:T(512)S(6)} %gt.16), kind=kOutput, calls=%fused_computation.69 | convolution fusion | flops 1209728640 | bytes 6292993 | tf_op jit(solution)/shard_map/qd,kd->qk/dot_general | solution.py:40
  283.3 0.5 fusion.13
  283.8 0.8 fusion.9
  284.6 0.8 fusion.5
  285.5 0.6 collective-permute-start.5
  286.1 3.4 %fusion.21 = f32[384,1024]{1,0:T(8,128)S(1)} fusion(bf16[1536,1024]{1,0:T(8,128)(2,1)} %collective-permute-done.1, f32[384,1536]{1,0:T(8,128)S(1)} %get-tuple-element.26, f32[384]{0:T(512)S(1)} %get-tuple-element.16), kind=kOutput, calls=%fused_computation.30 | convolution fusion | flops 1209139200 | bytes 7079424 | tf_op jit(solution)/shard_map/dot_general | solution.py:48
  289.4 3.4 %fusion.19 = f32[384,1024]{1,0:T(8,128)S(1)} fusion(bf16[1536,1024]{1,0:T(8,128)(2,1)} %collective-permute-done.2, f32[384,1536]{1,0:T(8,128)S(1)} %get-tuple-element.24, f32[384]{0:T(512)S(1)} %get-tuple-element.15), kind=kOutput, calls=%fused_computation.29 | convolution fusion | flops 1209139200 | bytes 7079424 | tf_op jit(solution)/shard_map/dot_general | solution.py:48
  292.8 0.0 copy-start.2
  292.8 3.5 %fusion.17 = f32[384,1024]{1,0:T(8,128)S(1)} fusion(bf16[1536,1024]{1,0:T(8,128)(2,1)} %collective-permute-done.3, f32[384,1536]{1,0:T(8,128)S(1)} %get-tuple-element.22, f32[384]{0:T(512)S(1)} %get-tuple-element.14), kind=kOutput, calls=%fused_computation.28 | convolution fusion | flops 1209139200 | bytes 7079424 | tf_op jit(solution)/shard_map/dot_general | solution.py:48
  296.4 0.0 copy-done.2
  296.4 1.5 fusion.23
  297.9 5.0 %fusion.30 = bf16[1,384,1024]{2,1,0:T(8,128)(2,1)} fusion(f32[384]{0:T(512)S(1)} %get-tuple-element.8, f32[384]{0:T(512)S(1)} %get-tuple-element.12, f32[384,1024]{1,0:T(8,128)S(1)} %fusion.17, f32[384]{0:T(512)S(1)} %get-tuple-element.11, f32[384,1024]{1,0:T(8,128)S(1)} %fusion.19, f32[384]{0:T(512)S(1)} %get-tuple-element.10, ...), kind=kOutput, calls=%fused_computation.37 | convolution fusion | flops 1213464576 | bytes 12593664 | tf_op jit(solution)/shard_map/dot_general | solution.py:48
  302.8 0.0 collective-permute-done.5
  302.8 0.6 broadcast_in_dim.45
  (3 shorter events, 0.0 us)
Async XLA Ops:
  7.2 77.9 %copy-start.1 = (bf16[1,384,1024]{2,1,0:T(8,128)(2,1)S(1)}, bf16[1,384,1024]{2,1,0:T(8,128)(2,1)}, u32[]{:S(2)}) copy-start(bf16[1,384,1024]{2,1,0:T(8,128)(2,1)} %param.2) | copy-start | bytes 2359300
  7.2 60.0 %all-gather.2.cloned.1.call-start = ((), (), s32[]{:S(2)}) async-start(), calls=%async_computation | async-start | bytes 3932160 | tf_op jit(solution)/shard_map/all_gather | solution.py:62
  7.2 18.5 %collective-permute-start = (bf16[384,1024]{1,0:T(8,128)(2,1)}, bf16[384,1024]{1,0:T(8,128)(2,1)S(1)}, u32[]{:S(2)}, u32[]{:S(2)}) collective-permute-start(bf16[384,1024]{1,0:T(8,128)(2,1)} %bitcast.36), channel_id=1, source_target_pairs={{0,128},{128,0},{1,129},{129,1},{2,130},{130,2},{3,131},{131,3},{4... | collective-permute-start | bytes 2359304 | tf_op jit(solution)/shard_map/ppermute | solution.py:20
  25.8 0.9 copy-start
  67.2 143.2 %collective-permute-start.4 = (bf16[1536,1024]{1,0:T(8,128)(2,1)}, bf16[1536,1024]{1,0:T(8,128)(2,1)}, u32[]{:S(2)}, u32[]{:S(2)}) collective-permute-start(bf16[1536,1024]{1,0:T(8,128)(2,1)} %all-gather.2.cloned.1.call-done), channel_id=1, source_target_pairs={{0,8},{4,12},{8,16},{12,20},{16,24},{20,28},{24,32},{28,36},{32,40... | collective-permute-start | bytes 9437192 | tf_op jit(solution)/shard_map/ppermute | solution.py:14
  69.5 144.3 %collective-permute-start.3 = (bf16[1536,1024]{1,0:T(8,128)(2,1)}, bf16[1536,1024]{1,0:T(8,128)(2,1)}, u32[]{:S(2)}, u32[]{:S(2)}) collective-permute-start(bf16[1536,1024]{1,0:T(8,128)(2,1)} %all-gather.2.cloned.1.call-done), channel_id=1, source_target_pairs={{0,120},{4,124},{8,0},{12,4},{16,8},{20,12},{24,16},{28,20},{32,24... | collective-permute-start | bytes 9437192 | tf_op jit(solution)/shard_map/ppermute | solution.py:14
  73.2 203.3 %collective-permute-start.2 = (bf16[1536,1024]{1,0:T(8,128)(2,1)}, bf16[1536,1024]{1,0:T(8,128)(2,1)}, u32[]{:S(2)}, u32[]{:S(2)}) collective-permute-start(bf16[1536,1024]{1,0:T(8,128)(2,1)} %all-gather.2.cloned.1.call-done), channel_id=1, source_target_pairs={{0,4},{4,8},{8,12},{12,16},{16,20},{20,24},{24,28},{28,32},{32,36}... | collective-permute-start | bytes 9437192 | tf_op jit(solution)/shard_map/ppermute | solution.py:14
  74.2 205.7 %collective-permute-start.1 = (bf16[1536,1024]{1,0:T(8,128)(2,1)}, bf16[1536,1024]{1,0:T(8,128)(2,1)}, u32[]{:S(2)}, u32[]{:S(2)}) collective-permute-start(bf16[1536,1024]{1,0:T(8,128)(2,1)} %all-gather.2.cloned.1.call-done), channel_id=1, source_target_pairs={{0,124},{4,0},{8,4},{12,8},{16,12},{20,16},{24,20},{28,24},{32,28}... | collective-permute-start | bytes 9437192 | tf_op jit(solution)/shard_map/ppermute | solution.py:14
  285.5 17.4 %collective-permute-start.5 = (f32[384]{0:T(512)S(1)}, f32[384]{0:T(512)S(1)}, u32[]{:S(2)}, u32[]{:S(2)}) collective-permute-start(f32[384]{0:T(512)S(1)} %get-tuple-element.7), channel_id=1, source_target_pairs={{0,128},{128,0},{1,129},{129,1},{2,130},{130,2},{3,131},{131,3},{4... | collective-permute-start | bytes 4616 | tf_op jit(solution)/shard_map/ppermute | solution.py:20
  292.8 3.5 %copy-start.2 = (bf16[1536,1024]{1,0:T(8,128)(2,1)S(1)}, bf16[1536,1024]{1,0:T(8,128)(2,1)}, u32[]{:S(2)}) copy-start(bf16[1536,1024]{1,0:T(8,128)(2,1)} %all-gather.2.cloned.1.call-done) | copy-start | bytes 9437188
Sparse Core Ops, SparseCore 0:
  26.8 40.3 all-gather.1
where the time goes:
time: 311 us; the launch traced here: 310 us
  waiting for transfers between devices  238 us (77%)
  matrix products  33.8 us (11%)
  between operations  17.2 us (6%)
  starting transfers between devices  13.6 us (4%)
  other arithmetic  5.22 us (2%)
    ppermute x4, waiting for transfers between devices, shifted(): return lax.ppermute(value, axis, pairs)  181 us
    all_gather x1, waiting for transfers between devices, shards(): key_block = lax.all_gather(counterpart, 'pb', axis=0, tiled=True)  40.5 us
    dot_general x5, matrix products, absorb(): jnp.einsum('qd,kd->qk', own_rows, keys_here, preferred_element_type=jnp.f...  17.1 us
    dot_general x5, matrix products, absorb(): jnp.dot(weights.astype(jnp.bfloat16), keys_here, preferred_element_type=j...  16.7 us
    ppermute x2, waiting for transfers between devices, partner(): return lax.ppermute(value, axis, pairs)  16.3 us
    ppermute x4, starting transfers between devices, shifted(): return lax.ppermute(value, axis, pairs)  10.8 us
  transfers between devices with their start and end apart: 7, of which 4 were waited for; matrix products, arithmetic and copies ran while one was open for 11% of the time, Pallas kernels for 0%

commit v1 on v0

v1 whole, which is shorter than its diff:
```python
import functools
import math

import jax
import jax.numpy as jnp
from jax import lax
from jax.experimental import pallas as pl
from jax.experimental.pallas import tpu as pltpu
from jax.sharding import PartitionSpec as P

sharpness = 3.0
AXES = ("dir", "loop", "pb")


def moved(value, route):
    sides, blocks, slabs = (lax.axis_size(axis) for axis in AXES)
    pairs = []
    for side in range(sides):
        for block in range(blocks):
            for slab in range(slabs):
                half, core = divmod(slab, 2)
                side_to, block_to, half_to, core_to = route(side, block, half, core)
                target = (side_to * blocks + block_to % blocks) * slabs + half_to * 2 + core_to
                pairs.append(((side * blocks + block) * slabs + slab, target))
    return lax.ppermute(value, AXES, pairs)


def across_near(side, block, half, core):
    return 1 - side, block, half, core


def across_far(side, block, half, core):
    return 1 - side, block, 1 - half, core


def sibling(side, block, half, core):
    return side, block, half, 1 - core


def ahead(side, block, half, core):
    return side, block + (1 if core == 0 else -1), half, core


def behind(side, block, half, core):
    return side, block - (1 if core == 0 else -1), half, core


def attend_kernel(slab_count, first, last, score_scale, *refs):
    refs = list(refs)
    flag_ref = None if first else refs.pop(0)
    query_ref = refs.pop(0)
    slab_refs = [refs.pop(0) for _ in range(slab_count)]
    if not first:
        max_in, total_in, sum_in = (refs.pop(0) for _ in range(3))
    if first:
        max_ref, total_ref, sum_ref, pair_ref = (refs.pop(0) for _ in range(4))
    elif last:
        blended_ref, log_ref = (refs.pop(0) for _ in range(2))
        max_ref, total_ref, sum_ref = (refs.pop(0) for _ in range(3))
    else:
        max_ref, total_ref, sum_ref = (refs.pop(0) for _ in range(3))
    key_ref, copy_sems = refs
    rows = query_ref.shape[0]
    copies = []
    for index, slab_ref in enumerate(slab_refs):
        copy = pltpu.make_async_copy(
            slab_ref, key_ref.at[pl.ds(index * rows, rows)], copy_sems.at[index]
        )
        copy.start()
        copies.append(copy)
    if first:
        max_ref[...] = jnp.full(max_ref.shape, -1e30, jnp.float32)
        total_ref[...] = jnp.zeros(total_ref.shape, jnp.float32)
        sum_ref[...] = jnp.zeros(sum_ref.shape, jnp.float32)
    else:
        max_ref[...] = max_in[...]
        total_ref[...] = total_in[...]
        sum_ref[...] = sum_in[...]

    def absorb(group):
        keys = key_ref[pl.ds(group * 2 * rows, 2 * rows), :]
        scores = (
            lax.dot_general(
                query_ref[...], keys, (((1,), (1,)), ((), ())), preferred_element_type=jnp.float32
            )
            * score_scale
        )
        old_max = max_ref[...]
        new_max = jnp.maximum(old_max, jnp.max(scores, axis=1, keepdims=True))
        weights = jnp.exp(scores - new_max)
        correction = jnp.exp(old_max - new_max)
        max_ref[...] = new_max
        total_ref[...] = total_ref[...] * correction + jnp.sum(weights, axis=1, keepdims=True)
        sum_ref[...] = sum_ref[...] * correction + jnp.dot(
            weights.astype(jnp.bfloat16), keys, preferred_element_type=jnp.float32
        )

    for group in range(slab_count // 2):
        copies[2 * group].wait()
        copies[2 * group + 1].wait()
        if first:
            absorb(group)
        else:
            pl.when(flag_ref[group] > 0)(functools.partial(absorb, group))
    if first:
        pair_ref[...] = (
            jnp.sum(
                query_ref[...].astype(jnp.float32) * key_ref[:rows, :].astype(jnp.float32),
                axis=1,
                keepdims=True,
            )
            * score_scale
        ).T
    if last:
        total = total_ref[...]
        blended_ref[...] = (sum_ref[...] / total).astype(jnp.bfloat16)
        log_ref[...] = (max_ref[...] + jnp.log(total)).T


def attend(query, slabs, score_scale, flags=None, state=None, last=False):
    rows, width = query.shape
    first = state is None
    count = len(slabs)
    vmem = pl.BlockSpec(memory_space=pltpu.VMEM)
    held = [
        jax.ShapeDtypeStruct((rows, 1), jnp.float32),
        jax.ShapeDtypeStruct((rows, 1), jnp.float32),
        jax.ShapeDtypeStruct((rows, width), jnp.float32),
    ]
    line = jax.ShapeDtypeStruct((1, rows), jnp.float32)
    scratch = [
        pltpu.VMEM((count * rows, width), jnp.bfloat16),
        pltpu.SemaphoreType.DMA((count,)),
    ]
    if first:
        out = held + [line]
    elif last:
        out = [jax.ShapeDtypeStruct((rows, width), jnp.bfloat16), line]
        scratch = [pltpu.VMEM(a.shape, a.dtype) for a in held] + scratch
    else:
        out = held
    in_specs = ([] if first else [pl.BlockSpec(memory_space=pltpu.SMEM)]) + [vmem]
    in_specs += [pl.BlockSpec(memory_space=pl.ANY)] * count
    in_specs += [] if first else [vmem] * 3
    operands = ([] if first else [flags]) + [query] + list(slabs) + ([] if first else list(state))
    return pl.pallas_call(
        functools.partial(attend_kernel, count, first, last, score_scale),
        out_shape=out,
        in_specs=in_specs,
        out_specs=[vmem] * len(out),
        scratch_shapes=scratch,
        compiler_params=pltpu.CompilerParams(vmem_limit_bytes=28 * 2**20),
        cost_estimate=pl.CostEstimate(
            flops=4 * count * rows * rows * width,
            bytes_accessed=2 * (count + 1) * rows * width + 8 * rows * width,
            transcendentals=count * rows * rows,
        ),
    )(*operands)


def shards(embeddings, block_mask):
    own = embeddings[0]
    score_scale = sharpness / math.sqrt(own.shape[1])
    side = lax.axis_index("dir")
    block = lax.axis_index("loop")
    core = lax.axis_index("pb") % 2
    count = lax.axis_size("loop")
    lines = jnp.where(side == 0, block_mask, block_mask.T)
    line = lax.dynamic_index_in_dim(lines, block, 0, False)
    step = jnp.where(core == 0, 1, -1)

    def flag(offset):
        return line[(block + offset * step) % count]

    near = moved(own, across_near)
    far = moved(own, across_far)
    ahead_1 = moved(own, ahead)
    near_sib = moved(near, sibling)
    far_sib = moved(far, sibling)
    ahead_2 = moved(ahead_1, ahead)

    behind_1 = [moved(near, behind), moved(far, behind)]
    cross_1 = [moved(ahead_1, across_near), moved(ahead_1, across_far)]
    max_0, total_0, sum_0, pair_score = attend(own, [near, far, near_sib, far_sib], score_scale)

    behind_2 = [moved(slab, behind) for slab in behind_1]
    cross_2 = [moved(ahead_2, across_near), moved(ahead_2, across_far)]
    behind_1_sib = [moved(slab, sibling) for slab in behind_1]
    cross_1_sib = [moved(slab, sibling) for slab in cross_1]
    state = attend(
        own,
        behind_1 + cross_1 + behind_1_sib + cross_1_sib,
        score_scale,
        jnp.stack([flag(1), flag(-1), flag(-1), flag(1)]),
        (max_0, total_0, sum_0),
    )
    behind_2_sib = [moved(slab, sibling) for slab in behind_2]
    cross_2_sib = [moved(slab, sibling) for slab in cross_2]
    state = attend(
        own, behind_2 + cross_2, score_scale, jnp.stack([flag(2), flag(-2)]), state
    )
    blended, own_log = attend(
        own,
        behind_2_sib + cross_2_sib,
        score_scale,
        jnp.stack([flag(-2), flag(2)]),
        state,
        last=True,
    )
    margin = pair_score - 0.5 * (own_log + moved(own_log, across_near))
    return (blended[None], margin)


def solution(mesh):
    placed = (P("dir", ("loop", "pb"), None), P())
    return jax.shard_map(
        shards,
        mesh=mesh,
        in_specs=placed,
        out_specs=(P("dir", ("loop", "pb"), None), P("dir", ("loop", "pb"))),
        check_vma=False,
    )
```

time: 311 us -> 121 us (0.39)
  waiting for transfers between devices: 238 us -> 33.7 us
  matrix products: 33.8 us -> 0 us
  Pallas kernels: 0 us -> 30.8 us
  starting transfers between devices: 13.6 us -> 42.7 us
  between operations: 17.2 us -> 0.81 us
  local copies, waits for them, and re-layouts: 2.35 us -> 7.16 us
    ppermute x6 -> x23, waiting for transfers between devices: 198 us -> 33.7 us  [moved(): return lax.ppermute(value, AXES, pairs)]
    all_gather x1 -> x0, waiting for transfers between devices: 40.5 us -> none  [shards(): key_block = lax.all_gather(counterpart, 'pb', axis=0, tiled=True)]
    dot_general x10 -> x0, matrix products: 33.8 us -> none  [the longest x5 17.1 us: absorb(): jnp.einsum('qd,kd->qk', own_rows, keys_here, preferred_element_type=jnp.f...]
    pallas_call x0 -> x4, Pallas kernels: none -> 30.8 us  [attend(): pl.pallas_call(functools.partial(attend_kernel, count, first, last, score...]
    ppermute x6 -> x23, starting transfers between devices: 13.6 us -> 42.7 us  [moved(): return lax.ppermute(value, AXES, pairs)]
    unnamed x6 -> x19, local copies, waits for them, and re-layouts: 0.89 us -> 6.49 us
    reduce_sum x5 -> x0, other arithmetic: 5.18 us -> none  [the longest x3 2.09 us: absorb(): denominator = denominator * correction + jnp.sum(weights, axis=1)]
    another operation x0 -> x3, other arithmetic: none -> 4.08 us  [the longest x1 1.37 us: shards(): jnp.stack([flag(-2), flag(2)])]
  transfers between devices with their start and end apart: 7 -> 23, of which waited for: 4 -> 7; matrix products, arithmetic and copies ran while one was open for 11% -> 5% of each run, Pallas kernels for 0% -> 20%
where the time goes in v1:
time: 121 us; the launch traced here: 120 us
  starting transfers between devices  42.7 us (35%)
  waiting for transfers between devices  33.7 us (28%)
  Pallas kernels  30.8 us (25%)
  local copies, waits for them, and re-layouts  7.16 us (6%)
  other arithmetic  5.37 us (4%)
    ppermute x23, starting transfers between devices, moved(): return lax.ppermute(value, AXES, pairs)  42.7 us
    ppermute x23, waiting for transfers between devices, moved(): return lax.ppermute(value, AXES, pairs)  33.7 us
    pallas_call x4, Pallas kernels, attend(): pl.pallas_call(functools.partial(attend_kernel, count, first, last, score...  30.8 us
    unnamed x19, local copies, waits for them, and re-layouts  6.49 us
  transfers between devices with their start and end apart: 23, of which 7 were waited for; matrix products, arithmetic and copies ran while one was open for 5% of the time, Pallas kernels for 20%

profile of v1, /device:TPU:1, one launch (start us, length us, event | category | flops | bytes accessed | tf_op | source)
XLA Modules:
  0.0 120.5 jit_solution(18396328880468978014)
XLA Ops:
  0.6 2.2 %collective-permute-start = (bf16[384,1024]{1,0:T(8,128)(2,1)}, bf16[384,1024]{1,0:T(8,128)(2,1)S(1)}, u32[]{:S(2)}, u32[]{:S(2)}) collective-permute-start(bf16[384,1024]{1,0:T(8,128)(2,1)} %bitcast.8), channel_id=1, source_target_pairs={{0,128},{1,129},{2,130},{3,131},{4,132},{5,133},{6,134},{7,135},{8... | collective-permute-start | bytes 2359304 | tf_op jit(solution)/shard_map/ppermute | solution.py:25
  2.8 1.9 %collective-permute-start.4 = (bf16[384,1024]{1,0:T(8,128)(2,1)}, bf16[384,1024]{1,0:T(8,128)(2,1)S(1)}, u32[]{:S(2)}, u32[]{:S(2)}) collective-permute-start(bf16[384,1024]{1,0:T(8,128)(2,1)} %bitcast.9), channel_id=1, source_target_pairs={{0,130},{1,131},{2,128},{3,129},{4,134},{5,135},{6,132},{7,133},{8... | collective-permute-start | bytes 2359304 | tf_op jit(solution)/shard_map/ppermute | solution.py:25
  4.7 7.8 %collective-permute-start.8 = (bf16[384,1024]{1,0:T(8,128)(2,1)}, bf16[384,1024]{1,0:T(8,128)(2,1)S(1)}, u32[]{:S(2)}, u32[]{:S(2)}) collective-permute-start(bf16[384,1024]{1,0:T(8,128)(2,1)} %bitcast.10), channel_id=1, source_target_pairs={{0,4},{1,125},{2,6},{3,127},{4,8},{5,1},{6,10},{7,3},{8,12},{9,5},... | collective-permute-start | bytes 2359304 | tf_op jit(solution)/shard_map/ppermute | solution.py:25
  12.5 6.7 %collective-permute-done.refs_1_ = bf16[384,1024]{1,0:T(8,128)(2,1)S(1)} collective-permute-done((bf16[384,1024]{1,0:T(8,128)(2,1)}, bf16[384,1024]{1,0:T(8,128)(2,1)S(1)}, u32[]{:S(2)}, u32[]{:S(2)}) %collective-permute-start) | collective-permute-done | bytes 786464 | tf_op jit(solution)/shard_map/ppermute | solution.py:25
  19.2 2.4 %collective-permute-start.20 = (bf16[384,1024]{1,0:T(8,128)(2,1)S(1)}, bf16[384,1024]{1,0:T(8,128)(2,1)S(1)}, u32[]{:S(2)}, u32[]{:S(2)}) collective-permute-start(bf16[384,1024]{1,0:T(8,128)(2,1)S(1)} %collective-permute-done.refs_1_), channel_id=1, source_target_pairs={{0,1},{1,0},{2,3},{3,2},{4,5},{5,4},{6,7},{7,6},{8,9},{9,8},{10,11... | collective-permute-start | bytes 2359304 | tf_op jit(solution)/shard_map/ppermute | solution.py:25
  21.6 0.5 collective-permute-done.4.refs_2_
  22.1 2.1 %collective-permute-start.21 = (bf16[384,1024]{1,0:T(8,128)(2,1)S(1)}, bf16[384,1024]{1,0:T(8,128)(2,1)S(1)}, u32[]{:S(2)}, u32[]{:S(2)}) collective-permute-start(bf16[384,1024]{1,0:T(8,128)(2,1)S(1)} %collective-permute-done.4.refs_2_), channel_id=1, source_target_pairs={{0,1},{1,0},{2,3},{3,2},{4,5},{5,4},{6,7},{7,6},{8,9},{9,8},{10,11... | collective-permute-start | bytes 2359304 | tf_op jit(solution)/shard_map/ppermute | solution.py:25
  24.2 1.6 %collective-permute-start.1 = (bf16[384,1024]{1,0:T(8,128)(2,1)S(1)}, bf16[384,1024]{1,0:T(8,128)(2,1)S(1)}, u32[]{:S(2)}, u32[]{:S(2)}) collective-permute-start(bf16[384,1024]{1,0:T(8,128)(2,1)S(1)} %collective-permute-done.refs_1_), channel_id=1, source_target_pairs={{0,124},{1,5},{2,126},{3,7},{4,0},{5,9},{6,2},{7,11},{8,4},{9,13},... | collective-permute-start | bytes 2359304 | tf_op jit(solution)/shard_map/ppermute | solution.py:25
  25.9 1.6 %collective-permute-start.5 = (bf16[384,1024]{1,0:T(8,128)(2,1)S(1)}, bf16[384,1024]{1,0:T(8,128)(2,1)}, u32[]{:S(2)}, u32[]{:S(2)}) collective-permute-start(bf16[384,1024]{1,0:T(8,128)(2,1)S(1)} %collective-permute-done.4.refs_2_), channel_id=1, source_target_pairs={{0,124},{1,5},{2,126},{3,7},{4,0},{5,9},{6,2},{7,11},{8,4},{9,13},... | collective-permute-start | bytes 2359304 | tf_op jit(solution)/shard_map/ppermute | solution.py:25
  27.5 0.0 collective-permute-done.8
  27.5 0.0 collective-permute-start.14
  27.5 0.0 collective-permute-done.20.refs_3_
  27.5 2.0 %collective-permute-start.15 = (bf16[384,1024]{1,0:T(8,128)(2,1)S(1)}, bf16[384,1024]{1,0:T(8,128)(2,1)S(1)}, u32[]{:S(2)}, u32[]{:S(2)}) collective-permute-start(bf16[384,1024]{1,0:T(8,128)(2,1)S(1)} %collective-permute-done.8), channel_id=1, source_target_pairs={{0,130},{1,131},{2,128},{3,129},{4,134},{5,135},{6,132},{7,133},{8... | collective-permute-start | bytes 2359304 | tf_op jit(solution)/shard_map/ppermute | solution.py:25
  29.5 0.0 collective-permute-done.21.refs_4_
  29.5 0.9 copy-done.1
  30.4 4.6 %collective-permute-start.9 = (bf16[384,1024]{1,0:T(8,128)(2,1)S(1)}, bf16[384,1024]{1,0:T(8,128)(2,1)}, u32[]{:S(2)}, u32[]{:S(2)}) collective-permute-start(bf16[384,1024]{1,0:T(8,128)(2,1)S(1)} %collective-permute-done.8), channel_id=1, source_target_pairs={{0,4},{1,125},{2,6},{3,127},{4,8},{5,1},{6,10},{7,3},{8,12},{9,5},... | collective-permute-start | bytes 2359304 | tf_op jit(solution)/shard_map/ppermute | solution.py:25
  35.0 6.3 %collective-permute-done.1.refs_2_ = bf16[384,1024]{1,0:T(8,128)(2,1)S(1)} collective-permute-done((bf16[384,1024]{1,0:T(8,128)(2,1)S(1)}, bf16[384,1024]{1,0:T(8,128)(2,1)S(1)}, u32[]{:S(2)}, u32[]{:S(2)}) %collective-permute-start.1) | collective-permute-done | bytes 786464 | tf_op jit(solution)/shard_map/ppermute | solution.py:25
  41.4 6.2 %collective-permute-start.16 = (bf16[384,1024]{1,0:T(8,128)(2,1)S(1)}, bf16[384,1024]{1,0:T(8,128)(2,1)S(1)}, u32[]{:S(2)}, u32[]{:S(2)}) collective-permute-start(bf16[384,1024]{1,0:T(8,128)(2,1)S(1)} %collective-permute-done.1.refs_2_), channel_id=1, source_target_pairs={{0,1},{1,0},{2,3},{3,2},{4,5},{5,4},{6,7},{7,6},{8,9},{9,8},{10,11... | collective-permute-start | bytes 2359304 | tf_op jit(solution)/shard_map/ppermute | solution.py:25
  47.5 9.7 %collective-permute-done.5.refs_3_ = bf16[384,1024]{1,0:T(8,128)(2,1)} collective-permute-done((bf16[384,1024]{1,0:T(8,128)(2,1)S(1)}, bf16[384,1024]{1,0:T(8,128)(2,1)}, u32[]{:S(2)}, u32[]{:S(2)}) %collective-permute-start.5) | collective-permute-done | bytes 786464 | tf_op jit(solution)/shard_map/ppermute | solution.py:25
  57.2 1.4 %collective-permute-start.17 = (bf16[384,1024]{1,0:T(8,128)(2,1)}, bf16[384,1024]{1,0:T(8,128)(2,1)S(1)}, u32[]{:S(2)}, u32[]{:S(2)}) collective-permute-start(bf16[384,1024]{1,0:T(8,128)(2,1)} %collective-permute-done.5.refs_3_), channel_id=1, source_target_pairs={{0,1},{1,0},{2,3},{3,2},{4,5},{5,4},{6,7},{7,6},{8,9},{9,8},{10,11... | collective-permute-start | bytes 2359304 | tf_op jit(solution)/shard_map/ppermute | solution.py:25
  58.6 0.0 collective-permute-done.14.refs_4_
  58.6 0.0 collective-permute-start.18
  58.6 0.0 collective-permute-done.15.refs_5_
  58.6 0.0 copy-start.3
  58.7 0.1 collective-permute-start.2
  58.8 0.0 collective-permute-done.9
  58.8 0.1 collective-permute-start.6
  58.9 0.0 collective-permute-done.16.refs_6_
  58.9 0.7 copy-done.3
  59.5 0.9 copy-done.5
  60.4 0.0 collective-permute-start.10
  60.5 1.4 %collective-permute-done.17.refs_7_ = bf16[384,1024]{1,0:T(8,128)(2,1)S(1)} collective-permute-done((bf16[384,1024]{1,0:T(8,128)(2,1)}, bf16[384,1024]{1,0:T(8,128)(2,1)S(1)}, u32[]{:S(2)}, u32[]{:S(2)}) %collective-permute-start.17) | collective-permute-done | bytes 786464 | tf_op jit(solution)/shard_map/ppermute | solution.py:25
  61.8 0.9 copy-done.7
  62.7 1.0 collective-permute-start.12
  63.7 0.8 copy.4
  64.5 0.0 collective-permute-done.18.refs_8_
  64.5 5.6 %collective-permute-start.19 = (bf16[384,1024]{1,0:T(8,128)(2,1)}, bf16[384,1024]{1,0:T(8,128)(2,1)S(1)}, u32[]{:S(2)}, u32[]{:S(2)}) collective-permute-start(bf16[384,1024]{1,0:T(8,128)(2,1)} %copy-done.3), channel_id=1, source_target_pairs={{0,1},{1,0},{2,3},{3,2},{4,5},{5,4},{6,7},{7,6},{8,9},{9,8},{10,11... | collective-permute-start | bytes 2359304 | tf_op jit(solution)/shard_map/ppermute | solution.py:25
  70.1 0.7 bitcast_select_fusion
  70.8 0.7 fusion
  71.5 1.4 %pad_add_fusion.1.refs_0_ = s32[2]{0:T(128)S(1)} fusion(s32[1]{0:T(128)} %bitcast.1, s32[1]{0:T(128)} %bitcast.2), kind=kLoop, calls=%fused_computation.3 | loop fusion | flops 2 | bytes 16 | tf_op jit(solution)/shard_map/stack | solution.py:200
  72.9 1.4 %pad_add_fusion.refs_0_ = s32[2]{0:T(128)S(1)} fusion(s32[1]{0:T(128)} %bitcast.2, s32[1]{0:T(128)} %bitcast.1), kind=kLoop, calls=%fused_computation.2 | loop fusion | flops 2 | bytes 16 | tf_op jit(solution)/shard_map/stack | solution.py:206
  74.2 1.3 %pad_add_fusion.2.refs_0_ = s32[4]{0:T(128)S(1)} fusion(s32[1]{0:T(128)} %bitcast.4, s32[1]{0:T(128)} %bitcast.5), kind=kLoop, calls=%fused_computation.4 | loop fusion | flops 12 | bytes 24 | tf_op jit(solution)/shard_map/stack | solution.py:194
  75.6 0.0 collective-permute-done.2.refs_2_
  75.6 0.1 collective-permute-start.3
  75.6 6.6 %collective-permute-done.6.refs_3_ = bf16[384,1024]{1,0:T(8,128)(2,1)} collective-permute-done((bf16[384,1024]{1,0:T(8,128)(2,1)}, bf16[384,1024]{1,0:T(8,128)(2,1)}, u32[]{:S(2)}, u32[]{:S(2)}) %collective-permute-start.6) | collective-permute-done | bytes 786464 | tf_op jit(solution)/shard_map/ppermute | solution.py:25
  82.3 0.8 collective-permute-start.7
  83.1 0.0 collective-permute-done.10.refs_4_
  83.1 0.0 collective-permute-start.11
  83.1 0.0 collective-permute-done.12.refs_5_
  83.1 1.1 collective-permute-start.13
  84.2 1.1 copy-done
  85.4 1.1 copy-done.2
  86.5 4.9 %shard_map.41 = (f32[384,1]{1,0:T(8,128)S(1)}, f32[384,1]{1,0:T(8,128)S(1)}, f32[384,1024]{1,0:T(8,128)S(1)}, f32[1,384]{1,0:T(1,128)S(1)}) custom-call(bf16[384,1024]{1,0:T(8,128)(2,1)S(1)} %bitcast.11, bf16[384,1024]{1,0:T(8,128)(2,1)S(1)} %collective-permute-done.refs_1_, bf16[384,1024]{1,0:T(8,128)(2,1)S(1)} %collective-permute-done.4.refs_2_, ...), custom_call_target="tpu_custom_call" | custom-call | flops 2415919104 | bytes 7077888 | tf_op jit(solution)/shard_map/pallas_call | solution.py:146
  91.4 0.0 collective-permute-done.19.refs_9_
  91.4 12.0 %shard_map.42 = (f32[384,1]{1,0:T(8,128)S(1)}, f32[384,1]{1,0:T(8,128)S(1)}, f32[384,1024]{1,0:T(8,128)S(1)}) custom-call(s32[4]{0:T(128)S(1)} %pad_add_fusion.2.refs_0_, bf16[384,1024]{1,0:T(8,128)(2,1)S(1)} %bitcast.12, bf16[384,1024]{1,0:T(8,128)(2,1)S(1)} %collective-permute-done.1.refs_2_, bf16[384,1024]{1,0:T(8,128)(2,1)} %collective-permute-done.5.refs_3_, ...), custom_call_target="tpu_custom_call" | custom-call | flops 4831838208 | bytes 10223616 | tf_op jit(solution)/shard_map/pallas_call | solution.py:146
  103.4 7.0 %shard_map.43 = (f32[384,1]{1,0:T(8,128)S(1)}, f32[384,1]{1,0:T(8,128)S(1)}, f32[384,1024]{1,0:T(8,128)S(1)}) custom-call(s32[2]{0:T(128)S(1)} %pad_add_fusion.1.refs_0_, bf16[384,1024]{1,0:T(8,128)(2,1)S(1)} %bitcast.13, bf16[384,1024]{1,0:T(8,128)(2,1)} %collective-permute-done.2.refs_2_, bf16[384,1024]{1,0:T(8,128)(2,1)} %collective-permute-done.6.refs_3_, ...), custom_call_target="tpu_custom_call" | custom-call | flops 2415919104 | bytes 7077888 | tf_op jit(solution)/shard_map/pallas_call | solution.py:146
  110.4 0.0 collective-permute-done.3.refs_2_
  110.4 0.0 collective-permute-done.7.refs_3_
  110.4 0.0 collective-permute-done.11.refs_4_
  110.4 0.0 collective-permute-done.13.refs_5_
  110.4 6.9 %shard_map.44 = (bf16[384,1024]{1,0:T(8,128)(2,1)}, f32[1,384]{1,0:T(1,128)S(1)}) custom-call(s32[2]{0:T(128)S(1)} %pad_add_fusion.refs_0_, bf16[384,1024]{1,0:T(8,128)(2,1)S(1)} %bitcast.14, bf16[384,1024]{1,0:T(8,128)(2,1)S(1)} %collective-permute-done.3.refs_2_, bf16[384,1024]{1,0:T(8,128)(2,1)S(1)} %collective-permute-done.7.refs_3_, ...), custom_call_target="tpu_custom_call" | custom-call | flops 2415919104 | bytes 7077888 | tf_op jit(solution)/shard_map/pallas_call | solution.py:146
  117.4 0.1 collective-permute-start.22
  117.5 2.4 %collective-permute-done.22 = f32[1,384]{1,0:T(1,128)S(1)} collective-permute-done((f32[1,384]{1,0:T(1,128)S(1)}, f32[1,384]{1,0:T(1,128)S(1)}, u32[]{:S(2)}, u32[]{:S(2)}) %collective-permute-start.22) | collective-permute-done | bytes 1568 | tf_op jit(solution)/shard_map/ppermute | solution.py:25
  119.9 0.6 multiply_subtract_fusion
  (11 shorter events, 0.0 us)
Async XLA Ops:
  0.6 18.5 %collective-permute-start = (bf16[384,1024]{1,0:T(8,128)(2,1)}, bf16[384,1024]{1,0:T(8,128)(2,1)S(1)}, u32[]{:S(2)}, u32[]{:S(2)}) collective-permute-start(bf16[384,1024]{1,0:T(8,128)(2,1)} %bitcast.8), channel_id=1, source_target_pairs={{0,128},{1,129},{2,130},{3,131},{4,132},{5,133},{6,134},{7,135},{8... | collective-permute-start | bytes 2359304 | tf_op jit(solution)/shard_map/ppermute | solution.py:25
  2.8 19.2 %collective-permute-start.4 = (bf16[384,1024]{1,0:T(8,128)(2,1)}, bf16[384,1024]{1,0:T(8,128)(2,1)S(1)}, u32[]{:S(2)}, u32[]{:S(2)}) collective-permute-start(bf16[384,1024]{1,0:T(8,128)(2,1)} %bitcast.9), channel_id=1, source_target_pairs={{0,130},{1,131},{2,128},{3,129},{4,134},{5,135},{6,132},{7,133},{8... | collective-permute-start | bytes 2359304 | tf_op jit(solution)/shard_map/ppermute | solution.py:25
  4.7 22.8 %collective-permute-start.8 = (bf16[384,1024]{1,0:T(8,128)(2,1)}, bf16[384,1024]{1,0:T(8,128)(2,1)S(1)}, u32[]{:S(2)}, u32[]{:S(2)}) collective-permute-start(bf16[384,1024]{1,0:T(8,128)(2,1)} %bitcast.10), channel_id=1, source_target_pairs={{0,4},{1,125},{2,6},{3,127},{4,8},{5,1},{6,10},{7,3},{8,12},{9,5},... | collective-permute-start | bytes 2359304 | tf_op jit(solution)/shard_map/ppermute | solution.py:25
  19.2 8.3 %collective-permute-start.20 = (bf16[384,1024]{1,0:T(8,128)(2,1)S(1)}, bf16[384,1024]{1,0:T(8,128)(2,1)S(1)}, u32[]{:S(2)}, u32[]{:S(2)}) collective-permute-start(bf16[384,1024]{1,0:T(8,128)(2,1)S(1)} %collective-permute-done.refs_1_), channel_id=1, source_target_pairs={{0,1},{1,0},{2,3},{3,2},{4,5},{5,4},{6,7},{7,6},{8,9},{9,8},{10,11... | collective-permute-start | bytes 2359304 | tf_op jit(solution)/shard_map/ppermute | solution.py:25
  22.1 7.4 %collective-permute-start.21 = (bf16[384,1024]{1,0:T(8,128)(2,1)S(1)}, bf16[384,1024]{1,0:T(8,128)(2,1)S(1)}, u32[]{:S(2)}, u32[]{:S(2)}) collective-permute-start(bf16[384,1024]{1,0:T(8,128)(2,1)S(1)} %collective-permute-done.4.refs_2_), channel_id=1, source_target_pairs={{0,1},{1,0},{2,3},{3,2},{4,5},{5,4},{6,7},{7,6},{8,9},{9,8},{10,11... | collective-permute-start | bytes 2359304 | tf_op jit(solution)/shard_map/ppermute | solution.py:25
  24.2 17.1 %collective-permute-start.1 = (bf16[384,1024]{1,0:T(8,128)(2,1)S(1)}, bf16[384,1024]{1,0:T(8,128)(2,1)S(1)}, u32[]{:S(2)}, u32[]{:S(2)}) collective-permute-start(bf16[384,1024]{1,0:T(8,128)(2,1)S(1)} %collective-permute-done.refs_1_), channel_id=1, source_target_pairs={{0,124},{1,5},{2,126},{3,7},{4,0},{5,9},{6,2},{7,11},{8,4},{9,13},... | collective-permute-start | bytes 2359304 | tf_op jit(solution)/shard_map/ppermute | solution.py:25
  25.9 31.4 %collective-permute-start.5 = (bf16[384,1024]{1,0:T(8,128)(2,1)S(1)}, bf16[384,1024]{1,0:T(8,128)(2,1)}, u32[]{:S(2)}, u32[]{:S(2)}) collective-permute-start(bf16[384,1024]{1,0:T(8,128)(2,1)S(1)} %collective-permute-done.4.refs_2_), channel_id=1, source_target_pairs={{0,124},{1,5},{2,126},{3,7},{4,0},{5,9},{6,2},{7,11},{8,4},{9,13},... | collective-permute-start | bytes 2359304 | tf_op jit(solution)/shard_map/ppermute | solution.py:25
  27.5 31.1 %collective-permute-start.14 = (bf16[384,1024]{1,0:T(8,128)(2,1)S(1)}, bf16[384,1024]{1,0:T(8,128)(2,1)}, u32[]{:S(2)}, u32[]{:S(2)}) collective-permute-start(bf16[384,1024]{1,0:T(8,128)(2,1)S(1)} %collective-permute-done.8), channel_id=1, source_target_pairs={{0,128},{1,129},{2,130},{3,131},{4,132},{5,133},{6,134},{7,135},{8... | collective-permute-start | bytes 2359304 | tf_op jit(solution)/shard_map/ppermute | solution.py:25
  27.5 31.1 %collective-permute-start.15 = (bf16[384,1024]{1,0:T(8,128)(2,1)S(1)}, bf16[384,1024]{1,0:T(8,128)(2,1)S(1)}, u32[]{:S(2)}, u32[]{:S(2)}) collective-permute-start(bf16[384,1024]{1,0:T(8,128)(2,1)S(1)} %collective-permute-done.8), channel_id=1, source_target_pairs={{0,130},{1,131},{2,128},{3,129},{4,134},{5,135},{6,132},{7,133},{8... | collective-permute-start | bytes 2359304 | tf_op jit(solution)/shard_map/ppermute | solution.py:25
  29.5 0.9 copy-start.1
  30.4 28.3 %collective-permute-start.9 = (bf16[384,1024]{1,0:T(8,128)(2,1)S(1)}, bf16[384,1024]{1,0:T(8,128)(2,1)}, u32[]{:S(2)}, u32[]{:S(2)}) collective-permute-start(bf16[384,1024]{1,0:T(8,128)(2,1)S(1)} %collective-permute-done.8), channel_id=1, source_target_pairs={{0,4},{1,125},{2,6},{3,127},{4,8},{5,1},{6,10},{7,3},{8,12},{9,5},... | collective-permute-start | bytes 2359304 | tf_op jit(solution)/shard_map/ppermute | solution.py:25
  41.4 17.5 %collective-permute-start.16 = (bf16[384,1024]{1,0:T(8,128)(2,1)S(1)}, bf16[384,1024]{1,0:T(8,128)(2,1)S(1)}, u32[]{:S(2)}, u32[]{:S(2)}) collective-permute-start(bf16[384,1024]{1,0:T(8,128)(2,1)S(1)} %collective-permute-done.1.refs_2_), channel_id=1, source_target_pairs={{0,1},{1,0},{2,3},{3,2},{4,5},{5,4},{6,7},{7,6},{8,9},{9,8},{10,11... | collective-permute-start | bytes 2359304 | tf_op jit(solution)/shard_map/ppermute | solution.py:25
  57.2 4.6 %collective-permute-start.17 = (bf16[384,1024]{1,0:T(8,128)(2,1)}, bf16[384,1024]{1,0:T(8,128)(2,1)S(1)}, u32[]{:S(2)}, u32[]{:S(2)}) collective-permute-start(bf16[384,1024]{1,0:T(8,128)(2,1)} %collective-permute-done.5.refs_3_), channel_id=1, source_target_pairs={{0,1},{1,0},{2,3},{3,2},{4,5},{5,4},{6,7},{7,6},{8,9},{9,8},{10,11... | collective-permute-start | bytes 2359304 | tf_op jit(solution)/shard_map/ppermute | solution.py:25
  58.6 5.9 %collective-permute-start.18 = (bf16[384,1024]{1,0:T(8,128)(2,1)}, bf16[384,1024]{1,0:T(8,128)(2,1)}, u32[]{:S(2)}, u32[]{:S(2)}) collective-permute-start(bf16[384,1024]{1,0:T(8,128)(2,1)} %collective-permute-done.14.refs_4_), channel_id=1, source_target_pairs={{0,1},{1,0},{2,3},{3,2},{4,5},{5,4},{6,7},{7,6},{8,9},{9,8},{10,11... | collective-permute-start | bytes 2359304 | tf_op jit(solution)/shard_map/ppermute | solution.py:25
  58.6 0.9 copy-start.3
  58.7 16.9 %collective-permute-start.2 = (bf16[384,1024]{1,0:T(8,128)(2,1)S(1)}, bf16[384,1024]{1,0:T(8,128)(2,1)}, u32[]{:S(2)}, u32[]{:S(2)}) collective-permute-start(bf16[384,1024]{1,0:T(8,128)(2,1)S(1)} %collective-permute-done.1.refs_2_), channel_id=1, source_target_pairs={{0,124},{1,5},{2,126},{3,7},{4,0},{5,9},{6,2},{7,11},{8,4},{9,13},... | collective-permute-start | bytes 2359304 | tf_op jit(solution)/shard_map/ppermute | solution.py:25
  58.8 23.5 %collective-permute-start.6 = (bf16[384,1024]{1,0:T(8,128)(2,1)}, bf16[384,1024]{1,0:T(8,128)(2,1)}, u32[]{:S(2)}, u32[]{:S(2)}) collective-permute-start(bf16[384,1024]{1,0:T(8,128)(2,1)} %collective-permute-done.5.refs_3_), channel_id=1, source_target_pairs={{0,124},{1,5},{2,126},{3,7},{4,0},{5,9},{6,2},{7,11},{8,4},{9,13},... | collective-permute-start | bytes 2359304 | tf_op jit(solution)/shard_map/ppermute | solution.py:25
  59.5 0.9 copy-start.5
  60.4 22.7 %collective-permute-start.10 = (bf16[384,1024]{1,0:T(8,128)(2,1)}, bf16[384,1024]{1,0:T(8,128)(2,1)}, u32[]{:S(2)}, u32[]{:S(2)}) collective-permute-start(bf16[384,1024]{1,0:T(8,128)(2,1)} %collective-permute-done.9), channel_id=1, source_target_pairs={{0,128},{1,129},{2,130},{3,131},{4,132},{5,133},{6,134},{7,135},{8... | collective-permute-start | bytes 2359304 | tf_op jit(solution)/shard_map/ppermute | solution.py:25
  61.8 0.9 copy-start.7
  62.7 20.4 %collective-permute-start.12 = (bf16[384,1024]{1,0:T(8,128)(2,1)}, bf16[384,1024]{1,0:T(8,128)(2,1)}, u32[]{:S(2)}, u32[]{:S(2)}) collective-permute-start(bf16[384,1024]{1,0:T(8,128)(2,1)} %collective-permute-done.9), channel_id=1, source_target_pairs={{0,130},{1,131},{2,128},{3,129},{4,134},{5,135},{6,132},{7,133},{8... | collective-permute-start | bytes 2359304 | tf_op jit(solution)/shard_map/ppermute | solution.py:25
  64.5 26.9 %collective-permute-start.19 = (bf16[384,1024]{1,0:T(8,128)(2,1)}, bf16[384,1024]{1,0:T(8,128)(2,1)S(1)}, u32[]{:S(2)}, u32[]{:S(2)}) collective-permute-start(bf16[384,1024]{1,0:T(8,128)(2,1)} %copy-done.3), channel_id=1, source_target_pairs={{0,1},{1,0},{2,3},{3,2},{4,5},{5,4},{6,7},{7,6},{8,9},{9,8},{10,11... | collective-permute-start | bytes 2359304 | tf_op jit(solution)/shard_map/ppermute | solution.py:25
  75.6 34.8 %collective-permute-start.3 = (bf16[384,1024]{1,0:T(8,128)(2,1)}, bf16[384,1024]{1,0:T(8,128)(2,1)S(1)}, u32[]{:S(2)}, u32[]{:S(2)}) collective-permute-start(bf16[384,1024]{1,0:T(8,128)(2,1)} %collective-permute-done.2.refs_2_), channel_id=1, source_target_pairs={{0,1},{1,0},{2,3},{3,2},{4,5},{5,4},{6,7},{7,6},{8,9},{9,8},{10,11... | collective-permute-start | bytes 2359304 | tf_op jit(solution)/shard_map/ppermute | solution.py:25
  82.3 28.1 %collective-permute-start.7 = (bf16[384,1024]{1,0:T(8,128)(2,1)}, bf16[384,1024]{1,0:T(8,128)(2,1)S(1)}, u32[]{:S(2)}, u32[]{:S(2)}) collective-permute-start(bf16[384,1024]{1,0:T(8,128)(2,1)} %collective-permute-done.6.refs_3_), channel_id=1, source_target_pairs={{0,1},{1,0},{2,3},{3,2},{4,5},{5,4},{6,7},{7,6},{8,9},{9,8},{10,11... | collective-permute-start | bytes 2359304 | tf_op jit(solution)/shard_map/ppermute | solution.py:25
  83.1 27.3 %collective-permute-start.11 = (bf16[384,1024]{1,0:T(8,128)(2,1)}, bf16[384,1024]{1,0:T(8,128)(2,1)S(1)}, u32[]{:S(2)}, u32[]{:S(2)}) collective-permute-start(bf16[384,1024]{1,0:T(8,128)(2,1)} %collective-permute-done.10.refs_4_), channel_id=1, source_target_pairs={{0,1},{1,0},{2,3},{3,2},{4,5},{5,4},{6,7},{7,6},{8,9},{9,8},{10,11... | collective-permute-start | bytes 2359304 | tf_op jit(solution)/shard_map/ppermute | solution.py:25
  83.1 27.3 %collective-permute-start.13 = (bf16[384,1024]{1,0:T(8,128)(2,1)}, bf16[384,1024]{1,0:T(8,128)(2,1)S(1)}, u32[]{:S(2)}, u32[]{:S(2)}) collective-permute-start(bf16[384,1024]{1,0:T(8,128)(2,1)} %collective-permute-done.12.refs_5_), channel_id=1, source_target_pairs={{0,1},{1,0},{2,3},{3,2},{4,5},{5,4},{6,7},{7,6},{8,9},{9,8},{10,11... | collective-permute-start | bytes 2359304 | tf_op jit(solution)/shard_map/ppermute | solution.py:25
  84.2 1.1 copy-start
  85.4 1.1 copy-start.2
  86.5 4.9 %copy-start.4 = (bf16[384,1024]{1,0:T(8,128)(2,1)S(1)}, bf16[384,1024]{1,0:T(8,128)(2,1)}, u32[]{:S(2)}) copy-start(bf16[384,1024]{1,0:T(8,128)(2,1)} %copy-done.3) | copy-start | bytes 2359300
  86.5 4.9 %copy-start.6 = (bf16[384,1024]{1,0:T(8,128)(2,1)S(1)}, bf16[384,1024]{1,0:T(8,128)(2,1)}, u32[]{:S(2)}) copy-start(bf16[384,1024]{1,0:T(8,128)(2,1)} %copy-done.5) | copy-start | bytes 2359300
  86.5 4.9 %copy-start.8 = (bf16[384,1024]{1,0:T(8,128)(2,1)S(1)}, bf16[384,1024]{1,0:T(8,128)(2,1)}, u32[]{:S(2)}) copy-start(bf16[384,1024]{1,0:T(8,128)(2,1)} %copy-done.7) | copy-start | bytes 2359300
  117.4 2.5 %collective-permute-start.22 = (f32[1,384]{1,0:T(1,128)S(1)}, f32[1,384]{1,0:T(1,128)S(1)}, u32[]{:S(2)}, u32[]{:S(2)}) collective-permute-start(f32[1,384]{1,0:T(1,128)S(1)} %get-tuple-element.25), channel_id=1, source_target_pairs={{0,128},{1,129},{2,130},{3,131},{4,132},{5,133},{6,134},{7,135},{8... | collective-permute-start | bytes 4616 | tf_op jit(solution)/shard_map/ppermute | solution.py:25

commit v2 on v1

v2 whole, which is shorter than its diff:
```python
import functools
import math

import jax
import jax.numpy as jnp
from jax import lax
from jax.experimental import pallas as pl
from jax.experimental.pallas import tpu as pltpu
from jax.sharding import PartitionSpec as P

sharpness = 3.0
AXES = ("dir", "loop", "pb")
PARTS = 1
VMEM = pl.BlockSpec(memory_space=pltpu.VMEM)
SMEM = pl.BlockSpec(memory_space=pltpu.SMEM)
ANY = pl.BlockSpec(memory_space=pl.ANY)


def moved(value, route):
    sides, blocks, slabs = (lax.axis_size(axis) for axis in AXES)
    pairs = []
    for side in range(sides):
        for block in range(blocks):
            for slab in range(slabs):
                half, core = divmod(slab, 2)
                side_to, block_to, half_to, core_to = route(side, block, half, core)
                target = (side_to * blocks + block_to % blocks) * slabs + half_to * 2 + core_to
                pairs.append(((side * blocks + block) * slabs + slab, target))
    return lax.ppermute(value, AXES, pairs)


def across_near(side, block, half, core):
    return 1 - side, block, half, core


def across_far(side, block, half, core):
    return 1 - side, block, 1 - half, core


def across_other(side, block, half, core):
    return 1 - side, block, half, 1 - core


def sibling(side, block, half, core):
    return side, block, half, 1 - core


def ahead(side, block, half, core):
    return side, block + (1 if core == 0 else -1), half, core


def behind(side, block, half, core):
    return side, block - (1 if core == 0 else -1), half, core


def attend_kernel(first, last, level, score_scale, *refs):
    refs = list(refs)

    def take(count):
        return [refs.pop(0) for _ in range(count)]

    if not first:
        (mask_ref,) = take(1)
    query_refs = take(2)
    state_in = [] if first else take(3)
    slab_refs = take(len(refs) - (7 if first else 10 if last else 6))
    if first:
        max_ref, total_ref, sum_ref, pair_ref = take(4)
    elif last:
        own_sum_ref, other_sum_ref, own_stat_ref, other_stat_ref = take(4)
        max_ref, total_ref, sum_ref = take(3)
    else:
        max_ref, total_ref, sum_ref = take(3)
    query_ref, key_ref, copy_sems = refs
    rows = query_ref.shape[0] // 2
    copies = []
    for sources, target in ((query_refs, query_ref), (slab_refs, key_ref)):
        begin = 0
        for source in sources:
            copy = pltpu.make_async_copy(
                source, target.at[pl.ds(begin, source.shape[0])], copy_sems.at[len(copies)]
            )
            copy.start()
            copies.append(copy)
            begin += source.shape[0]

    def absorb():
        keys = key_ref[...]
        for start in (rows, 0):
            here = pl.ds(start, rows)
            scores = (
                lax.dot_general(
                    query_ref[here, :], keys, (((1,), (1,)), ((), ())),
                    preferred_element_type=jnp.float32,
                )
                * score_scale
            )
            new_max = jnp.max(scores, axis=1, keepdims=True)
            if not first:
                new_max = jnp.maximum(state_in[0][here, :], new_max)
            weights = jnp.exp(scores - new_max)
            total = jnp.sum(weights, axis=1, keepdims=True)
            blended = jnp.dot(weights.astype(jnp.bfloat16), keys, preferred_element_type=jnp.float32)
            if not first:
                correction = jnp.exp(state_in[0][here, :] - new_max)
                total += state_in[1][here, :] * correction
                blended += state_in[2][here, :] * correction
            max_ref[here, :] = new_max
            total_ref[here, :] = total
            sum_ref[here, :] = blended

    for copy in copies:
        copy.wait()
    if first:
        absorb()
        pair_ref[...] = (
            jnp.sum(
                query_ref[:rows, :].astype(jnp.float32) * key_ref[:rows, :].astype(jnp.float32),
                axis=1,
                keepdims=True,
            )
            * score_scale
        ).T
    else:
        side, block = lax.axis_index("dir"), lax.axis_index("loop")
        blocks = mask_ref.shape[0]
        offset = jnp.where(lax.axis_index("pb") % 2 == 0, level, -level)
        target = lax.rem(block + offset + blocks, blocks)
        flag = jnp.where(side == 0, mask_ref[block, target], mask_ref[target, block])
        pl.when(flag > 0)(absorb)

        @pl.when(flag <= 0)
        def _():
            max_ref[...] = state_in[0][...]
            total_ref[...] = state_in[1][...]
            sum_ref[...] = state_in[2][...]

    if last:
        for index, (sum_out, stat_out) in enumerate(
            [(own_sum_ref, own_stat_ref), (other_sum_ref, other_stat_ref)]
        ):
            here = pl.ds(index * rows, rows)
            sum_out[...] = sum_ref[here, :]
            stat_out[0:1, :] = max_ref[here, :].T
            stat_out[1:2, :] = total_ref[here, :].T


def attend(queries, slabs, score_scale, level=0, mask=None, state=None, last=False):
    rows, width = queries[0].shape
    first = state is None
    keys = sum(slab.shape[0] for slab in slabs)
    held = [
        jax.ShapeDtypeStruct((2 * rows, 1), jnp.float32),
        jax.ShapeDtypeStruct((2 * rows, 1), jnp.float32),
        jax.ShapeDtypeStruct((2 * rows, width), jnp.float32),
    ]
    scratch = [
        pltpu.VMEM((2 * rows, width), jnp.bfloat16),
        pltpu.VMEM((keys, width), jnp.bfloat16),
        pltpu.SemaphoreType.DMA((len(slabs) + 2,)),
    ]
    if first:
        out = held + [jax.ShapeDtypeStruct((1, rows), jnp.float32)]
    elif last:
        out = [jax.ShapeDtypeStruct((rows, width), jnp.float32)] * 2
        out += [jax.ShapeDtypeStruct((2, rows), jnp.float32)] * 2
        scratch = [pltpu.VMEM(a.shape, a.dtype) for a in held] + scratch
    else:
        out = held
    in_specs = [ANY, ANY] if first else [SMEM, ANY, ANY, VMEM, VMEM, VMEM]
    operands = list(queries) if first else [mask] + list(queries) + list(state)
    return pl.pallas_call(
        functools.partial(attend_kernel, first, last, level, score_scale),
        out_shape=out,
        in_specs=in_specs + [ANY] * len(slabs),
        out_specs=[VMEM] * len(out),
        scratch_shapes=scratch,
        compiler_params=pltpu.CompilerParams(vmem_limit_bytes=24 * 2**20),
        cost_estimate=pl.CostEstimate(
            flops=8 * keys * rows * width,
            bytes_accessed=2 * (keys + 2 * rows) * width + 16 * rows * width,
            transcendentals=2 * keys * rows,
        ),
    )(*operands, *slabs)


def finish_kernel(
    sum_ref, sum_in_ref, stat_ref, stat_in_ref, far_stat_ref, far_stat_in_ref, pair_ref,
    blended_ref, margin_ref,
):
    def merged(here, there):
        top = jnp.maximum(here[0:1, :], there[0:1, :])
        left, right = jnp.exp(here[0:1, :] - top), jnp.exp(there[0:1, :] - top)
        total = here[1:2, :] * left + there[1:2, :] * right
        return left, right, total, top + jnp.log(total)

    left, right, total, own_log = merged(stat_ref[...], stat_in_ref[...])
    far_log = merged(far_stat_ref[...], far_stat_in_ref[...])[3]
    margin_ref[...] = pair_ref[...] - 0.5 * (own_log + far_log)
    blended_ref[...] = (
        sum_ref[...] * (left / total).T + sum_in_ref[...] * (right / total).T
    ).astype(jnp.bfloat16)


def finish(*operands):
    rows, width = operands[0].shape
    return pl.pallas_call(
        finish_kernel,
        out_shape=[
            jax.ShapeDtypeStruct((rows, width), jnp.bfloat16),
            jax.ShapeDtypeStruct((1, rows), jnp.float32),
        ],
        in_specs=[VMEM] * len(operands),
        out_specs=[VMEM] * 2,
        compiler_params=pltpu.CompilerParams(vmem_limit_bytes=20 * 2**20),
    )(*operands)


def shards(embeddings, block_mask):
    own = embeddings[0]
    score_scale = sharpness / math.sqrt(own.shape[1])
    rows = own.shape[0]
    part = rows // PARTS
    parts = [own[start : start + part] for start in range(0, rows, part)]

    ahead_1 = moved(own, ahead)
    near = [moved(piece, across_near) for piece in parts]
    far = [moved(piece, across_far) for piece in parts]
    queries = (own, moved(own, sibling))
    ahead_2 = moved(ahead_1, ahead)
    cross_1 = [moved(ahead_1, across_near), moved(ahead_1, across_far)]
    behind_1 = [moved(piece, behind) for piece in near + far]
    *state, pair_score = attend(queries, near + far, score_scale)
    ahead_2, state[0] = lax.optimization_barrier((ahead_2, state[0]))
    cross_2 = [moved(ahead_2, across_near), moved(ahead_2, across_far)]
    state = list(attend(queries, cross_1, score_scale, -1, block_mask, state))
    behind_2 = [moved(piece, behind) for piece in behind_1]
    state = attend(queries, behind_1, score_scale, 1, block_mask, state)
    state = attend(queries, cross_2, score_scale, -2, block_mask, state)
    own_sum, other_sum, own_stat, other_stat = attend(
        queries, behind_2, score_scale, 2, block_mask, state, last=True
    )
    blended, margin = finish(
        own_sum,
        moved(other_sum, sibling),
        own_stat,
        moved(other_stat, sibling),
        moved(own_stat, across_near),
        moved(other_stat, across_other),
        pair_score,
    )
    return (blended[None], margin)


def solution(mesh):
    placed = (P("dir", ("loop", "pb"), None), P())
    return jax.shard_map(
        shards,
        mesh=mesh,
        in_specs=placed,
        out_specs=(P("dir", ("loop", "pb"), None), P("dir", ("loop", "pb"))),
        check_vma=False,
    )
```

time: 121 us -> 81.8 us (0.68)
  starting transfers between devices: 42.7 us -> 28.3 us
  waiting for transfers between devices: 33.7 us -> 25.7 us
  local copies, waits for them, and re-layouts: 7.16 us -> 1.14 us
  other arithmetic: 5.37 us -> 0 us
  Pallas kernels: 30.8 us -> 25.7 us
    ppermute x23 -> x17, starting transfers between devices: 42.7 us -> 28.3 us  [moved(): return lax.ppermute(value, AXES, pairs)]
    ppermute x23 -> x17, waiting for transfers between devices: 33.7 us -> 25.7 us  [moved(): return lax.ppermute(value, AXES, pairs)]
    unnamed x19 -> x4, local copies, waits for them, and re-layouts: 6.49 us -> 1.14 us
    pallas_call x4 -> x6, Pallas kernels: 30.8 us -> 25.7 us  [the longest x5 24.3 us: attend(): pl.pallas_call(functools.partial(attend_kernel, first, last, level, score...]
    another operation x3 -> x0, other arithmetic: 4.08 us -> none  [the longest x1 1.37 us: shards(): jnp.stack([flag(-2), flag(2)])]
  transfers between devices with their start and end apart: 23 -> 17, of which waited for: 7 -> 10; matrix products, arithmetic and copies ran while one was open for 5% -> 0% of each run, Pallas kernels for 20% -> 23%
where the time goes in v2:
time: 81.8 us; the launch traced here: 81.7 us
  starting transfers between devices  28.3 us (35%)
  waiting for transfers between devices  25.7 us (31%)
  Pallas kernels  25.7 us (31%)
  local copies, waits for them, and re-layouts  1.14 us (1%)
    ppermute x17, starting transfers between devices, moved(): return lax.ppermute(value, AXES, pairs)  28.3 us
    ppermute x17, waiting for transfers between devices, moved(): return lax.ppermute(value, AXES, pairs)  25.7 us
    pallas_call x5, Pallas kernels, attend(): pl.pallas_call(functools.partial(attend_kernel, first, last, level, score...  24.3 us
  transfers between devices with their start and end apart: 17, of which 10 were waited for; matrix products, arithmetic and copies ran while one was open for 0% of the time, Pallas kernels for 23%

profile of v2, /device:TPU:1, one launch (start us, length us, event | category | flops | bytes accessed | tf_op | source)
XLA Modules:
  0.0 81.7 jit_solution(5852261068382104820)
XLA Ops:
  0.6 8.7 %collective-permute-start.1 = (bf16[384,1024]{1,0:T(8,128)(2,1)}, bf16[384,1024]{1,0:T(8,128)(2,1)S(1)}, u32[]{:S(2)}, u32[]{:S(2)}) collective-permute-start(bf16[384,1024]{1,0:T(8,128)(2,1)} %bitcast.2), channel_id=1, source_target_pairs={{0,4},{1,125},{2,6},{3,127},{4,8},{5,1},{6,10},{7,3},{8,12},{9,5},... | collective-permute-start | bytes 2359304 | tf_op jit(solution)/shard_map/ppermute | solution.py:29
  9.3 1.3 %collective-permute-start.3 = (bf16[384,1024]{1,0:T(8,128)(2,1)}, bf16[384,1024]{1,0:T(8,128)(2,1)S(1)}, u32[]{:S(2)}, u32[]{:S(2)}) collective-permute-start(bf16[384,1024]{1,0:T(8,128)(2,1)} %bitcast.3), channel_id=1, source_target_pairs={{0,128},{1,129},{2,130},{3,131},{4,132},{5,133},{6,134},{7,135},{8... | collective-permute-start | bytes 2359304 | tf_op jit(solution)/shard_map/ppermute | solution.py:29
  10.6 1.9 %collective-permute-start.4 = (bf16[384,1024]{1,0:T(8,128)(2,1)}, bf16[384,1024]{1,0:T(8,128)(2,1)S(1)}, u32[]{:S(2)}, u32[]{:S(2)}) collective-permute-start(bf16[384,1024]{1,0:T(8,128)(2,1)} %bitcast.4), channel_id=1, source_target_pairs={{0,130},{1,131},{2,128},{3,129},{4,134},{5,135},{6,132},{7,133},{8... | collective-permute-start | bytes 2359304 | tf_op jit(solution)/shard_map/ppermute | solution.py:29
  12.5 0.0 collective-permute-start
  12.5 6.0 %collective-permute-done.1 = bf16[384,1024]{1,0:T(8,128)(2,1)S(1)} collective-permute-done((bf16[384,1024]{1,0:T(8,128)(2,1)}, bf16[384,1024]{1,0:T(8,128)(2,1)S(1)}, u32[]{:S(2)}, u32[]{:S(2)}) %collective-permute-start.1) | collective-permute-done | bytes 786464 | tf_op jit(solution)/shard_map/ppermute | solution.py:29
  18.6 5.1 %collective-permute-start.2 = (bf16[384,1024]{1,0:T(8,128)(2,1)S(1)}, bf16[384,1024]{1,0:T(8,128)(2,1)S(1)}, u32[]{:S(2)}, u32[]{:S(2)}) collective-permute-start(bf16[384,1024]{1,0:T(8,128)(2,1)S(1)} %collective-permute-done.1), channel_id=1, source_target_pairs={{0,4},{1,125},{2,6},{3,127},{4,8},{5,1},{6,10},{7,3},{8,12},{9,5},... | collective-permute-start | bytes 2359304 | tf_op jit(solution)/shard_map/ppermute | solution.py:29
  23.7 1.3 %collective-permute-start.5 = (bf16[384,1024]{1,0:T(8,128)(2,1)S(1)}, bf16[384,1024]{1,0:T(8,128)(2,1)S(1)}, u32[]{:S(2)}, u32[]{:S(2)}) collective-permute-start(bf16[384,1024]{1,0:T(8,128)(2,1)S(1)} %collective-permute-done.1), channel_id=1, source_target_pairs={{0,128},{1,129},{2,130},{3,131},{4,132},{5,133},{6,134},{7,135},{8... | collective-permute-start | bytes 2359304 | tf_op jit(solution)/shard_map/ppermute | solution.py:29
  25.0 0.1 collective-permute-done.3.refs_2_
  25.0 0.0 collective-permute-start.7
  25.0 2.1 %collective-permute-done.4.refs_3_ = bf16[384,1024]{1,0:T(8,128)(2,1)S(1)} collective-permute-done((bf16[384,1024]{1,0:T(8,128)(2,1)}, bf16[384,1024]{1,0:T(8,128)(2,1)S(1)}, u32[]{:S(2)}, u32[]{:S(2)}) %collective-permute-start.4) | collective-permute-done | bytes 786464 | tf_op jit(solution)/shard_map/ppermute | solution.py:29
  27.1 0.0 collective-permute-start.8
  27.2 0.0 collective-permute-done.refs_1_.refs_2_
  27.2 1.6 %collective-permute-start.6 = (bf16[384,1024]{1,0:T(8,128)(2,1)S(1)}, bf16[384,1024]{1,0:T(8,128)(2,1)S(1)}, u32[]{:S(2)}, u32[]{:S(2)}) collective-permute-start(bf16[384,1024]{1,0:T(8,128)(2,1)S(1)} %collective-permute-done.1), channel_id=1, source_target_pairs={{0,130},{1,131},{2,128},{3,129},{4,134},{5,135},{6,132},{7,133},{8... | collective-permute-start | bytes 2359304 | tf_op jit(solution)/shard_map/ppermute | solution.py:29
  28.8 0.0 copy-start
  28.8 1.1 %copy-done = bf16[1,384,1024]{2,1,0:T(8,128)(2,1)S(1)} copy-done((bf16[1,384,1024]{2,1,0:T(8,128)(2,1)S(1)}, bf16[1,384,1024]{2,1,0:T(8,128)(2,1)}, u32[]{:S(2)}) %copy-start) | copy-done | bytes 786456
  29.9 0.0 copy-start.1
  29.9 3.6 %shard_map.41 = (f32[768,1]{1,0:T(8,128)S(1)}, f32[768,1]{1,0:T(8,128)S(1)}, f32[768,1024]{1,0:T(8,128)S(1)}, f32[1,384]{1,0:T(1,128)S(1)}) custom-call(bf16[384,1024]{1,0:T(8,128)(2,1)S(1)} %bitcast.6, bf16[384,1024]{1,0:T(8,128)(2,1)S(1)} %collective-permute-done.refs_1_.refs_2_, bf16[384,1024]{1,0:T(8,128)(2,1)S(1)} %collective-permute-done.3.refs_2_, ...), custom_call_target="tpu_custom_call" | custom-call | flops 2415919104 | bytes 9437184 | tf_op jit(solution)/shard_map/pallas_call | solution.py:172
  33.5 0.6 collective-permute-done.2
  34.1 2.8 %collective-permute-start.10 = (bf16[384,1024]{1,0:T(8,128)(2,1)S(1)}, bf16[384,1024]{1,0:T(8,128)(2,1)S(1)}, u32[]{:S(2)}, u32[]{:S(2)}) collective-permute-start(bf16[384,1024]{1,0:T(8,128)(2,1)S(1)} %collective-permute-done.2), channel_id=1, source_target_pairs={{0,130},{1,131},{2,128},{3,129},{4,134},{5,135},{6,132},{7,133},{8... | collective-permute-start | bytes 2359304 | tf_op jit(solution)/shard_map/ppermute | solution.py:29
  36.9 4.3 %collective-permute-done.5.refs_6_ = bf16[384,1024]{1,0:T(8,128)(2,1)S(1)} collective-permute-done((bf16[384,1024]{1,0:T(8,128)(2,1)S(1)}, bf16[384,1024]{1,0:T(8,128)(2,1)S(1)}, u32[]{:S(2)}, u32[]{:S(2)}) %collective-permute-start.5) | collective-permute-done | bytes 786464 | tf_op jit(solution)/shard_map/ppermute | solution.py:29
  41.2 1.3 %collective-permute-start.9 = (bf16[384,1024]{1,0:T(8,128)(2,1)S(1)}, bf16[384,1024]{1,0:T(8,128)(2,1)S(1)}, u32[]{:S(2)}, u32[]{:S(2)}) collective-permute-start(bf16[384,1024]{1,0:T(8,128)(2,1)S(1)} %collective-permute-done.2), channel_id=1, source_target_pairs={{0,128},{1,129},{2,130},{3,131},{4,132},{5,133},{6,134},{7,135},{8... | collective-permute-start | bytes 2359304 | tf_op jit(solution)/shard_map/ppermute | solution.py:29
  42.5 1.0 %collective-permute-done.7.refs_6_ = bf16[384,1024]{1,0:T(8,128)(2,1)S(1)} collective-permute-done((bf16[384,1024]{1,0:T(8,128)(2,1)S(1)}, bf16[384,1024]{1,0:T(8,128)(2,1)S(1)}, u32[]{:S(2)}, u32[]{:S(2)}) %collective-permute-start.7) | collective-permute-done | bytes 786464 | tf_op jit(solution)/shard_map/ppermute | solution.py:29
  43.5 0.0 collective-permute-start.11
  43.5 8.4 %collective-permute-done.8.refs_7_ = bf16[384,1024]{1,0:T(8,128)(2,1)S(1)} collective-permute-done((bf16[384,1024]{1,0:T(8,128)(2,1)S(1)}, bf16[384,1024]{1,0:T(8,128)(2,1)S(1)}, u32[]{:S(2)}, u32[]{:S(2)}) %collective-permute-start.8) | collective-permute-done | bytes 786464 | tf_op jit(solution)/shard_map/ppermute | solution.py:29
  51.9 0.0 collective-permute-start.12
  51.9 0.0 collective-permute-done.6.refs_7_
  51.9 0.0 copy-done.1
  51.9 5.1 %shard_map.42 = (f32[768,1]{1,0:T(8,128)S(1)}, f32[768,1]{1,0:T(8,128)S(1)}, f32[768,1024]{1,0:T(8,128)S(1)}) custom-call(s32[32,32]{1,0:T(8,128)S(1)} %copy-done.1, bf16[384,1024]{1,0:T(8,128)(2,1)S(1)} %bitcast.7, bf16[384,1024]{1,0:T(8,128)(2,1)S(1)} %collective-permute-done.refs_1_.refs_2_, f32[768,1]{1,0:T(8,128)S(1)} %get-tuple-element.24.refs_3_, ...), custom_call_target="tpu_custom_call" | custom-call | flops 2415919104 | bytes 9437184 | tf_op jit(solution)/shard_map/pallas_call | solution.py:172
  57.1 5.0 %shard_map.43 = (f32[768,1]{1,0:T(8,128)S(1)}, f32[768,1]{1,0:T(8,128)S(1)}, f32[768,1024]{1,0:T(8,128)S(1)}) custom-call(s32[32,32]{1,0:T(8,128)S(1)} %copy-done.1, bf16[384,1024]{1,0:T(8,128)(2,1)S(1)} %bitcast.8, bf16[384,1024]{1,0:T(8,128)(2,1)S(1)} %collective-permute-done.refs_1_.refs_2_, f32[768,1]{1,0:T(8,128)S(1)} %get-tuple-element.27.refs_3_, ...), custom_call_target="tpu_custom_call" | custom-call | flops 2415919104 | bytes 9437184 | tf_op jit(solution)/shard_map/pallas_call | solution.py:172
  62.1 0.0 collective-permute-done.10.refs_7_
  62.1 0.0 collective-permute-done.9.refs_6_
  62.1 5.0 %shard_map.44 = (f32[768,1]{1,0:T(8,128)S(1)}, f32[768,1]{1,0:T(8,128)S(1)}, f32[768,1024]{1,0:T(8,128)S(1)}) custom-call(s32[32,32]{1,0:T(8,128)S(1)} %copy-done.1, bf16[384,1024]{1,0:T(8,128)(2,1)S(1)} %bitcast.9, bf16[384,1024]{1,0:T(8,128)(2,1)S(1)} %collective-permute-done.refs_1_.refs_2_, f32[768,1]{1,0:T(8,128)S(1)} %get-tuple-element.30.refs_3_, ...), custom_call_target="tpu_custom_call" | custom-call | flops 2415919104 | bytes 9437184 | tf_op jit(solution)/shard_map/pallas_call | solution.py:172
  67.1 0.0 collective-permute-done.11.refs_6_
  67.1 1.7 %collective-permute-done.12.refs_7_ = bf16[384,1024]{1,0:T(8,128)(2,1)S(1)} collective-permute-done((bf16[384,1024]{1,0:T(8,128)(2,1)S(1)}, bf16[384,1024]{1,0:T(8,128)(2,1)S(1)}, u32[]{:S(2)}, u32[]{:S(2)}) %collective-permute-start.12) | collective-permute-done | bytes 786464 | tf_op jit(solution)/shard_map/ppermute | solution.py:29
  68.8 5.6 %shard_map.45 = (f32[384,1024]{1,0:T(8,128)S(1)}, f32[384,1024]{1,0:T(8,128)S(1)}, f32[2,384]{1,0:T(2,128)S(1)}, f32[2,384]{1,0:T(2,128)S(1)}) custom-call(s32[32,32]{1,0:T(8,128)S(1)} %copy-done.1, bf16[384,1024]{1,0:T(8,128)(2,1)S(1)} %bitcast.10, bf16[384,1024]{1,0:T(8,128)(2,1)S(1)} %collective-permute-done.refs_1_.refs_2_, ...), custom_call_target="tpu_custom_call" | custom-call | flops 2415919104 | bytes 9437184 | tf_op jit(solution)/shard_map/pallas_call | solution.py:172
  74.4 2.2 %collective-permute-start.13 = (f32[384,1024]{1,0:T(8,128)S(1)}, f32[384,1024]{1,0:T(8,128)S(1)}, u32[]{:S(2)}, u32[]{:S(2)}) collective-permute-start(f32[384,1024]{1,0:T(8,128)S(1)} %get-tuple-element.38), channel_id=1, source_target_pairs={{0,1},{1,0},{2,3},{3,2},{4,5},{5,4},{6,7},{7,6},{8,9},{9,8},{10,11... | collective-permute-start | bytes 4718600 | tf_op jit(solution)/shard_map/ppermute | solution.py:29
  76.5 0.1 collective-permute-start.14
  76.6 0.0 collective-permute-start.15
  76.6 2.0 %collective-permute-start.16 = (f32[2,384]{1,0:T(2,128)S(1)}, f32[2,384]{1,0:T(2,128)S(1)}, u32[]{:S(2)}, u32[]{:S(2)}) collective-permute-start(f32[2,384]{1,0:T(2,128)S(1)} %get-tuple-element.40), channel_id=1, source_target_pairs={{0,129},{1,128},{2,131},{3,130},{4,133},{5,132},{6,135},{7,134},{8... | collective-permute-start | bytes 9224 | tf_op jit(solution)/shard_map/ppermute | solution.py:29
  78.7 0.9 %collective-permute-done.14.stat_in_ref = f32[2,384]{1,0:T(2,128)S(1)} collective-permute-done((f32[2,384]{1,0:T(2,128)S(1)}, f32[2,384]{1,0:T(2,128)S(1)}, u32[]{:S(2)}, u32[]{:S(2)}) %collective-permute-start.14) | collective-permute-done | bytes 3104 | tf_op jit(solution)/shard_map/ppermute | solution.py:29
  79.6 0.0 collective-permute-done.15.far_stat_ref
  79.6 0.7 collective-permute-done.16.far_stat_in_ref
  80.2 0.0 collective-permute-done.13.sum_in_ref
  80.2 1.4 %shard_map.46 = (bf16[384,1024]{1,0:T(8,128)(2,1)}, f32[1,384]{1,0:T(1,128)}) custom-call(f32[384,1024]{1,0:T(8,128)S(1)} %get-tuple-element.37.sum_ref, f32[384,1024]{1,0:T(8,128)S(1)} %collective-permute-done.13.sum_in_ref, f32[2,384]{1,0:T(2,128)S(1)} %get-tuple-element.39.stat_ref, f32[2,384]{1,0:T(2,128)S(1)} %collective-permute-done.14.stat_in_ref, ...), custom_call_target="tpu_custom_call" | custom-call | tf_op jit(solution)/shard_map/pallas_call | solution.py:207
Async XLA Ops:
  0.6 17.9 %collective-permute-start.1 = (bf16[384,1024]{1,0:T(8,128)(2,1)}, bf16[384,1024]{1,0:T(8,128)(2,1)S(1)}, u32[]{:S(2)}, u32[]{:S(2)}) collective-permute-start(bf16[384,1024]{1,0:T(8,128)(2,1)} %bitcast.2), channel_id=1, source_target_pairs={{0,4},{1,125},{2,6},{3,127},{4,8},{5,1},{6,10},{7,3},{8,12},{9,5},... | collective-permute-start | bytes 2359304 | tf_op jit(solution)/shard_map/ppermute | solution.py:29
  9.3 15.7 %collective-permute-start.3 = (bf16[384,1024]{1,0:T(8,128)(2,1)}, bf16[384,1024]{1,0:T(8,128)(2,1)S(1)}, u32[]{:S(2)}, u32[]{:S(2)}) collective-permute-start(bf16[384,1024]{1,0:T(8,128)(2,1)} %bitcast.3), channel_id=1, source_target_pairs={{0,128},{1,129},{2,130},{3,131},{4,132},{5,133},{6,134},{7,135},{8... | collective-permute-start | bytes 2359304 | tf_op jit(solution)/shard_map/ppermute | solution.py:29
  10.6 16.5 %collective-permute-start.4 = (bf16[384,1024]{1,0:T(8,128)(2,1)}, bf16[384,1024]{1,0:T(8,128)(2,1)S(1)}, u32[]{:S(2)}, u32[]{:S(2)}) collective-permute-start(bf16[384,1024]{1,0:T(8,128)(2,1)} %bitcast.4), channel_id=1, source_target_pairs={{0,130},{1,131},{2,128},{3,129},{4,134},{5,135},{6,132},{7,133},{8... | collective-permute-start | bytes 2359304 | tf_op jit(solution)/shard_map/ppermute | solution.py:29
  12.5 14.6 %collective-permute-start = (bf16[384,1024]{1,0:T(8,128)(2,1)}, bf16[384,1024]{1,0:T(8,128)(2,1)S(1)}, u32[]{:S(2)}, u32[]{:S(2)}) collective-permute-start(bf16[384,1024]{1,0:T(8,128)(2,1)} %bitcast.5), channel_id=1, source_target_pairs={{0,1},{1,0},{2,3},{3,2},{4,5},{5,4},{6,7},{7,6},{8,9},{9,8},{10,11... | collective-permute-start | bytes 2359304 | tf_op jit(solution)/shard_map/ppermute | solution.py:29
  18.6 15.6 %collective-permute-start.2 = (bf16[384,1024]{1,0:T(8,128)(2,1)S(1)}, bf16[384,1024]{1,0:T(8,128)(2,1)S(1)}, u32[]{:S(2)}, u32[]{:S(2)}) collective-permute-start(bf16[384,1024]{1,0:T(8,128)(2,1)S(1)} %collective-permute-done.1), channel_id=1, source_target_pairs={{0,4},{1,125},{2,6},{3,127},{4,8},{5,1},{6,10},{7,3},{8,12},{9,5},... | collective-permute-start | bytes 2359304 | tf_op jit(solution)/shard_map/ppermute | solution.py:29
  23.7 17.5 %collective-permute-start.5 = (bf16[384,1024]{1,0:T(8,128)(2,1)S(1)}, bf16[384,1024]{1,0:T(8,128)(2,1)S(1)}, u32[]{:S(2)}, u32[]{:S(2)}) collective-permute-start(bf16[384,1024]{1,0:T(8,128)(2,1)S(1)} %collective-permute-done.1), channel_id=1, source_target_pairs={{0,128},{1,129},{2,130},{3,131},{4,132},{5,133},{6,134},{7,135},{8... | collective-permute-start | bytes 2359304 | tf_op jit(solution)/shard_map/ppermute | solution.py:29
  25.0 18.4 %collective-permute-start.7 = (bf16[384,1024]{1,0:T(8,128)(2,1)S(1)}, bf16[384,1024]{1,0:T(8,128)(2,1)S(1)}, u32[]{:S(2)}, u32[]{:S(2)}) collective-permute-start(bf16[384,1024]{1,0:T(8,128)(2,1)S(1)} %collective-permute-done.3.refs_2_), channel_id=1, source_target_pairs={{0,124},{1,5},{2,126},{3,7},{4,0},{5,9},{6,2},{7,11},{8,4},{9,13},... | collective-permute-start | bytes 2359304 | tf_op jit(solution)/shard_map/ppermute | solution.py:29
  27.1 24.8 %collective-permute-start.8 = (bf16[384,1024]{1,0:T(8,128)(2,1)S(1)}, bf16[384,1024]{1,0:T(8,128)(2,1)S(1)}, u32[]{:S(2)}, u32[]{:S(2)}) collective-permute-start(bf16[384,1024]{1,0:T(8,128)(2,1)S(1)} %collective-permute-done.4.refs_3_), channel_id=1, source_target_pairs={{0,124},{1,5},{2,126},{3,7},{4,0},{5,9},{6,2},{7,11},{8,4},{9,13},... | collective-permute-start | bytes 2359304 | tf_op jit(solution)/shard_map/ppermute | solution.py:29
  27.2 24.8 %collective-permute-start.6 = (bf16[384,1024]{1,0:T(8,128)(2,1)S(1)}, bf16[384,1024]{1,0:T(8,128)(2,1)S(1)}, u32[]{:S(2)}, u32[]{:S(2)}) collective-permute-start(bf16[384,1024]{1,0:T(8,128)(2,1)S(1)} %collective-permute-done.1), channel_id=1, source_target_pairs={{0,130},{1,131},{2,128},{3,129},{4,134},{5,135},{6,132},{7,133},{8... | collective-permute-start | bytes 2359304 | tf_op jit(solution)/shard_map/ppermute | solution.py:29
  28.8 1.1 %copy-start = (bf16[1,384,1024]{2,1,0:T(8,128)(2,1)S(1)}, bf16[1,384,1024]{2,1,0:T(8,128)(2,1)}, u32[]{:S(2)}) copy-start(bf16[1,384,1024]{2,1,0:T(8,128)(2,1)} %param.2) | copy-start | bytes 2359300
  29.9 22.0 %copy-start.1 = (s32[32,32]{1,0:T(8,128)S(1)}, s32[32,32]{1,0:T(8,128)}, u32[]{:S(2)}) copy-start(s32[32,32]{1,0:T(8,128)} %refs_0_.7) | copy-start | bytes 12292
  34.1 28.0 %collective-permute-start.10 = (bf16[384,1024]{1,0:T(8,128)(2,1)S(1)}, bf16[384,1024]{1,0:T(8,128)(2,1)S(1)}, u32[]{:S(2)}, u32[]{:S(2)}) collective-permute-start(bf16[384,1024]{1,0:T(8,128)(2,1)S(1)} %collective-permute-done.2), channel_id=1, source_target_pairs={{0,130},{1,131},{2,128},{3,129},{4,134},{5,135},{6,132},{7,133},{8... | collective-permute-start | bytes 2359304 | tf_op jit(solution)/shard_map/ppermute | solution.py:29
  41.2 20.9 %collective-permute-start.9 = (bf16[384,1024]{1,0:T(8,128)(2,1)S(1)}, bf16[384,1024]{1,0:T(8,128)(2,1)S(1)}, u32[]{:S(2)}, u32[]{:S(2)}) collective-permute-start(bf16[384,1024]{1,0:T(8,128)(2,1)S(1)} %collective-permute-done.2), channel_id=1, source_target_pairs={{0,128},{1,129},{2,130},{3,131},{4,132},{5,133},{6,134},{7,135},{8... | collective-permute-start | bytes 2359304 | tf_op jit(solution)/shard_map/ppermute | solution.py:29
  43.5 23.6 %collective-permute-start.11 = (bf16[384,1024]{1,0:T(8,128)(2,1)S(1)}, bf16[384,1024]{1,0:T(8,128)(2,1)S(1)}, u32[]{:S(2)}, u32[]{:S(2)}) collective-permute-start(bf16[384,1024]{1,0:T(8,128)(2,1)S(1)} %collective-permute-done.7.refs_6_), channel_id=1, source_target_pairs={{0,124},{1,5},{2,126},{3,7},{4,0},{5,9},{6,2},{7,11},{8,4},{9,13},... | collective-permute-start | bytes 2359304 | tf_op jit(solution)/shard_map/ppermute | solution.py:29
  51.9 16.9 %collective-permute-start.12 = (bf16[384,1024]{1,0:T(8,128)(2,1)S(1)}, bf16[384,1024]{1,0:T(8,128)(2,1)S(1)}, u32[]{:S(2)}, u32[]{:S(2)}) collective-permute-start(bf16[384,1024]{1,0:T(8,128)(2,1)S(1)} %collective-permute-done.8.refs_7_), channel_id=1, source_target_pairs={{0,124},{1,5},{2,126},{3,7},{4,0},{5,9},{6,2},{7,11},{8,4},{9,13},... | collective-permute-start | bytes 2359304 | tf_op jit(solution)/shard_map/ppermute | solution.py:29
  74.4 5.9 %collective-permute-start.13 = (f32[384,1024]{1,0:T(8,128)S(1)}, f32[384,1024]{1,0:T(8,128)S(1)}, u32[]{:S(2)}, u32[]{:S(2)}) collective-permute-start(f32[384,1024]{1,0:T(8,128)S(1)} %get-tuple-element.38), channel_id=1, source_target_pairs={{0,1},{1,0},{2,3},{3,2},{4,5},{5,4},{6,7},{7,6},{8,9},{9,8},{10,11... | collective-permute-start | bytes 4718600 | tf_op jit(solution)/shard_map/ppermute | solution.py:29
  76.5 3.0 %collective-permute-start.14 = (f32[2,384]{1,0:T(2,128)S(1)}, f32[2,384]{1,0:T(2,128)S(1)}, u32[]{:S(2)}, u32[]{:S(2)}) collective-permute-start(f32[2,384]{1,0:T(2,128)S(1)} %get-tuple-element.40), channel_id=1, source_target_pairs={{0,1},{1,0},{2,3},{3,2},{4,5},{5,4},{6,7},{7,6},{8,9},{9,8},{10,11... | collective-permute-start | bytes 9224 | tf_op jit(solution)/shard_map/ppermute | solution.py:29
  76.6 2.9 %collective-permute-start.15 = (f32[2,384]{1,0:T(2,128)S(1)}, f32[2,384]{1,0:T(2,128)S(1)}, u32[]{:S(2)}, u32[]{:S(2)}) collective-permute-start(f32[2,384]{1,0:T(2,128)S(1)} %get-tuple-element.39.stat_ref), channel_id=1, source_target_pairs={{0,128},{1,129},{2,130},{3,131},{4,132},{5,133},{6,134},{7,135},{8... | collective-permute-start | bytes 9224 | tf_op jit(solution)/shard_map/ppermute | solution.py:29
  76.6 3.6 %collective-permute-start.16 = (f32[2,384]{1,0:T(2,128)S(1)}, f32[2,384]{1,0:T(2,128)S(1)}, u32[]{:S(2)}, u32[]{:S(2)}) collective-permute-start(f32[2,384]{1,0:T(2,128)S(1)} %get-tuple-element.40), channel_id=1, source_target_pairs={{0,129},{1,128},{2,131},{3,130},{4,133},{5,132},{6,135},{7,134},{8... | collective-permute-start | bytes 9224 | tf_op jit(solution)/shard_map/ppermute | solution.py:29

commit v3 on v0

v3 whole, which is shorter than its diff:
```python
import functools
import math

import jax
import jax.numpy as jnp
from jax import lax
from jax.experimental import pallas as pl
from jax.experimental.pallas import tpu as pltpu
from jax.sharding import PartitionSpec as P

sharpness = 3.0
AXES = ("dir", "loop", "pb")
LOG2_E = math.log2(math.e)
VMEM = pl.BlockSpec(memory_space=pltpu.VMEM)
SMEM = pl.BlockSpec(memory_space=pltpu.SMEM)


def moved(value, route):
    sides, blocks, slabs = (lax.axis_size(axis) for axis in AXES)
    pairs = []
    for side in range(sides):
        for block in range(blocks):
            for slab in range(slabs):
                half, core = divmod(slab, 2)
                side_to, block_to, half_to, core_to = route(side, block, half, core)
                target = (side_to * blocks + block_to % blocks) * slabs + half_to * 2 + core_to
                pairs.append(((side * blocks + block) * slabs + slab, target))
    return lax.ppermute(value, AXES, pairs)


def across_near(side, block, half, core):
    return 1 - side, block, half, core


def across_far(side, block, half, core):
    return 1 - side, block, 1 - half, core


def other_half(side, block, half, core):
    return side, block, 1 - half, core


def sibling(side, block, half, core):
    return side, block, half, 1 - core


def forward(side, block, half, core):
    return side, block + 1, half, core


def backward(side, block, half, core):
    return side, block - 1, half, core


def key_bias(mask_ref, offsets, rows):
    side, block = lax.axis_index("dir"), lax.axis_index("loop")
    blocks = mask_ref.shape[0]
    column = lax.broadcasted_iota(jnp.int32, (1, rows * len(offsets)), 1)
    bias = jnp.zeros(column.shape, jnp.float32)
    for index, offset in enumerate(offsets):
        target = lax.rem(block + offset + blocks, blocks)
        flag = jnp.where(side == 1, mask_ref[block, target], mask_ref[target, block])
        here = (column >= index * rows) & (column < (index + 1) * rows)
        bias = jnp.where(here & (flag <= 0), -jnp.inf, bias)
    return bias


def flash(query_ref, key_refs, score_scale, bias, state, out, begin, chunk, chunks):
    keys = jnp.concatenate([ref[...] for ref in key_refs], axis=0)
    heres = [pl.ds(begin + index * chunk, chunk) for index in range(chunks)]
    max_ref, total_ref, sum_ref = out

    def scored(here):
        scores = lax.dot_general(
            query_ref[here, :], keys, (((1,), (1,)), ((), ())), preferred_element_type=jnp.float32
        )
        return scores if bias is None else scores + bias

    ahead = scored(heres[0])
    for index, here in enumerate(heres):
        scores = ahead
        if index + 1 < chunks:
            ahead = scored(heres[index + 1])
        new_max = jnp.max(scores, axis=1, keepdims=True)
        if state:
            old_max = state[0][here, :]
            new_max = jnp.maximum(old_max, new_max)
        weights = jnp.exp2((scores - new_max) * (score_scale * LOG2_E))
        total = jnp.sum(weights, axis=1, keepdims=True)
        blended = jnp.dot(weights.astype(jnp.bfloat16), keys, preferred_element_type=jnp.float32)
        if state:
            correction = jnp.exp2((old_max - new_max) * (score_scale * LOG2_E))
            total += state[1][here, :] * correction
            blended += state[2][here, :] * correction
        max_ref[here, :] = new_max
        total_ref[here, :] = total
        sum_ref[here, :] = blended


def thirds_kernel(one_ref, two_ref, *pieces):
    rows = one_ref.shape[0]
    size = pieces[0].shape[0]
    pieces[0][...] = one_ref[:size, :]
    pieces[1][: rows - size, :] = one_ref[size:, :]
    pieces[1][rows - size :, :] = two_ref[: 2 * size - rows, :]
    pieces[2][...] = two_ref[2 * size - rows :, :]


def parts_of(rows):
    return rows - rows // 3, rows // 3


def first_kernel(
    score_scale, near_ref, far_ref, own_ref, sibling_ref,
    max_ref, total_ref, sum_ref, pair_ref, query_ref,
):
    rows = own_ref.shape[0]
    early, late = parts_of(rows)
    query_ref[:early, :] = near_ref[:early, :]
    query_ref[early : 2 * early, :] = far_ref[:early, :]
    query_ref[2 * early : 2 * early + late, :] = near_ref[early:, :]
    query_ref[2 * early + late :, :] = far_ref[early:, :]

    flash(
        query_ref, (own_ref, sibling_ref), score_scale, None, None,
        (max_ref, total_ref, sum_ref), 0, rows, 2,
    )
    pair_ref[...] = (
        jnp.sum(
            near_ref[...].astype(jnp.float32) * own_ref[...].astype(jnp.float32),
            axis=1,
            keepdims=True,
        )
        * score_scale
    ).T


def middle_kernel(score_scale, offsets, mask_ref, query_ref, *refs):
    state, key_refs, out = refs[:3], refs[3:-3], refs[-3:]
    rows = query_ref.shape[0] // 2
    bias = key_bias(mask_ref, offsets, rows)
    flash(query_ref, key_refs, score_scale, bias, state, out, 0, rows, 2)


def in_three(line):
    high = line.astype(jnp.bfloat16).astype(jnp.float32)
    middle = (line - high).astype(jnp.bfloat16).astype(jnp.float32)
    low = line - high - middle
    row = lax.broadcasted_iota(jnp.int32, (16, line.shape[1]), 0)
    tile = jnp.where(row == 0, high, jnp.where(row == 1, middle, jnp.where(row == 2, low, 0.0)))
    return tile.astype(jnp.bfloat16)


def of_three(tile):
    return jnp.sum(tile.astype(jnp.float32), axis=0, keepdims=True)


def last_kernel(score_scale, late, mask_ref, query_ref, *refs):
    state, key_refs, refs = refs[:3], refs[3:5], list(refs[5:])
    early_logs = [refs.pop(0), refs.pop(0)] if late else []
    near_ref, far_ref, near_log_ref, far_log_ref = refs[:4]
    out = refs[4:]
    rows = near_ref.shape[0] - (16 if late else 0)
    start = query_ref.shape[0] - 2 * rows if late else 0
    bias = key_bias(mask_ref, (-2, 2), key_refs[0].shape[0])
    chunks = 1 if late else 2
    flash(query_ref, key_refs, score_scale, bias, state, out, start, 2 * rows // chunks, chunks)
    max_ref, total_ref, sum_ref = out
    for index, (part_ref, log_ref) in enumerate(
        ((near_ref, near_log_ref), (far_ref, far_log_ref))
    ):
        these = pl.ds(start + index * rows, rows)
        total = total_ref[these, :]
        part_ref[:rows, :] = (sum_ref[these, :] / total).astype(jnp.bfloat16)
        log = (max_ref[these, :] * score_scale + jnp.log(total)).T
        if late:
            early = early_logs[index].shape[1]
            log_ref[:, :early] = early_logs[index][...]
            log_ref[:, early:] = log
            part_ref[rows:, :] = jnp.zeros((16, part_ref.shape[1]), jnp.bfloat16)
            part_ref[rows:, : early + rows] = in_three(log_ref[...])
        else:
            log_ref[...] = log


def call(kernel, out, operands, scratch=(), keys=0, query_rows=0, smem=False):
    width = max(operand.shape[1] for operand in operands)
    return pl.pallas_call(
        kernel,
        out_shape=out,
        in_specs=[SMEM if smem and index == 0 else VMEM for index in range(len(operands))],
        out_specs=[VMEM] * len(out),
        scratch_shapes=list(scratch),
        compiler_params=pltpu.CompilerParams(vmem_limit_bytes=24 * 2**20),
        cost_estimate=pl.CostEstimate(
            flops=4 * keys * query_rows * width,
            bytes_accessed=2 * (keys + query_rows) * width + 8 * query_rows * width,
            transcendentals=keys * query_rows,
        ),
    )(*operands)


def held(rows, width):
    return [
        jax.ShapeDtypeStruct((rows, 1), jnp.float32),
        jax.ShapeDtypeStruct((rows, 1), jnp.float32),
        jax.ShapeDtypeStruct((rows, width), jnp.float32),
    ]


def finish_kernel(
    here_log_ref, half_log_ref, pair_ref,
    near_early_ref, near_late_ref, far_early_ref, far_late_ref, blended_ref, margin_ref,
):
    def merged(one, two):
        top = jnp.maximum(one, two)
        return top + jnp.log(jnp.exp(one - top) + jnp.exp(two - top))

    rows, early = blended_ref.shape[0], near_early_ref.shape[0]
    late = rows - early
    near_log = of_three(near_late_ref[late:, :rows])
    far_log = of_three(far_late_ref[late:, :rows])
    own_log = merged(near_log, far_log)
    margin_ref[...] = pair_ref[...] - 0.5 * (
        own_log + merged(here_log_ref[...], half_log_ref[...])
    )
    near_share, far_share = jnp.exp(near_log - own_log).T, jnp.exp(far_log - own_log).T
    for here, count, near_ref, far_ref in (
        (slice(0, early), early, near_early_ref, far_early_ref),
        (slice(early, rows), late, near_late_ref, far_late_ref),
    ):
        blended_ref[here, :] = (
            near_ref[:count, :].astype(jnp.float32) * near_share[here, :]
            + far_ref[:count, :].astype(jnp.float32) * far_share[here, :]
        ).astype(jnp.bfloat16)


def after(value, *others):
    return lax.optimization_barrier((value, *others))[0]


def shards(embeddings, block_mask):
    own = embeddings[0]
    rows, width = own.shape
    early, late = parts_of(rows)
    score_scale = sharpness / math.sqrt(width)
    line = jax.ShapeDtypeStruct((1, rows), jnp.float32)

    near = moved(own, across_near)
    far = moved(own, across_far)
    before_1 = moved(own, forward)
    after_1 = moved(own, backward)
    own_sib = moved(own, sibling)

    before_2, after_2 = moved(before_1, forward), moved(after_1, backward)
    piece = jax.ShapeDtypeStruct((2 * rows // 3, width), own.dtype)
    ring_1 = call(thirds_kernel, [piece] * 3, [before_1, after_1])
    ring_1_sib = [moved(value, sibling) for value in ring_1]
    *state, pair_score, queries = call(
        functools.partial(first_kernel, score_scale),
        held(2 * rows, width) + [line, jax.ShapeDtypeStruct((2 * rows, width), jnp.bfloat16)],
        [near, far, own, own_sib],
    )
    state = call(
        functools.partial(middle_kernel, score_scale, (-1, 1, -1, 1)),
        held(2 * rows, width),
        [block_mask, queries, *state, before_1, after_1, *ring_1_sib],
        smem=True,
    )
    before_2, after_2, state = lax.optimization_barrier((before_2, after_2, state))
    before_2_sib, after_2_sib = moved(before_2, sibling), moved(after_2, sibling)
    state = call(
        functools.partial(middle_kernel, score_scale, (-2, 2)),
        held(2 * rows, width),
        [block_mask, queries, *state, before_2, after_2],
        keys=2 * rows, query_rows=2 * rows, smem=True,
    )
    logs, sent = [], []
    for size in (early, late):
        near_part, far_part, *logs = call(
            functools.partial(last_kernel, score_scale, bool(sent)),
            [jax.ShapeDtypeStruct((size + (16 if sent else 0), width), jnp.bfloat16)] * 2
            + [jax.ShapeDtypeStruct((1, rows if sent else size), jnp.float32)] * 2,
            [block_mask, queries, *state, before_2_sib, after_2_sib, *logs],
            scratch=[pltpu.VMEM(a.shape, a.dtype) for a in held(2 * rows, width)],
            keys=2 * rows, query_rows=2 * size, smem=True,
        )
        sent.append((moved(near_part, across_near), moved(far_part, across_far)))
    near_log, far_log = logs
    blended, margin = call(
        finish_kernel,
        [jax.ShapeDtypeStruct((rows, width), jnp.bfloat16), line],
        [
            near_log,
            moved(far_log, other_half),
            pair_score,
            sent[0][0], sent[1][0], sent[0][1], sent[1][1],
        ],
    )
    return (blended[None], margin)


def solution(mesh):
    placed = (P("dir", ("loop", "pb"), None), P())
    return jax.shard_map(
        shards,
        mesh=mesh,
        in_specs=placed,
        out_specs=(P("dir", ("loop", "pb"), None), P("dir", ("loop", "pb"))),
        check_vma=False,
    )
```

time: 311 us -> 79.9 us (0.26)
  waiting for transfers between devices: 238 us -> 28.7 us
  matrix products: 33.8 us -> 0 us
  Pallas kernels: 0 us -> 19.7 us
  between operations: 17.2 us -> 0.76 us
  starting transfers between devices: 13.6 us -> 29.5 us
  other arithmetic: 5.22 us -> 0 us
    ppermute x6 -> x17, waiting for transfers between devices: 198 us -> 28.7 us  [moved(): return lax.ppermute(value, AXES, pairs)]
    all_gather x1 -> x0, waiting for transfers between devices: 40.5 us -> none  [shards(): key_block = lax.all_gather(counterpart, 'pb', axis=0, tiled=True)]
    dot_general x10 -> x0, matrix products: 33.8 us -> none  [the longest x5 17.1 us: absorb(): jnp.einsum('qd,kd->qk', own_rows, keys_here, preferred_element_type=jnp.f...]
    pallas_call x0 -> x7, Pallas kernels: none -> 19.7 us  [call(): pl.pallas_call(kernel, out_shape=out, in_specs=[SMEM if smem and index ==...]
    ppermute x6 -> x17, starting transfers between devices: 13.6 us -> 29.5 us  [moved(): return lax.ppermute(value, AXES, pairs)]
    reduce_sum x5 -> x0, other arithmetic: 5.18 us -> none  [the longest x3 2.09 us: absorb(): denominator = denominator * correction + jnp.sum(weights, axis=1)]
  transfers between devices with their start and end apart: 7 -> 17, of which waited for: 4 -> 3; matrix products, arithmetic and copies ran while one was open for 11% -> 0% of each run, Pallas kernels for 0% -> 19%
where the time goes in v3:
time: 79.9 us; the launch traced here: 79.8 us
  starting transfers between devices  29.5 us (37%)
  waiting for transfers between devices  28.7 us (36%)
  Pallas kernels  19.7 us (25%)
  local copies, waits for them, and re-layouts  1.14 us (1%)
    ppermute x17, starting transfers between devices, moved(): return lax.ppermute(value, AXES, pairs)  29.5 us
    ppermute x17, waiting for transfers between devices, moved(): return lax.ppermute(value, AXES, pairs)  28.7 us
    pallas_call x7, Pallas kernels, call(): pl.pallas_call(kernel, out_shape=out, in_specs=[SMEM if smem and index ==...  19.7 us
  transfers between devices with their start and end apart: 17, of which 3 were waited for; matrix products, arithmetic and copies ran while one was open for 0% of the time, Pallas kernels for 19%

profile of v3, /device:TPU:1, one launch (start us, length us, event | category | flops | bytes accessed | tf_op | source)
XLA Modules:
  0.0 79.8 jit_solution(9624449355462314718)
XLA Ops:
  0.6 0.0 copy-start.1
  0.6 2.5 %collective-permute-start.3 = (bf16[384,1024]{1,0:T(8,128)(2,1)}, bf16[384,1024]{1,0:T(8,128)(2,1)S(1)}, u32[]{:S(2)}, u32[]{:S(2)}) collective-permute-start(bf16[384,1024]{1,0:T(8,128)(2,1)} %bitcast.2), channel_id=1, source_target_pairs={{0,4},{1,5},{2,6},{3,7},{4,8},{5,9},{6,10},{7,11},{8,12},{9,13},{1... | collective-permute-start | bytes 2359304 | tf_op jit(solution)/shard_map/ppermute | solution.py:28
  3.2 6.2 %collective-permute-start.5 = (bf16[384,1024]{1,0:T(8,128)(2,1)}, bf16[384,1024]{1,0:T(8,128)(2,1)S(1)}, u32[]{:S(2)}, u32[]{:S(2)}) collective-permute-start(bf16[384,1024]{1,0:T(8,128)(2,1)} %bitcast.3), channel_id=1, source_target_pairs={{0,124},{1,125},{2,126},{3,127},{4,0},{5,1},{6,2},{7,3},{8,4},{9,5... | collective-permute-start | bytes 2359304 | tf_op jit(solution)/shard_map/ppermute | solution.py:28
  9.4 1.3 %collective-permute-start = (bf16[384,1024]{1,0:T(8,128)(2,1)}, bf16[384,1024]{1,0:T(8,128)(2,1)S(1)}, u32[]{:S(2)}, u32[]{:S(2)}) collective-permute-start(bf16[384,1024]{1,0:T(8,128)(2,1)} %bitcast.4), channel_id=1, source_target_pairs={{0,128},{1,129},{2,130},{3,131},{4,132},{5,133},{6,134},{7,135},{8... | collective-permute-start | bytes 2359304 | tf_op jit(solution)/shard_map/ppermute | solution.py:28
  10.7 1.9 %collective-permute-start.1 = (bf16[384,1024]{1,0:T(8,128)(2,1)}, bf16[384,1024]{1,0:T(8,128)(2,1)S(1)}, u32[]{:S(2)}, u32[]{:S(2)}) collective-permute-start(bf16[384,1024]{1,0:T(8,128)(2,1)} %bitcast.5), channel_id=1, source_target_pairs={{0,130},{1,131},{2,128},{3,129},{4,134},{5,135},{6,132},{7,133},{8... | collective-permute-start | bytes 2359304 | tf_op jit(solution)/shard_map/ppermute | solution.py:28
  12.6 1.5 %collective-permute-start.2 = (bf16[384,1024]{1,0:T(8,128)(2,1)}, bf16[384,1024]{1,0:T(8,128)(2,1)S(1)}, u32[]{:S(2)}, u32[]{:S(2)}) collective-permute-start(bf16[384,1024]{1,0:T(8,128)(2,1)} %bitcast.6), channel_id=1, source_target_pairs={{0,1},{1,0},{2,3},{3,2},{4,5},{5,4},{6,7},{7,6},{8,9},{9,8},{10,11... | collective-permute-start | bytes 2359304 | tf_op jit(solution)/shard_map/ppermute | solution.py:28
  14.1 12.7 %collective-permute-done.3.one_ref.refs_3_ = bf16[384,1024]{1,0:T(8,128)(2,1)S(1)} collective-permute-done((bf16[384,1024]{1,0:T(8,128)(2,1)}, bf16[384,1024]{1,0:T(8,128)(2,1)S(1)}, u32[]{:S(2)}, u32[]{:S(2)}) %collective-permute-start.3) | collective-permute-done | bytes 786464 | tf_op jit(solution)/shard_map/ppermute | solution.py:28
  26.8 0.0 collective-permute-start.4
  26.8 0.0 collective-permute-done.5.two_ref.refs_4_
  26.8 4.8 %collective-permute-start.6 = (bf16[384,1024]{1,0:T(8,128)(2,1)S(1)}, bf16[384,1024]{1,0:T(8,128)(2,1)S(1)}, u32[]{:S(2)}, u32[]{:S(2)}) collective-permute-start(bf16[384,1024]{1,0:T(8,128)(2,1)S(1)} %collective-permute-done.5.two_ref.refs_4_), channel_id=1, source_target_pairs={{0,124},{1,125},{2,126},{3,127},{4,0},{5,1},{6,2},{7,3},{8,4},{9,5... | collective-permute-start | bytes 2359304 | tf_op jit(solution)/shard_map/ppermute | solution.py:28
  31.6 0.1 shard_map.42
  31.7 0.0 collective-permute-done.near_ref
  31.7 1.9 %collective-permute-start.7 = (bf16[256,1024]{1,0:T(8,128)(2,1)S(1)}, bf16[256,1024]{1,0:T(8,128)(2,1)S(1)}, u32[]{:S(2)}, u32[]{:S(2)}) collective-permute-start(bf16[256,1024]{1,0:T(8,128)(2,1)S(1)} %get-tuple-element.35), channel_id=1, source_target_pairs={{0,1},{1,0},{2,3},{3,2},{4,5},{5,4},{6,7},{7,6},{8,9},{9,8},{10,11... | collective-permute-start | bytes 1572872 | tf_op jit(solution)/shard_map/ppermute | solution.py:28
  33.6 0.0 collective-permute-done.1.far_ref
  33.6 0.1 collective-permute-start.8
  33.7 0.0 collective-permute-done.2.sibling_ref
  33.7 0.4 collective-permute-start.9
  34.1 0.0 copy-start
  34.1 1.1 %copy-done = bf16[1,384,1024]{2,1,0:T(8,128)(2,1)S(1)} copy-done((bf16[1,384,1024]{2,1,0:T(8,128)(2,1)S(1)}, bf16[1,384,1024]{2,1,0:T(8,128)(2,1)}, u32[]{:S(2)}) %copy-start) | copy-done | bytes 786456
  35.2 2.7 %shard_map.41 = (f32[768,1]{1,0:T(8,128)S(1)}, f32[768,1]{1,0:T(8,128)S(1)}, f32[768,1024]{1,0:T(8,128)S(1)}, f32[1,384]{1,0:T(1,128)S(1)}, bf16[768,1024]{1,0:T(8,128)(2,1)S(1)}) custom-call(bf16[384,1024]{1,0:T(8,128)(2,1)S(1)} %collective-permute-done.near_ref, bf16[384,1024]{1,0:T(8,128)(2,1)S(1)} %collective-permute-done.1.far_ref, ...), custom_call_target="tpu_custom_call" | custom-call | tf_op jit(solution)/shard_map/pallas_call | solution.py:188
  38.0 0.0 collective-permute-done.7.refs_5_
  38.0 0.0 collective-permute-done.8.refs_6_
  38.0 0.0 collective-permute-done.9.refs_7_
  38.0 0.0 copy-done.1
  38.0 6.3 %shard_map.43 = (f32[768,1]{1,0:T(8,128)S(1)}, f32[768,1]{1,0:T(8,128)S(1)}, f32[768,1024]{1,0:T(8,128)S(1)}) custom-call(s32[32,32]{1,0:T(8,128)S(1)} %copy-done.1, bf16[768,1024]{1,0:T(8,128)(2,1)S(1)} %get-tuple-element.31.query_ref, f32[768,1]{1,0:T(8,128)S(1)} %get-tuple-element.32.refs_0_, f32[768,1]{1,0:T(8,128)S(1)} %get-tuple-element.33.refs_1_, ...), custom_call_target="tpu_custom_call" | custom-call | tf_op jit(solution)/shard_map/pallas_call | solution.py:188
  44.3 3.6 %collective-permute-done.4.refs_3_ = bf16[384,1024]{1,0:T(8,128)(2,1)S(1)} collective-permute-done((bf16[384,1024]{1,0:T(8,128)(2,1)S(1)}, bf16[384,1024]{1,0:T(8,128)(2,1)S(1)}, u32[]{:S(2)}, u32[]{:S(2)}) %collective-permute-start.4) | collective-permute-done | bytes 786464 | tf_op jit(solution)/shard_map/ppermute | solution.py:28
  47.9 0.0 collective-permute-done.6.refs_4_
  47.9 2.2 %collective-permute-start.10 = (bf16[384,1024]{1,0:T(8,128)(2,1)S(1)}, bf16[384,1024]{1,0:T(8,128)(2,1)S(1)}, u32[]{:S(2)}, u32[]{:S(2)}) collective-permute-start(bf16[384,1024]{1,0:T(8,128)(2,1)S(1)} %collective-permute-done.4.refs_3_), channel_id=1, source_target_pairs={{0,1},{1,0},{2,3},{3,2},{4,5},{5,4},{6,7},{7,6},{8,9},{9,8},{10,11... | collective-permute-start | bytes 2359304 | tf_op jit(solution)/shard_map/ppermute | solution.py:28
  50.1 0.0 collective-permute-start.11
  50.1 3.7 %shard_map.44 = (f32[768,1]{1,0:T(8,128)S(1)}, f32[768,1]{1,0:T(8,128)S(1)}, f32[768,1024]{1,0:T(8,128)S(1)}) custom-call(s32[32,32]{1,0:T(8,128)S(1)} %copy-done.1, bf16[768,1024]{1,0:T(8,128)(2,1)S(1)} %get-tuple-element.31.query_ref, f32[768,1]{1,0:T(8,128)S(1)} %get-tuple-element.41.refs_0_, f32[768,1]{1,0:T(8,128)S(1)} %get-tuple-element.42.refs_1_, ...), custom_call_target="tpu_custom_call" | custom-call | flops 2415919104 | bytes 9437184 | tf_op jit(solution)/shard_map/pallas_call | solution.py:188
  53.8 0.0 collective-permute-done.10.refs_3_
  53.8 0.0 collective-permute-done.11.refs_4_
  53.8 2.8 %shard_map.45 = (bf16[256,1024]{1,0:T(8,128)(2,1)S(1)}, bf16[256,1024]{1,0:T(8,128)(2,1)S(1)}, f32[1,256]{1,0:T(1,128)S(1)}, f32[1,256]{1,0:T(1,128)S(1)}) custom-call(s32[32,32]{1,0:T(8,128)S(1)} %copy-done.1, bf16[768,1024]{1,0:T(8,128)(2,1)S(1)} %get-tuple-element.31.query_ref, f32[768,1]{1,0:T(8,128)S(1)} %get-tuple-element.46.refs_0_, ...), custom_call_target="tpu_custom_call" | custom-call | flops 1610612736 | bytes 6815744 | tf_op jit(solution)/shard_map/pallas_call | solution.py:188
  56.7 1.4 %collective-permute-start.13 = (bf16[256,1024]{1,0:T(8,128)(2,1)S(1)}, bf16[256,1024]{1,0:T(8,128)(2,1)S(1)}, u32[]{:S(2)}, u32[]{:S(2)}) collective-permute-start(bf16[256,1024]{1,0:T(8,128)(2,1)S(1)} %get-tuple-element.54), channel_id=1, source_target_pairs={{0,128},{1,129},{2,130},{3,131},{4,132},{5,133},{6,134},{7,135},{8... | collective-permute-start | bytes 1572872 | tf_op jit(solution)/shard_map/ppermute | solution.py:28
  58.1 1.9 %collective-permute-start.15 = (bf16[256,1024]{1,0:T(8,128)(2,1)S(1)}, bf16[256,1024]{1,0:T(8,128)(2,1)S(1)}, u32[]{:S(2)}, u32[]{:S(2)}) collective-permute-start(bf16[256,1024]{1,0:T(8,128)(2,1)S(1)} %get-tuple-element.56), channel_id=1, source_target_pairs={{0,130},{1,131},{2,128},{3,129},{4,134},{5,135},{6,132},{7,133},{8... | collective-permute-start | bytes 1572872 | tf_op jit(solution)/shard_map/ppermute | solution.py:28
  60.0 2.6 %shard_map.46 = (bf16[144,1024]{1,0:T(8,128)(2,1)S(1)}, bf16[144,1024]{1,0:T(8,128)(2,1)S(1)}, f32[1,384]{1,0:T(1,128)S(1)}, f32[1,384]{1,0:T(1,128)S(1)}) custom-call(s32[32,32]{1,0:T(8,128)S(1)} %copy-done.1, bf16[768,1024]{1,0:T(8,128)(2,1)S(1)} %get-tuple-element.31.query_ref, f32[768,1]{1,0:T(8,128)S(1)} %get-tuple-element.46.refs_0_, ...), custom_call_target="tpu_custom_call" | custom-call | flops 805306368 | bytes 4194304 | tf_op jit(solution)/shard_map/pallas_call | solution.py:188
  62.6 0.5 collective-permute-start.14
  63.1 0.6 collective-permute-start.16
  63.7 2.2 %collective-permute-start.12 = (f32[1,384]{1,0:T(1,128)S(1)}, f32[1,384]{1,0:T(1,128)S(1)}, u32[]{:S(2)}, u32[]{:S(2)}) collective-permute-start(f32[1,384]{1,0:T(1,128)S(1)} %get-tuple-element.52), channel_id=1, source_target_pairs={{0,2},{1,3},{2,0},{3,1},{4,6},{5,7},{6,4},{7,5},{8,10},{9,11},{10,... | collective-permute-start | bytes 4616 | tf_op jit(solution)/shard_map/ppermute | solution.py:28
  65.9 12.4 %collective-permute-done.12.half_log_ref = f32[1,384]{1,0:T(1,128)S(1)} collective-permute-done((f32[1,384]{1,0:T(1,128)S(1)}, f32[1,384]{1,0:T(1,128)S(1)}, u32[]{:S(2)}, u32[]{:S(2)}) %collective-permute-start.12) | collective-permute-done | bytes 1568 | tf_op jit(solution)/shard_map/ppermute | solution.py:28
  78.3 0.0 collective-permute-done.14.near_late_ref
  78.3 0.0 collective-permute-done.16.far_late_ref
  78.3 0.0 collective-permute-done.13.near_early_ref
  78.3 0.0 collective-permute-done.15.far_early_ref
  78.3 1.4 %shard_map.47 = (bf16[384,1024]{1,0:T(8,128)(2,1)}, f32[1,384]{1,0:T(1,128)}) custom-call(f32[1,384]{1,0:T(1,128)S(1)} %get-tuple-element.51.here_log_ref, f32[1,384]{1,0:T(1,128)S(1)} %collective-permute-done.12.half_log_ref, f32[1,384]{1,0:T(1,128)S(1)} %get-tuple-element.53.pair_ref, bf16[256,1024]{1,0:T(8,128)(2,1)S(1)} %collective-permute-done.13.near_early_ref, ...), custom_call_target="tpu_custom_call" | custom-call | tf_op jit(solution)/shard_map/pallas_call | solution.py:188
Async XLA Ops:
  0.6 37.4 %copy-start.1 = (s32[32,32]{1,0:T(8,128)S(1)}, s32[32,32]{1,0:T(8,128)}, u32[]{:S(2)}) copy-start(s32[32,32]{1,0:T(8,128)} %mask_ref.7) | copy-start | bytes 12292
  0.6 26.2 %collective-permute-start.3 = (bf16[384,1024]{1,0:T(8,128)(2,1)}, bf16[384,1024]{1,0:T(8,128)(2,1)S(1)}, u32[]{:S(2)}, u32[]{:S(2)}) collective-permute-start(bf16[384,1024]{1,0:T(8,128)(2,1)} %bitcast.2), channel_id=1, source_target_pairs={{0,4},{1,5},{2,6},{3,7},{4,8},{5,9},{6,10},{7,11},{8,12},{9,13},{1... | collective-permute-start | bytes 2359304 | tf_op jit(solution)/shard_map/ppermute | solution.py:28
  3.2 23.6 %collective-permute-start.5 = (bf16[384,1024]{1,0:T(8,128)(2,1)}, bf16[384,1024]{1,0:T(8,128)(2,1)S(1)}, u32[]{:S(2)}, u32[]{:S(2)}) collective-permute-start(bf16[384,1024]{1,0:T(8,128)(2,1)} %bitcast.3), channel_id=1, source_target_pairs={{0,124},{1,125},{2,126},{3,127},{4,0},{5,1},{6,2},{7,3},{8,4},{9,5... | collective-permute-start | bytes 2359304 | tf_op jit(solution)/shard_map/ppermute | solution.py:28
  9.4 22.3 %collective-permute-start = (bf16[384,1024]{1,0:T(8,128)(2,1)}, bf16[384,1024]{1,0:T(8,128)(2,1)S(1)}, u32[]{:S(2)}, u32[]{:S(2)}) collective-permute-start(bf16[384,1024]{1,0:T(8,128)(2,1)} %bitcast.4), channel_id=1, source_target_pairs={{0,128},{1,129},{2,130},{3,131},{4,132},{5,133},{6,134},{7,135},{8... | collective-permute-start | bytes 2359304 | tf_op jit(solution)/shard_map/ppermute | solution.py:28
  10.7 22.9 %collective-permute-start.1 = (bf16[384,1024]{1,0:T(8,128)(2,1)}, bf16[384,1024]{1,0:T(8,128)(2,1)S(1)}, u32[]{:S(2)}, u32[]{:S(2)}) collective-permute-start(bf16[384,1024]{1,0:T(8,128)(2,1)} %bitcast.5), channel_id=1, source_target_pairs={{0,130},{1,131},{2,128},{3,129},{4,134},{5,135},{6,132},{7,133},{8... | collective-permute-start | bytes 2359304 | tf_op jit(solution)/shard_map/ppermute | solution.py:28
  12.6 21.1 %collective-permute-start.2 = (bf16[384,1024]{1,0:T(8,128)(2,1)}, bf16[384,1024]{1,0:T(8,128)(2,1)S(1)}, u32[]{:S(2)}, u32[]{:S(2)}) collective-permute-start(bf16[384,1024]{1,0:T(8,128)(2,1)} %bitcast.6), channel_id=1, source_target_pairs={{0,1},{1,0},{2,3},{3,2},{4,5},{5,4},{6,7},{7,6},{8,9},{9,8},{10,11... | collective-permute-start | bytes 2359304 | tf_op jit(solution)/shard_map/ppermute | solution.py:28
  26.8 21.1 %collective-permute-start.4 = (bf16[384,1024]{1,0:T(8,128)(2,1)S(1)}, bf16[384,1024]{1,0:T(8,128)(2,1)S(1)}, u32[]{:S(2)}, u32[]{:S(2)}) collective-permute-start(bf16[384,1024]{1,0:T(8,128)(2,1)S(1)} %collective-permute-done.3.one_ref.refs_3_), channel_id=1, source_target_pairs={{0,4},{1,5},{2,6},{3,7},{4,8},{5,9},{6,10},{7,11},{8,12},{9,13},{1... | collective-permute-start | bytes 2359304 | tf_op jit(solution)/shard_map/ppermute | solution.py:28
  26.8 21.1 %collective-permute-start.6 = (bf16[384,1024]{1,0:T(8,128)(2,1)S(1)}, bf16[384,1024]{1,0:T(8,128)(2,1)S(1)}, u32[]{:S(2)}, u32[]{:S(2)}) collective-permute-start(bf16[384,1024]{1,0:T(8,128)(2,1)S(1)} %collective-permute-done.5.two_ref.refs_4_), channel_id=1, source_target_pairs={{0,124},{1,125},{2,126},{3,127},{4,0},{5,1},{6,2},{7,3},{8,4},{9,5... | collective-permute-start | bytes 2359304 | tf_op jit(solution)/shard_map/ppermute | solution.py:28
  31.7 6.3 %collective-permute-start.7 = (bf16[256,1024]{1,0:T(8,128)(2,1)S(1)}, bf16[256,1024]{1,0:T(8,128)(2,1)S(1)}, u32[]{:S(2)}, u32[]{:S(2)}) collective-permute-start(bf16[256,1024]{1,0:T(8,128)(2,1)S(1)} %get-tuple-element.35), channel_id=1, source_target_pairs={{0,1},{1,0},{2,3},{3,2},{4,5},{5,4},{6,7},{7,6},{8,9},{9,8},{10,11... | collective-permute-start | bytes 1572872 | tf_op jit(solution)/shard_map/ppermute | solution.py:28
  33.6 4.4 %collective-permute-start.8 = (bf16[256,1024]{1,0:T(8,128)(2,1)S(1)}, bf16[256,1024]{1,0:T(8,128)(2,1)S(1)}, u32[]{:S(2)}, u32[]{:S(2)}) collective-permute-start(bf16[256,1024]{1,0:T(8,128)(2,1)S(1)} %get-tuple-element.36), channel_id=1, source_target_pairs={{0,1},{1,0},{2,3},{3,2},{4,5},{5,4},{6,7},{7,6},{8,9},{9,8},{10,11... | collective-permute-start | bytes 1572872 | tf_op jit(solution)/shard_map/ppermute | solution.py:28
  33.7 4.3 %collective-permute-start.9 = (bf16[256,1024]{1,0:T(8,128)(2,1)S(1)}, bf16[256,1024]{1,0:T(8,128)(2,1)S(1)}, u32[]{:S(2)}, u32[]{:S(2)}) collective-permute-start(bf16[256,1024]{1,0:T(8,128)(2,1)S(1)} %get-tuple-element.37), channel_id=1, source_target_pairs={{0,1},{1,0},{2,3},{3,2},{4,5},{5,4},{6,7},{7,6},{8,9},{9,8},{10,11... | collective-permute-start | bytes 1572872 | tf_op jit(solution)/shard_map/ppermute | solution.py:28
  34.1 1.1 %copy-start = (bf16[1,384,1024]{2,1,0:T(8,128)(2,1)S(1)}, bf16[1,384,1024]{2,1,0:T(8,128)(2,1)}, u32[]{:S(2)}) copy-start(bf16[1,384,1024]{2,1,0:T(8,128)(2,1)} %param.2) | copy-start | bytes 2359300
  47.9 5.9 %collective-permute-start.10 = (bf16[384,1024]{1,0:T(8,128)(2,1)S(1)}, bf16[384,1024]{1,0:T(8,128)(2,1)S(1)}, u32[]{:S(2)}, u32[]{:S(2)}) collective-permute-start(bf16[384,1024]{1,0:T(8,128)(2,1)S(1)} %collective-permute-done.4.refs_3_), channel_id=1, source_target_pairs={{0,1},{1,0},{2,3},{3,2},{4,5},{5,4},{6,7},{7,6},{8,9},{9,8},{10,11... | collective-permute-start | bytes 2359304 | tf_op jit(solution)/shard_map/ppermute | solution.py:28
  50.1 3.7 %collective-permute-start.11 = (bf16[384,1024]{1,0:T(8,128)(2,1)S(1)}, bf16[384,1024]{1,0:T(8,128)(2,1)S(1)}, u32[]{:S(2)}, u32[]{:S(2)}) collective-permute-start(bf16[384,1024]{1,0:T(8,128)(2,1)S(1)} %collective-permute-done.6.refs_4_), channel_id=1, source_target_pairs={{0,1},{1,0},{2,3},{3,2},{4,5},{5,4},{6,7},{7,6},{8,9},{9,8},{10,11... | collective-permute-start | bytes 2359304 | tf_op jit(solution)/shard_map/ppermute | solution.py:28
  56.7 21.6 %collective-permute-start.13 = (bf16[256,1024]{1,0:T(8,128)(2,1)S(1)}, bf16[256,1024]{1,0:T(8,128)(2,1)S(1)}, u32[]{:S(2)}, u32[]{:S(2)}) collective-permute-start(bf16[256,1024]{1,0:T(8,128)(2,1)S(1)} %get-tuple-element.54), channel_id=1, source_target_pairs={{0,128},{1,129},{2,130},{3,131},{4,132},{5,133},{6,134},{7,135},{8... | collective-permute-start | bytes 1572872 | tf_op jit(solution)/shard_map/ppermute | solution.py:28
  58.1 20.2 %collective-permute-start.15 = (bf16[256,1024]{1,0:T(8,128)(2,1)S(1)}, bf16[256,1024]{1,0:T(8,128)(2,1)S(1)}, u32[]{:S(2)}, u32[]{:S(2)}) collective-permute-start(bf16[256,1024]{1,0:T(8,128)(2,1)S(1)} %get-tuple-element.56), channel_id=1, source_target_pairs={{0,130},{1,131},{2,128},{3,129},{4,134},{5,135},{6,132},{7,133},{8... | collective-permute-start | bytes 1572872 | tf_op jit(solution)/shard_map/ppermute | solution.py:28
  62.6 15.7 %collective-permute-start.14 = (bf16[144,1024]{1,0:T(8,128)(2,1)S(1)}, bf16[144,1024]{1,0:T(8,128)(2,1)S(1)}, u32[]{:S(2)}, u32[]{:S(2)}) collective-permute-start(bf16[144,1024]{1,0:T(8,128)(2,1)S(1)} %get-tuple-element.55), channel_id=1, source_target_pairs={{0,128},{1,129},{2,130},{3,131},{4,132},{5,133},{6,134},{7,135},{8... | collective-permute-start | bytes 884744 | tf_op jit(solution)/shard_map/ppermute | solution.py:28
  63.1 15.2 %collective-permute-start.16 = (bf16[144,1024]{1,0:T(8,128)(2,1)S(1)}, bf16[144,1024]{1,0:T(8,128)(2,1)S(1)}, u32[]{:S(2)}, u32[]{:S(2)}) collective-permute-start(bf16[144,1024]{1,0:T(8,128)(2,1)S(1)} %get-tuple-element.57), channel_id=1, source_target_pairs={{0,130},{1,131},{2,128},{3,129},{4,134},{5,135},{6,132},{7,133},{8... | collective-permute-start | bytes 884744 | tf_op jit(solution)/shard_map/ppermute | solution.py:28
  63.7 14.6 %collective-permute-start.12 = (f32[1,384]{1,0:T(1,128)S(1)}, f32[1,384]{1,0:T(1,128)S(1)}, u32[]{:S(2)}, u32[]{:S(2)}) collective-permute-start(f32[1,384]{1,0:T(1,128)S(1)} %get-tuple-element.52), channel_id=1, source_target_pairs={{0,2},{1,3},{2,0},{3,1},{4,6},{5,7},{6,4},{7,5},{8,10},{9,11},{10,... | collective-permute-start | bytes 4616 | tf_op jit(solution)/shard_map/ppermute | solution.py:28

commit v4 on v3

--- a/solution.py
+++ b/solution.py
@@ -13,6 +13,7 @@
 LOG2_E = math.log2(math.e)
 VMEM = pl.BlockSpec(memory_space=pltpu.VMEM)
 SMEM = pl.BlockSpec(memory_space=pltpu.SMEM)
+ANY = pl.BlockSpec(memory_space=pl.ANY)
 
 
 def moved(value, route):
@@ -44,21 +45,18 @@
     return side, block, half, 1 - core
 
 
-def forward(side, block, half, core):
-    return side, block + 1, half, core
-
-
-def backward(side, block, half, core):
-    return side, block - 1, half, core
+def onward(side, block, half, core):
+    return side, block + (1 if core == 0 else -1), half, core
 
 
 def key_bias(mask_ref, offsets, rows):
     side, block = lax.axis_index("dir"), lax.axis_index("loop")
+    sign = jnp.where(lax.axis_index("pb") % 2 == 0, -1, 1)
     blocks = mask_ref.shape[0]
     column = lax.broadcasted_iota(jnp.int32, (1, rows * len(offsets)), 1)
     bias = jnp.zeros(column.shape, jnp.float32)
     for index, offset in enumerate(offsets):
-        target = lax.rem(block + offset + blocks, blocks)
+        target = lax.rem(block + offset * sign + blocks, blocks)
         flag = jnp.where(side == 1, mask_ref[block, target], mask_ref[target, block])
         here = (column >= index * rows) & (column < (index + 1) * rows)
         bias = jnp.where(here & (flag <= 0), -jnp.inf, bias)
@@ -97,34 +95,30 @@
         sum_ref[here, :] = blended
 
 
-def thirds_kernel(one_ref, two_ref, *pieces):
-    rows = one_ref.shape[0]
-    size = pieces[0].shape[0]
-    pieces[0][...] = one_ref[:size, :]
-    pieces[1][: rows - size, :] = one_ref[size:, :]
-    pieces[1][rows - size :, :] = two_ref[: 2 * size - rows, :]
-    pieces[2][...] = two_ref[2 * size - rows :, :]
-
-
 def parts_of(rows):
     return rows - rows // 3, rows // 3
 
 
 def first_kernel(
     score_scale, near_ref, far_ref, own_ref, sibling_ref,
-    max_ref, total_ref, sum_ref, pair_ref, query_ref,
+    max_ref, total_ref, sum_ref, query_ref, held_ref, copy_sem,
 ):
     rows = own_ref.shape[0]
     early, late = parts_of(rows)
+    copy = pltpu.make_async_copy(own_ref, held_ref, copy_sem)
+    copy.start()
     query_ref[:early, :] = near_ref[:early, :]
     query_ref[early : 2 * early, :] = far_ref[:early, :]
     query_ref[2 * early : 2 * early + late, :] = near_ref[early:, :]
     query_ref[2 * early + late :, :] = far_ref[early:, :]
-
+    copy.wait()
     flash(
-        query_ref, (own_ref, sibling_ref), score_scale, None, None,
+        query_ref, (held_ref, sibling_ref), score_scale, None, None,
         (max_ref, total_ref, sum_ref), 0, rows, 2,
     )
+
+
+def pair_kernel(score_scale, near_ref, own_ref, pair_ref):
     pair_ref[...] = (
         jnp.sum(
             near_ref[...].astype(jnp.float32) * own_ref[...].astype(jnp.float32),
@@ -162,7 +156,7 @@
     out = refs[4:]
     rows = near_ref.shape[0] - (16 if late else 0)
     start = query_ref.shape[0] - 2 * rows if late else 0
-    bias = key_bias(mask_ref, (-2, 2), key_refs[0].shape[0])
+    bias = key_bias(mask_ref, (2, -2), key_refs[0].shape[0])
     chunks = 1 if late else 2
     flash(query_ref, key_refs, score_scale, bias, state, out, start, 2 * rows // chunks, chunks)
     max_ref, total_ref, sum_ref = out
@@ -183,12 +177,15 @@
             log_ref[...] = log
 
 
-def call(kernel, out, operands, scratch=(), keys=0, query_rows=0, smem=False):
+def call(kernel, out, operands, scratch=(), keys=0, query_rows=0, smem=False, left=()):
     width = max(operand.shape[1] for operand in operands)
     return pl.pallas_call(
         kernel,
         out_shape=out,
-        in_specs=[SMEM if smem and index == 0 else VMEM for index in range(len(operands))],
+        in_specs=[
+            SMEM if smem and index == 0 else ANY if index in left else VMEM
+            for index in range(len(operands))
+        ],
         out_specs=[VMEM] * len(out),
         scratch_shapes=list(scratch),
         compiler_params=pltpu.CompilerParams(vmem_limit_bytes=24 * 2**20),
@@ -248,31 +245,31 @@
 
     near = moved(own, across_near)
     far = moved(own, across_far)
-    before_1 = moved(own, forward)
-    after_1 = moved(own, backward)
     own_sib = moved(own, sibling)
-
-    before_2, after_2 = moved(before_1, forward), moved(after_1, backward)
-    piece = jax.ShapeDtypeStruct((2 * rows // 3, width), own.dtype)
-    ring_1 = call(thirds_kernel, [piece] * 3, [before_1, after_1])
-    ring_1_sib = [moved(value, sibling) for value in ring_1]
-    *state, pair_score, queries = call(
+    first_1, second_1 = moved(own, onward), moved(own_sib, onward)
+    first_2, second_2 = moved(first_1, onward), moved(second_1, onward)
+    first_1_sib, second_1_sib = moved(first_1, sibling), moved(second_1, sibling)
+    *state, queries = call(
         functools.partial(first_kernel, score_scale),
-        held(2 * rows, width) + [line, jax.ShapeDtypeStruct((2 * rows, width), jnp.bfloat16)],
+        held(2 * rows, width) + [jax.ShapeDtypeStruct((2 * rows, width), jnp.bfloat16)],
         [near, far, own, own_sib],
-    )
+        scratch=[pltpu.VMEM(own.shape, own.dtype), pltpu.SemaphoreType.DMA(())],
+        left=(2,),
+    )
+    first_2, state = lax.optimization_barrier((first_2, state))
+    first_2_sib = moved(first_2, sibling)
     state = call(
-        functools.partial(middle_kernel, score_scale, (-1, 1, -1, 1)),
+        functools.partial(middle_kernel, score_scale, (1, 1, -1, -1)),
         held(2 * rows, width),
-        [block_mask, queries, *state, before_1, after_1, *ring_1_sib],
+        [block_mask, queries, *state, first_1, second_1, first_1_sib, second_1_sib],
         smem=True,
     )
-    before_2, after_2, state = lax.optimization_barrier((before_2, after_2, state))
-    before_2_sib, after_2_sib = moved(before_2, sibling), moved(after_2, sibling)
+    second_2, state = lax.optimization_barrier((second_2, state))
+    second_2_sib = moved(second_2, sibling)
     state = call(
-        functools.partial(middle_kernel, score_scale, (-2, 2)),
+        functools.partial(middle_kernel, score_scale, (2, -2)),
         held(2 * rows, width),
-        [block_mask, queries, *state, before_2, after_2],
+        [block_mask, queries, *state, first_2, first_2_sib],
         keys=2 * rows, query_rows=2 * rows, smem=True,
     )
     logs, sent = [], []
@@ -281,12 +278,15 @@
             functools.partial(last_kernel, score_scale, bool(sent)),
             [jax.ShapeDtypeStruct((size + (16 if sent else 0), width), jnp.bfloat16)] * 2
             + [jax.ShapeDtypeStruct((1, rows if sent else size), jnp.float32)] * 2,
-            [block_mask, queries, *state, before_2_sib, after_2_sib, *logs],
+            [block_mask, queries, *state, second_2, second_2_sib, *logs],
             scratch=[pltpu.VMEM(a.shape, a.dtype) for a in held(2 * rows, width)],
             keys=2 * rows, query_rows=2 * size, smem=True,
         )
         sent.append((moved(near_part, across_near), moved(far_part, across_far)))
     near_log, far_log = logs
+    pair_score = call(
+        functools.partial(pair_kernel, score_scale), [line], [after(near, near_log), own]
+    )[0]
     blended, margin = call(
         finish_kernel,
         [jax.ShapeDtypeStruct((rows, width), jnp.bfloat16), line],

time: 79.9 us -> 76.1 us (0.952)
  waiting for transfers between devices: 28.7 us -> 20.5 us
  starting transfers between devices: 29.5 us -> 33.7 us
    ppermute x17 -> x16, waiting for transfers between devices: 28.7 us -> 20.5 us  [moved(): return lax.ppermute(value, AXES, pairs)]
    ppermute x17 -> x16, starting transfers between devices: 29.5 us -> 33.7 us  [moved(): return lax.ppermute(value, AXES, pairs)]
  transfers between devices with their start and end apart: 17 -> 16, of which waited for: 3 -> 4; matrix products, arithmetic and copies ran while one was open for 0% -> 0% of each run, Pallas kernels for 19% -> 21%
where the time goes in v4:
time: 76.1 us; the launch traced here: 76 us
  starting transfers between devices  33.7 us (44%)
  waiting for transfers between devices  20.5 us (27%)
  Pallas kernels  19.9 us (26%)
  local copies, waits for them, and re-layouts  1.14 us (1%)
    ppermute x16, starting transfers between devices, moved(): return lax.ppermute(value, AXES, pairs)  33.7 us
    ppermute x16, waiting for transfers between devices, moved(): return lax.ppermute(value, AXES, pairs)  20.5 us
    pallas_call x7, Pallas kernels, call(): pl.pallas_call(kernel, out_shape=out, in_specs=[SMEM if smem and index ==...  19.9 us
  transfers between devices with their start and end apart: 16, of which 4 were waited for; matrix products, arithmetic and copies ran while one was open for 0% of the time, Pallas kernels for 21%

profile of v4, /device:TPU:1, one launch (start us, length us, event | category | flops | bytes accessed | tf_op | source)
XLA Modules:
  0.0 76.0 jit_solution(3128404834624534477)
XLA Ops:
  0.6 3.3 %collective-permute-start.2 = (bf16[384,1024]{1,0:T(8,128)(2,1)}, bf16[384,1024]{1,0:T(8,128)(2,1)S(1)}, u32[]{:S(2)}, u32[]{:S(2)}) collective-permute-start(bf16[384,1024]{1,0:T(8,128)(2,1)} %bitcast.2), channel_id=1, source_target_pairs={{0,1},{1,0},{2,3},{3,2},{4,5},{5,4},{6,7},{7,6},{8,9},{9,8},{10,11... | collective-permute-start | bytes 2359304 | tf_op jit(solution)/shard_map/ppermute | solution.py:29
  4.0 6.0 %collective-permute-start.5 = (bf16[384,1024]{1,0:T(8,128)(2,1)}, bf16[384,1024]{1,0:T(8,128)(2,1)S(1)}, u32[]{:S(2)}, u32[]{:S(2)}) collective-permute-start(bf16[384,1024]{1,0:T(8,128)(2,1)} %bitcast.3), channel_id=1, source_target_pairs={{0,4},{1,125},{2,6},{3,127},{4,8},{5,1},{6,10},{7,3},{8,12},{9,5},... | collective-permute-start | bytes 2359304 | tf_op jit(solution)/shard_map/ppermute | solution.py:29
  10.0 0.0 collective-permute-done.2.sibling_ref
  10.0 2.1 %collective-permute-start.3 = (bf16[384,1024]{1,0:T(8,128)(2,1)S(1)}, bf16[384,1024]{1,0:T(8,128)(2,1)S(1)}, u32[]{:S(2)}, u32[]{:S(2)}) collective-permute-start(bf16[384,1024]{1,0:T(8,128)(2,1)S(1)} %collective-permute-done.2.sibling_ref), channel_id=1, source_target_pairs={{0,4},{1,125},{2,6},{3,127},{4,8},{5,1},{6,10},{7,3},{8,12},{9,5},... | collective-permute-start | bytes 2359304 | tf_op jit(solution)/shard_map/ppermute | solution.py:29
  12.1 1.3 %collective-permute-start = (bf16[384,1024]{1,0:T(8,128)(2,1)}, bf16[384,1024]{1,0:T(8,128)(2,1)S(1)}, u32[]{:S(2)}, u32[]{:S(2)}) collective-permute-start(bf16[384,1024]{1,0:T(8,128)(2,1)} %bitcast.4), channel_id=1, source_target_pairs={{0,128},{1,129},{2,130},{3,131},{4,132},{5,133},{6,134},{7,135},{8... | collective-permute-start | bytes 2359304 | tf_op jit(solution)/shard_map/ppermute | solution.py:29
  13.4 1.9 %collective-permute-start.1 = (bf16[384,1024]{1,0:T(8,128)(2,1)}, bf16[384,1024]{1,0:T(8,128)(2,1)S(1)}, u32[]{:S(2)}, u32[]{:S(2)}) collective-permute-start(bf16[384,1024]{1,0:T(8,128)(2,1)} %bitcast.5), channel_id=1, source_target_pairs={{0,130},{1,131},{2,128},{3,129},{4,134},{5,135},{6,132},{7,133},{8... | collective-permute-start | bytes 2359304 | tf_op jit(solution)/shard_map/ppermute | solution.py:29
  15.3 3.9 %collective-permute-done.5.refs_3_ = bf16[384,1024]{1,0:T(8,128)(2,1)S(1)} collective-permute-done((bf16[384,1024]{1,0:T(8,128)(2,1)}, bf16[384,1024]{1,0:T(8,128)(2,1)S(1)}, u32[]{:S(2)}, u32[]{:S(2)}) %collective-permute-start.5) | collective-permute-done | bytes 786464 | tf_op jit(solution)/shard_map/ppermute | solution.py:29
  19.2 5.1 %collective-permute-start.6 = (bf16[384,1024]{1,0:T(8,128)(2,1)S(1)}, bf16[384,1024]{1,0:T(8,128)(2,1)S(1)}, u32[]{:S(2)}, u32[]{:S(2)}) collective-permute-start(bf16[384,1024]{1,0:T(8,128)(2,1)S(1)} %collective-permute-done.5.refs_3_), channel_id=1, source_target_pairs={{0,4},{1,125},{2,6},{3,127},{4,8},{5,1},{6,10},{7,3},{8,12},{9,5},... | collective-permute-start | bytes 2359304 | tf_op jit(solution)/shard_map/ppermute | solution.py:29
  24.4 0.0 collective-permute-start.7
  24.4 3.2 %collective-permute-done.3.refs_4_ = bf16[384,1024]{1,0:T(8,128)(2,1)S(1)} collective-permute-done((bf16[384,1024]{1,0:T(8,128)(2,1)S(1)}, bf16[384,1024]{1,0:T(8,128)(2,1)S(1)}, u32[]{:S(2)}, u32[]{:S(2)}) %collective-permute-start.3) | collective-permute-done | bytes 786464 | tf_op jit(solution)/shard_map/ppermute | solution.py:29
  27.6 1.4 %collective-permute-start.8 = (bf16[384,1024]{1,0:T(8,128)(2,1)S(1)}, bf16[384,1024]{1,0:T(8,128)(2,1)S(1)}, u32[]{:S(2)}, u32[]{:S(2)}) collective-permute-start(bf16[384,1024]{1,0:T(8,128)(2,1)S(1)} %collective-permute-done.3.refs_4_), channel_id=1, source_target_pairs={{0,1},{1,0},{2,3},{3,2},{4,5},{5,4},{6,7},{7,6},{8,9},{9,8},{10,11... | collective-permute-start | bytes 2359304 | tf_op jit(solution)/shard_map/ppermute | solution.py:29
  29.0 0.0 collective-permute-done.near_ref
  29.0 3.8 %collective-permute-start.4 = (bf16[384,1024]{1,0:T(8,128)(2,1)S(1)}, bf16[384,1024]{1,0:T(8,128)(2,1)S(1)}, u32[]{:S(2)}, u32[]{:S(2)}) collective-permute-start(bf16[384,1024]{1,0:T(8,128)(2,1)S(1)} %collective-permute-done.3.refs_4_), channel_id=1, source_target_pairs={{0,4},{1,125},{2,6},{3,127},{4,8},{5,1},{6,10},{7,3},{8,12},{9,5},... | collective-permute-start | bytes 2359304 | tf_op jit(solution)/shard_map/ppermute | solution.py:29
  32.8 0.0 collective-permute-done.1.far_ref
  32.8 0.0 copy-start
  32.8 1.1 %copy-done = bf16[1,384,1024]{2,1,0:T(8,128)(2,1)S(1)} copy-done((bf16[1,384,1024]{2,1,0:T(8,128)(2,1)S(1)}, bf16[1,384,1024]{2,1,0:T(8,128)(2,1)}, u32[]{:S(2)}) %copy-start) | copy-done | bytes 786456
  33.9 0.0 copy-start.2
  33.9 2.8 %shard_map.41 = (f32[768,1]{1,0:T(8,128)S(1)}, f32[768,1]{1,0:T(8,128)S(1)}, f32[768,1024]{1,0:T(8,128)S(1)}, bf16[768,1024]{1,0:T(8,128)(2,1)S(1)}) custom-call(bf16[384,1024]{1,0:T(8,128)(2,1)S(1)} %collective-permute-done.near_ref, bf16[384,1024]{1,0:T(8,128)(2,1)S(1)} %collective-permute-done.1.far_ref, bf16[384,1024]{1,0:T(8,128)(2,1)S(1)} %bitcast.6, ...), custom_call_target="tpu_custom_call" | custom-call | tf_op jit(solution)/shard_map/pallas_call | solution.py:182
  36.8 0.0 collective-permute-done.6.refs_3_
  36.8 0.6 collective-permute-start.9
  37.4 0.0 collective-permute-done.7.refs_5_
  37.4 0.0 collective-permute-done.8.refs_6_
  37.4 0.0 copy-done.2
  37.4 6.2 %shard_map.42 = (f32[768,1]{1,0:T(8,128)S(1)}, f32[768,1]{1,0:T(8,128)S(1)}, f32[768,1024]{1,0:T(8,128)S(1)}) custom-call(s32[32,32]{1,0:T(8,128)S(1)} %copy-done.2, bf16[768,1024]{1,0:T(8,128)(2,1)S(1)} %get-tuple-element.31.query_ref, f32[768,1]{1,0:T(8,128)S(1)} %get-tuple-element.35.refs_0_, f32[768,1]{1,0:T(8,128)S(1)} %get-tuple-element.36.refs_1_, ...), custom_call_target="tpu_custom_call" | custom-call | tf_op jit(solution)/shard_map/pallas_call | solution.py:182
  43.7 0.8 collective-permute-done.4.refs_3_
  44.4 1.4 %collective-permute-start.10 = (bf16[384,1024]{1,0:T(8,128)(2,1)S(1)}, bf16[384,1024]{1,0:T(8,128)(2,1)S(1)}, u32[]{:S(2)}, u32[]{:S(2)}) collective-permute-start(bf16[384,1024]{1,0:T(8,128)(2,1)S(1)} %collective-permute-done.4.refs_3_), channel_id=1, source_target_pairs={{0,1},{1,0},{2,3},{3,2},{4,5},{5,4},{6,7},{7,6},{8,9},{9,8},{10,11... | collective-permute-start | bytes 2359304 | tf_op jit(solution)/shard_map/ppermute | solution.py:29
  45.8 0.0 collective-permute-done.9.refs_4_
  45.8 3.7 %shard_map.43 = (f32[768,1]{1,0:T(8,128)S(1)}, f32[768,1]{1,0:T(8,128)S(1)}, f32[768,1024]{1,0:T(8,128)S(1)}) custom-call(s32[32,32]{1,0:T(8,128)S(1)} %copy-done.2, bf16[768,1024]{1,0:T(8,128)(2,1)S(1)} %get-tuple-element.31.query_ref, f32[768,1]{1,0:T(8,128)S(1)} %get-tuple-element.41.refs_0_, f32[768,1]{1,0:T(8,128)S(1)} %get-tuple-element.42.refs_1_, ...), custom_call_target="tpu_custom_call" | custom-call | flops 2415919104 | bytes 9437184 | tf_op jit(solution)/shard_map/pallas_call | solution.py:182
  49.5 0.0 collective-permute-done.10.refs_4_
  49.5 2.9 %shard_map.44 = (bf16[256,1024]{1,0:T(8,128)(2,1)S(1)}, bf16[256,1024]{1,0:T(8,128)(2,1)S(1)}, f32[1,256]{1,0:T(1,128)S(1)}, f32[1,256]{1,0:T(1,128)S(1)}) custom-call(s32[32,32]{1,0:T(8,128)S(1)} %copy-done.2, bf16[768,1024]{1,0:T(8,128)(2,1)S(1)} %get-tuple-element.31.query_ref, f32[768,1]{1,0:T(8,128)S(1)} %get-tuple-element.45.refs_0_, ...), custom_call_target="tpu_custom_call" | custom-call | flops 1610612736 | bytes 6815744 | tf_op jit(solution)/shard_map/pallas_call | solution.py:182
  52.4 1.4 %collective-permute-start.12 = (bf16[256,1024]{1,0:T(8,128)(2,1)S(1)}, bf16[256,1024]{1,0:T(8,128)(2,1)S(1)}, u32[]{:S(2)}, u32[]{:S(2)}) collective-permute-start(bf16[256,1024]{1,0:T(8,128)(2,1)S(1)} %get-tuple-element.54), channel_id=1, source_target_pairs={{0,128},{1,129},{2,130},{3,131},{4,132},{5,133},{6,134},{7,135},{8... | collective-permute-start | bytes 1572872 | tf_op jit(solution)/shard_map/ppermute | solution.py:29
  53.8 1.9 %collective-permute-start.14 = (bf16[256,1024]{1,0:T(8,128)(2,1)S(1)}, bf16[256,1024]{1,0:T(8,128)(2,1)S(1)}, u32[]{:S(2)}, u32[]{:S(2)}) collective-permute-start(bf16[256,1024]{1,0:T(8,128)(2,1)S(1)} %get-tuple-element.56), channel_id=1, source_target_pairs={{0,130},{1,131},{2,128},{3,129},{4,134},{5,135},{6,132},{7,133},{8... | collective-permute-start | bytes 1572872 | tf_op jit(solution)/shard_map/ppermute | solution.py:29
  55.7 0.0 copy-start.1
  55.7 2.6 %shard_map.45 = (bf16[144,1024]{1,0:T(8,128)(2,1)S(1)}, bf16[144,1024]{1,0:T(8,128)(2,1)S(1)}, f32[1,384]{1,0:T(1,128)S(1)}, f32[1,384]{1,0:T(1,128)S(1)}) custom-call(s32[32,32]{1,0:T(8,128)S(1)} %copy-done.2, bf16[768,1024]{1,0:T(8,128)(2,1)S(1)} %get-tuple-element.31.query_ref, f32[768,1]{1,0:T(8,128)S(1)} %get-tuple-element.45.refs_0_, ...), custom_call_target="tpu_custom_call" | custom-call | flops 805306368 | bytes 4194304 | tf_op jit(solution)/shard_map/pallas_call | solution.py:182
  58.3 0.5 collective-permute-start.13
  58.7 0.6 collective-permute-start.15
  59.4 2.2 %collective-permute-start.11 = (f32[1,384]{1,0:T(1,128)S(1)}, f32[1,384]{1,0:T(1,128)S(1)}, u32[]{:S(2)}, u32[]{:S(2)}) collective-permute-start(f32[1,384]{1,0:T(1,128)S(1)} %get-tuple-element.52), channel_id=1, source_target_pairs={{0,2},{1,3},{2,0},{3,1},{4,6},{5,7},{6,4},{7,5},{8,10},{9,11},{10,... | collective-permute-start | bytes 4616 | tf_op jit(solution)/shard_map/ppermute | solution.py:29
  61.6 0.0 copy-done.1
  61.6 0.3 shard_map.46.pair_ref
  61.9 12.6 %collective-permute-done.11.half_log_ref = f32[1,384]{1,0:T(1,128)S(1)} collective-permute-done((f32[1,384]{1,0:T(1,128)S(1)}, f32[1,384]{1,0:T(1,128)S(1)}, u32[]{:S(2)}, u32[]{:S(2)}) %collective-permute-start.11) | collective-permute-done | bytes 1568 | tf_op jit(solution)/shard_map/ppermute | solution.py:29
  74.5 0.0 collective-permute-done.13.near_late_ref
  74.5 0.0 collective-permute-done.15.far_late_ref
  74.5 0.0 collective-permute-done.12.near_early_ref
  74.6 0.0 collective-permute-done.14.far_early_ref
  74.6 1.4 %shard_map.47 = (bf16[384,1024]{1,0:T(8,128)(2,1)}, f32[1,384]{1,0:T(1,128)}) custom-call(f32[1,384]{1,0:T(1,128)S(1)} %get-tuple-element.51.here_log_ref, f32[1,384]{1,0:T(1,128)S(1)} %collective-permute-done.11.half_log_ref, f32[1,384]{1,0:T(1,128)S(1)} %shard_map.46.pair_ref, bf16[256,1024]{1,0:T(8,128)(2,1)S(1)} %collective-permute-done.12.near_early_ref, ...), custom_call_target="tpu_custom_call" | custom-call | tf_op jit(solution)/shard_map/pallas_call | solution.py:182
Async XLA Ops:
  0.6 9.4 %collective-permute-start.2 = (bf16[384,1024]{1,0:T(8,128)(2,1)}, bf16[384,1024]{1,0:T(8,128)(2,1)S(1)}, u32[]{:S(2)}, u32[]{:S(2)}) collective-permute-start(bf16[384,1024]{1,0:T(8,128)(2,1)} %bitcast.2), channel_id=1, source_target_pairs={{0,1},{1,0},{2,3},{3,2},{4,5},{5,4},{6,7},{7,6},{8,9},{9,8},{10,11... | collective-permute-start | bytes 2359304 | tf_op jit(solution)/shard_map/ppermute | solution.py:29
  4.0 15.3 %collective-permute-start.5 = (bf16[384,1024]{1,0:T(8,128)(2,1)}, bf16[384,1024]{1,0:T(8,128)(2,1)S(1)}, u32[]{:S(2)}, u32[]{:S(2)}) collective-permute-start(bf16[384,1024]{1,0:T(8,128)(2,1)} %bitcast.3), channel_id=1, source_target_pairs={{0,4},{1,125},{2,6},{3,127},{4,8},{5,1},{6,10},{7,3},{8,12},{9,5},... | collective-permute-start | bytes 2359304 | tf_op jit(solution)/shard_map/ppermute | solution.py:29
  10.0 17.6 %collective-permute-start.3 = (bf16[384,1024]{1,0:T(8,128)(2,1)S(1)}, bf16[384,1024]{1,0:T(8,128)(2,1)S(1)}, u32[]{:S(2)}, u32[]{:S(2)}) collective-permute-start(bf16[384,1024]{1,0:T(8,128)(2,1)S(1)} %collective-permute-done.2.sibling_ref), channel_id=1, source_target_pairs={{0,4},{1,125},{2,6},{3,127},{4,8},{5,1},{6,10},{7,3},{8,12},{9,5},... | collective-permute-start | bytes 2359304 | tf_op jit(solution)/shard_map/ppermute | solution.py:29
  12.1 16.9 %collective-permute-start = (bf16[384,1024]{1,0:T(8,128)(2,1)}, bf16[384,1024]{1,0:T(8,128)(2,1)S(1)}, u32[]{:S(2)}, u32[]{:S(2)}) collective-permute-start(bf16[384,1024]{1,0:T(8,128)(2,1)} %bitcast.4), channel_id=1, source_target_pairs={{0,128},{1,129},{2,130},{3,131},{4,132},{5,133},{6,134},{7,135},{8... | collective-permute-start | bytes 2359304 | tf_op jit(solution)/shard_map/ppermute | solution.py:29
  13.4 19.4 %collective-permute-start.1 = (bf16[384,1024]{1,0:T(8,128)(2,1)}, bf16[384,1024]{1,0:T(8,128)(2,1)S(1)}, u32[]{:S(2)}, u32[]{:S(2)}) collective-permute-start(bf16[384,1024]{1,0:T(8,128)(2,1)} %bitcast.5), channel_id=1, source_target_pairs={{0,130},{1,131},{2,128},{3,129},{4,134},{5,135},{6,132},{7,133},{8... | collective-permute-start | bytes 2359304 | tf_op jit(solution)/shard_map/ppermute | solution.py:29
  19.2 17.5 %collective-permute-start.6 = (bf16[384,1024]{1,0:T(8,128)(2,1)S(1)}, bf16[384,1024]{1,0:T(8,128)(2,1)S(1)}, u32[]{:S(2)}, u32[]{:S(2)}) collective-permute-start(bf16[384,1024]{1,0:T(8,128)(2,1)S(1)} %collective-permute-done.5.refs_3_), channel_id=1, source_target_pairs={{0,4},{1,125},{2,6},{3,127},{4,8},{5,1},{6,10},{7,3},{8,12},{9,5},... | collective-permute-start | bytes 2359304 | tf_op jit(solution)/shard_map/ppermute | solution.py:29
  24.4 13.0 %collective-permute-start.7 = (bf16[384,1024]{1,0:T(8,128)(2,1)S(1)}, bf16[384,1024]{1,0:T(8,128)(2,1)S(1)}, u32[]{:S(2)}, u32[]{:S(2)}) collective-permute-start(bf16[384,1024]{1,0:T(8,128)(2,1)S(1)} %collective-permute-done.5.refs_3_), channel_id=1, source_target_pairs={{0,1},{1,0},{2,3},{3,2},{4,5},{5,4},{6,7},{7,6},{8,9},{9,8},{10,11... | collective-permute-start | bytes 2359304 | tf_op jit(solution)/shard_map/ppermute | solution.py:29
  27.6 9.8 %collective-permute-start.8 = (bf16[384,1024]{1,0:T(8,128)(2,1)S(1)}, bf16[384,1024]{1,0:T(8,128)(2,1)S(1)}, u32[]{:S(2)}, u32[]{:S(2)}) collective-permute-start(bf16[384,1024]{1,0:T(8,128)(2,1)S(1)} %collective-permute-done.3.refs_4_), channel_id=1, source_target_pairs={{0,1},{1,0},{2,3},{3,2},{4,5},{5,4},{6,7},{7,6},{8,9},{9,8},{10,11... | collective-permute-start | bytes 2359304 | tf_op jit(solution)/shard_map/ppermute | solution.py:29
  29.0 15.4 %collective-permute-start.4 = (bf16[384,1024]{1,0:T(8,128)(2,1)S(1)}, bf16[384,1024]{1,0:T(8,128)(2,1)S(1)}, u32[]{:S(2)}, u32[]{:S(2)}) collective-permute-start(bf16[384,1024]{1,0:T(8,128)(2,1)S(1)} %collective-permute-done.3.refs_4_), channel_id=1, source_target_pairs={{0,4},{1,125},{2,6},{3,127},{4,8},{5,1},{6,10},{7,3},{8,12},{9,5},... | collective-permute-start | bytes 2359304 | tf_op jit(solution)/shard_map/ppermute | solution.py:29
  32.8 1.1 %copy-start = (bf16[1,384,1024]{2,1,0:T(8,128)(2,1)S(1)}, bf16[1,384,1024]{2,1,0:T(8,128)(2,1)}, u32[]{:S(2)}) copy-start(bf16[1,384,1024]{2,1,0:T(8,128)(2,1)} %param.2) | copy-start | bytes 2359300
  33.9 3.5 %copy-start.2 = (s32[32,32]{1,0:T(8,128)S(1)}, s32[32,32]{1,0:T(8,128)}, u32[]{:S(2)}) copy-start(s32[32,32]{1,0:T(8,128)} %mask_ref.7) | copy-start | bytes 12292
  36.8 9.0 %collective-permute-start.9 = (bf16[384,1024]{1,0:T(8,128)(2,1)S(1)}, bf16[384,1024]{1,0:T(8,128)(2,1)S(1)}, u32[]{:S(2)}, u32[]{:S(2)}) collective-permute-start(bf16[384,1024]{1,0:T(8,128)(2,1)S(1)} %collective-permute-done.6.refs_3_), channel_id=1, source_target_pairs={{0,1},{1,0},{2,3},{3,2},{4,5},{5,4},{6,7},{7,6},{8,9},{9,8},{10,11... | collective-permute-start | bytes 2359304 | tf_op jit(solution)/shard_map/ppermute | solution.py:29
  44.4 5.1 %collective-permute-start.10 = (bf16[384,1024]{1,0:T(8,128)(2,1)S(1)}, bf16[384,1024]{1,0:T(8,128)(2,1)S(1)}, u32[]{:S(2)}, u32[]{:S(2)}) collective-permute-start(bf16[384,1024]{1,0:T(8,128)(2,1)S(1)} %collective-permute-done.4.refs_3_), channel_id=1, source_target_pairs={{0,1},{1,0},{2,3},{3,2},{4,5},{5,4},{6,7},{7,6},{8,9},{9,8},{10,11... | collective-permute-start | bytes 2359304 | tf_op jit(solution)/shard_map/ppermute | solution.py:29
  52.4 22.2 %collective-permute-start.12 = (bf16[256,1024]{1,0:T(8,128)(2,1)S(1)}, bf16[256,1024]{1,0:T(8,128)(2,1)S(1)}, u32[]{:S(2)}, u32[]{:S(2)}) collective-permute-start(bf16[256,1024]{1,0:T(8,128)(2,1)S(1)} %get-tuple-element.54), channel_id=1, source_target_pairs={{0,128},{1,129},{2,130},{3,131},{4,132},{5,133},{6,134},{7,135},{8... | collective-permute-start | bytes 1572872 | tf_op jit(solution)/shard_map/ppermute | solution.py:29
  53.8 20.8 %collective-permute-start.14 = (bf16[256,1024]{1,0:T(8,128)(2,1)S(1)}, bf16[256,1024]{1,0:T(8,128)(2,1)S(1)}, u32[]{:S(2)}, u32[]{:S(2)}) collective-permute-start(bf16[256,1024]{1,0:T(8,128)(2,1)S(1)} %get-tuple-element.56), channel_id=1, source_target_pairs={{0,130},{1,131},{2,128},{3,129},{4,134},{5,135},{6,132},{7,133},{8... | collective-permute-start | bytes 1572872 | tf_op jit(solution)/shard_map/ppermute | solution.py:29
  55.7 5.9 %copy-start.1 = (bf16[1,384,1024]{2,1,0:T(8,128)(2,1)S(1)}, bf16[1,384,1024]{2,1,0:T(8,128)(2,1)}, u32[]{:S(2)}) copy-start(bf16[1,384,1024]{2,1,0:T(8,128)(2,1)} %param.2) | copy-start | bytes 2359300
  58.3 16.3 %collective-permute-start.13 = (bf16[144,1024]{1,0:T(8,128)(2,1)S(1)}, bf16[144,1024]{1,0:T(8,128)(2,1)S(1)}, u32[]{:S(2)}, u32[]{:S(2)}) collective-permute-start(bf16[144,1024]{1,0:T(8,128)(2,1)S(1)} %get-tuple-element.55), channel_id=1, source_target_pairs={{0,128},{1,129},{2,130},{3,131},{4,132},{5,133},{6,134},{7,135},{8... | collective-permute-start | bytes 884744 | tf_op jit(solution)/shard_map/ppermute | solution.py:29
  58.7 15.8 %collective-permute-start.15 = (bf16[144,1024]{1,0:T(8,128)(2,1)S(1)}, bf16[144,1024]{1,0:T(8,128)(2,1)S(1)}, u32[]{:S(2)}, u32[]{:S(2)}) collective-permute-start(bf16[144,1024]{1,0:T(8,128)(2,1)S(1)} %get-tuple-element.57), channel_id=1, source_target_pairs={{0,130},{1,131},{2,128},{3,129},{4,134},{5,135},{6,132},{7,133},{8... | collective-permute-start | bytes 884744 | tf_op jit(solution)/shard_map/ppermute | solution.py:29
  59.4 15.2 %collective-permute-start.11 = (f32[1,384]{1,0:T(1,128)S(1)}, f32[1,384]{1,0:T(1,128)S(1)}, u32[]{:S(2)}, u32[]{:S(2)}) collective-permute-start(f32[1,384]{1,0:T(1,128)S(1)} %get-tuple-element.52), channel_id=1, source_target_pairs={{0,2},{1,3},{2,0},{3,1},{4,6},{5,7},{6,4},{7,5},{8,10},{9,11},{10,... | collective-permute-start | bytes 4616 | tf_op jit(solution)/shard_map/ppermute | solution.py:29

commit v5 on v4

--- a/solution.py
+++ b/solution.py
@@ -131,9 +131,8 @@
 
 def middle_kernel(score_scale, offsets, mask_ref, query_ref, *refs):
     state, key_refs, out = refs[:3], refs[3:-3], refs[-3:]
-    rows = query_ref.shape[0] // 2
-    bias = key_bias(mask_ref, offsets, rows)
-    flash(query_ref, key_refs, score_scale, bias, state, out, 0, rows, 2)
+    bias = key_bias(mask_ref, offsets, query_ref.shape[0] // 2)
+    flash(query_ref, key_refs, score_scale, bias, state, out, 0, out[0].shape[0] // 2, 2)
 
 
 def in_three(line):
@@ -149,14 +148,15 @@
     return jnp.sum(tile.astype(jnp.float32), axis=0, keepdims=True)
 
 
-def last_kernel(score_scale, late, mask_ref, query_ref, *refs):
-    state, key_refs, refs = refs[:3], refs[3:5], list(refs[5:])
+def last_kernel(score_scale, late, offsets, mask_ref, query_ref, *refs):
+    count = len(offsets)
+    state, key_refs, refs = refs[:3], refs[3 : 3 + count], list(refs[3 + count :])
     early_logs = [refs.pop(0), refs.pop(0)] if late else []
     near_ref, far_ref, near_log_ref, far_log_ref = refs[:4]
     out = refs[4:]
     rows = near_ref.shape[0] - (16 if late else 0)
     start = query_ref.shape[0] - 2 * rows if late else 0
-    bias = key_bias(mask_ref, (2, -2), key_refs[0].shape[0])
+    bias = key_bias(mask_ref, offsets, key_refs[0].shape[0])
     chunks = 1 if late else 2
     flash(query_ref, key_refs, score_scale, bias, state, out, start, 2 * rows // chunks, chunks)
     max_ref, total_ref, sum_ref = out
@@ -248,7 +248,7 @@
     own_sib = moved(own, sibling)
     first_1, second_1 = moved(own, onward), moved(own_sib, onward)
     first_2, second_2 = moved(first_1, onward), moved(second_1, onward)
-    first_1_sib, second_1_sib = moved(first_1, sibling), moved(second_1, sibling)
+    first_1_sib, second_1_sib = moved(after(first_1, near), sibling), moved(after(second_1, near), sibling)
     *state, queries = call(
         functools.partial(first_kernel, score_scale),
         held(2 * rows, width) + [jax.ShapeDtypeStruct((2 * rows, width), jnp.bfloat16)],
@@ -266,21 +266,25 @@
     )
     second_2, state = lax.optimization_barrier((second_2, state))
     second_2_sib = moved(second_2, sibling)
-    state = call(
+    ring_2 = [first_2, first_2_sib, second_2, second_2_sib]
+    early_state = call(
         functools.partial(middle_kernel, score_scale, (2, -2)),
-        held(2 * rows, width),
-        [block_mask, queries, *state, first_2, first_2_sib],
-        keys=2 * rows, query_rows=2 * rows, smem=True,
+        held(2 * early, width),
+        [block_mask, queries, *state, *ring_2[:2]],
+        keys=2 * rows, query_rows=2 * early, smem=True,
     )
     logs, sent = [], []
-    for size in (early, late):
+    for size, offsets, keys, source in (
+        (early, (2, -2), ring_2[2:], early_state),
+        (late, (2, -2, 2, -2), ring_2, state),
+    ):
         near_part, far_part, *logs = call(
-            functools.partial(last_kernel, score_scale, bool(sent)),
+            functools.partial(last_kernel, score_scale, bool(sent), offsets),
             [jax.ShapeDtypeStruct((size + (16 if sent else 0), width), jnp.bfloat16)] * 2
             + [jax.ShapeDtypeStruct((1, rows if sent else size), jnp.float32)] * 2,
-            [block_mask, queries, *state, second_2, second_2_sib, *logs],
+            [block_mask, queries, *source, *keys, *logs],
             scratch=[pltpu.VMEM(a.shape, a.dtype) for a in held(2 * rows, width)],
-            keys=2 * rows, query_rows=2 * size, smem=True,
+            keys=len(keys) * rows, query_rows=2 * size, smem=True,
         )
         sent.append((moved(near_part, across_near), moved(far_part, across_far)))
     near_log, far_log = logs

time: 76.1 us -> 75.2 us (0.988)
  transfers between devices with their start and end apart: 16 -> 16, of which waited for: 4 -> 5; matrix products, arithmetic and copies ran while one was open for 0% -> 0% of each run, Pallas kernels for 21% -> 20%
where the time goes in v5:
time: 75.2 us; the launch traced here: 75 us
  starting transfers between devices  33.2 us (44%)
  waiting for transfers between devices  20.5 us (27%)
  Pallas kernels  19.5 us (26%)
  local copies, waits for them, and re-layouts  1.14 us (2%)
    ppermute x16, starting transfers between devices, moved(): return lax.ppermute(value, AXES, pairs)  33.2 us
    ppermute x16, waiting for transfers between devices, moved(): return lax.ppermute(value, AXES, pairs)  20.5 us
    pallas_call x7, Pallas kernels, call(): pl.pallas_call(kernel, out_shape=out, in_specs=[SMEM if smem and index ==...  19.5 us
  transfers between devices with their start and end apart: 16, of which 5 were waited for; matrix products, arithmetic and copies ran while one was open for 0% of the time, Pallas kernels for 20%

profile of v5, /device:TPU:1, one launch (start us, length us, event | category | flops | bytes accessed | tf_op | source)
XLA Modules:
  0.0 75.0 jit_solution(7331869505907344545)
XLA Ops:
  0.6 3.3 %collective-permute-start.2 = (bf16[384,1024]{1,0:T(8,128)(2,1)}, bf16[384,1024]{1,0:T(8,128)(2,1)S(1)}, u32[]{:S(2)}, u32[]{:S(2)}) collective-permute-start(bf16[384,1024]{1,0:T(8,128)(2,1)} %bitcast.2), channel_id=1, source_target_pairs={{0,1},{1,0},{2,3},{3,2},{4,5},{5,4},{6,7},{7,6},{8,9},{9,8},{10,11... | collective-permute-start | bytes 2359304 | tf_op jit(solution)/shard_map/ppermute | solution.py:29
  4.0 6.0 %collective-permute-start.5 = (bf16[384,1024]{1,0:T(8,128)(2,1)}, bf16[384,1024]{1,0:T(8,128)(2,1)S(1)}, u32[]{:S(2)}, u32[]{:S(2)}) collective-permute-start(bf16[384,1024]{1,0:T(8,128)(2,1)} %bitcast.3), channel_id=1, source_target_pairs={{0,4},{1,125},{2,6},{3,127},{4,8},{5,1},{6,10},{7,3},{8,12},{9,5},... | collective-permute-start | bytes 2359304 | tf_op jit(solution)/shard_map/ppermute | solution.py:29
  10.0 1.3 %collective-permute-start = (bf16[384,1024]{1,0:T(8,128)(2,1)}, bf16[384,1024]{1,0:T(8,128)(2,1)S(1)}, u32[]{:S(2)}, u32[]{:S(2)}) collective-permute-start(bf16[384,1024]{1,0:T(8,128)(2,1)} %bitcast.4), channel_id=1, source_target_pairs={{0,128},{1,129},{2,130},{3,131},{4,132},{5,133},{6,134},{7,135},{8... | collective-permute-start | bytes 2359304 | tf_op jit(solution)/shard_map/ppermute | solution.py:29
  11.3 0.0 collective-permute-done.2.sibling_ref
  11.3 0.8 %collective-permute-start.3 = (bf16[384,1024]{1,0:T(8,128)(2,1)S(1)}, bf16[384,1024]{1,0:T(8,128)(2,1)S(1)}, u32[]{:S(2)}, u32[]{:S(2)}) collective-permute-start(bf16[384,1024]{1,0:T(8,128)(2,1)S(1)} %collective-permute-done.2.sibling_ref), channel_id=1, source_target_pairs={{0,4},{1,125},{2,6},{3,127},{4,8},{5,1},{6,10},{7,3},{8,12},{9,5},... | collective-permute-start | bytes 2359304 | tf_op jit(solution)/shard_map/ppermute | solution.py:29
  12.1 2.7 %collective-permute-start.1 = (bf16[384,1024]{1,0:T(8,128)(2,1)}, bf16[384,1024]{1,0:T(8,128)(2,1)S(1)}, u32[]{:S(2)}, u32[]{:S(2)}) collective-permute-start(bf16[384,1024]{1,0:T(8,128)(2,1)} %bitcast.5), channel_id=1, source_target_pairs={{0,130},{1,131},{2,128},{3,129},{4,134},{5,135},{6,132},{7,133},{8... | collective-permute-start | bytes 2359304 | tf_op jit(solution)/shard_map/ppermute | solution.py:29
  14.8 4.4 %collective-permute-done.5.refs_3_ = bf16[384,1024]{1,0:T(8,128)(2,1)S(1)} collective-permute-done((bf16[384,1024]{1,0:T(8,128)(2,1)}, bf16[384,1024]{1,0:T(8,128)(2,1)S(1)}, u32[]{:S(2)}, u32[]{:S(2)}) %collective-permute-start.5) | collective-permute-done | bytes 786464 | tf_op jit(solution)/shard_map/ppermute | solution.py:29
  19.2 5.1 %collective-permute-start.6 = (bf16[384,1024]{1,0:T(8,128)(2,1)S(1)}, bf16[384,1024]{1,0:T(8,128)(2,1)S(1)}, u32[]{:S(2)}, u32[]{:S(2)}) collective-permute-start(bf16[384,1024]{1,0:T(8,128)(2,1)S(1)} %collective-permute-done.5.refs_3_), channel_id=1, source_target_pairs={{0,4},{1,125},{2,6},{3,127},{4,8},{5,1},{6,10},{7,3},{8,12},{9,5},... | collective-permute-start | bytes 2359304 | tf_op jit(solution)/shard_map/ppermute | solution.py:29
  24.4 0.1 collective-permute-done.near_ref
  24.5 0.0 collective-permute-start.7
  24.5 3.1 %collective-permute-done.3.refs_4_ = bf16[384,1024]{1,0:T(8,128)(2,1)S(1)} collective-permute-done((bf16[384,1024]{1,0:T(8,128)(2,1)S(1)}, bf16[384,1024]{1,0:T(8,128)(2,1)S(1)}, u32[]{:S(2)}, u32[]{:S(2)}) %collective-permute-start.3) | collective-permute-done | bytes 786464 | tf_op jit(solution)/shard_map/ppermute | solution.py:29
  27.6 1.4 %collective-permute-start.8 = (bf16[384,1024]{1,0:T(8,128)(2,1)S(1)}, bf16[384,1024]{1,0:T(8,128)(2,1)S(1)}, u32[]{:S(2)}, u32[]{:S(2)}) collective-permute-start(bf16[384,1024]{1,0:T(8,128)(2,1)S(1)} %collective-permute-done.3.refs_4_), channel_id=1, source_target_pairs={{0,1},{1,0},{2,3},{3,2},{4,5},{5,4},{6,7},{7,6},{8,9},{9,8},{10,11... | collective-permute-start | bytes 2359304 | tf_op jit(solution)/shard_map/ppermute | solution.py:29
  29.0 3.8 %collective-permute-start.4 = (bf16[384,1024]{1,0:T(8,128)(2,1)S(1)}, bf16[384,1024]{1,0:T(8,128)(2,1)S(1)}, u32[]{:S(2)}, u32[]{:S(2)}) collective-permute-start(bf16[384,1024]{1,0:T(8,128)(2,1)S(1)} %collective-permute-done.3.refs_4_), channel_id=1, source_target_pairs={{0,4},{1,125},{2,6},{3,127},{4,8},{5,1},{6,10},{7,3},{8,12},{9,5},... | collective-permute-start | bytes 2359304 | tf_op jit(solution)/shard_map/ppermute | solution.py:29
  32.8 0.0 collective-permute-done.1.far_ref
  32.8 0.0 copy-start
  32.8 1.1 %copy-done = bf16[1,384,1024]{2,1,0:T(8,128)(2,1)S(1)} copy-done((bf16[1,384,1024]{2,1,0:T(8,128)(2,1)S(1)}, bf16[1,384,1024]{2,1,0:T(8,128)(2,1)}, u32[]{:S(2)}) %copy-start) | copy-done | bytes 786456
  33.9 0.0 copy-start.2
  33.9 2.8 %shard_map.41 = (f32[768,1]{1,0:T(8,128)S(1)}, f32[768,1]{1,0:T(8,128)S(1)}, f32[768,1024]{1,0:T(8,128)S(1)}, bf16[768,1024]{1,0:T(8,128)(2,1)S(1)}) custom-call(bf16[384,1024]{1,0:T(8,128)(2,1)S(1)} %collective-permute-done.near_ref, bf16[384,1024]{1,0:T(8,128)(2,1)S(1)} %collective-permute-done.1.far_ref, bf16[384,1024]{1,0:T(8,128)(2,1)S(1)} %bitcast.6, ...), custom_call_target="tpu_custom_call" | custom-call | tf_op jit(solution)/shard_map/pallas_call | solution.py:182
  36.8 0.0 collective-permute-done.6.refs_3_
  36.8 0.6 collective-permute-start.9
  37.4 0.0 collective-permute-done.7.refs_5_
  37.4 0.0 collective-permute-done.8.refs_6_
  37.4 0.0 copy-done.2
  37.4 6.2 %shard_map.42 = (f32[768,1]{1,0:T(8,128)S(1)}, f32[768,1]{1,0:T(8,128)S(1)}, f32[768,1024]{1,0:T(8,128)S(1)}) custom-call(s32[32,32]{1,0:T(8,128)S(1)} %copy-done.2, bf16[768,1024]{1,0:T(8,128)(2,1)S(1)} %get-tuple-element.33.query_ref, f32[768,1]{1,0:T(8,128)S(1)} %get-tuple-element.37.refs_0_, f32[768,1]{1,0:T(8,128)S(1)} %get-tuple-element.38.refs_1_, ...), custom_call_target="tpu_custom_call" | custom-call | tf_op jit(solution)/shard_map/pallas_call | solution.py:182
  43.7 0.8 %collective-permute-done.4.refs_3_.refs_5_ = bf16[384,1024]{1,0:T(8,128)(2,1)S(1)} collective-permute-done((bf16[384,1024]{1,0:T(8,128)(2,1)S(1)}, bf16[384,1024]{1,0:T(8,128)(2,1)S(1)}, u32[]{:S(2)}, u32[]{:S(2)}) %collective-permute-start.4) | collective-permute-done | bytes 786464 | tf_op jit(solution)/shard_map/ppermute | solution.py:29
  44.4 1.4 %collective-permute-start.10 = (bf16[384,1024]{1,0:T(8,128)(2,1)S(1)}, bf16[384,1024]{1,0:T(8,128)(2,1)S(1)}, u32[]{:S(2)}, u32[]{:S(2)}) collective-permute-start(bf16[384,1024]{1,0:T(8,128)(2,1)S(1)} %collective-permute-done.4.refs_3_.refs_5_), channel_id=1, source_target_pairs={{0,1},{1,0},{2,3},{3,2},{4,5},{5,4},{6,7},{7,6},{8,9},{9,8},{10,11... | collective-permute-start | bytes 2359304 | tf_op jit(solution)/shard_map/ppermute | solution.py:29
  45.8 0.0 collective-permute-done.9.refs_4_
  45.8 2.8 %shard_map.43 = (f32[512,1]{1,0:T(8,128)S(1)}, f32[512,1]{1,0:T(8,128)S(1)}, f32[512,1024]{1,0:T(8,128)S(1)}) custom-call(s32[32,32]{1,0:T(8,128)S(1)} %copy-done.2, bf16[768,1024]{1,0:T(8,128)(2,1)S(1)} %get-tuple-element.33.query_ref, f32[768,1]{1,0:T(8,128)S(1)} %get-tuple-element.45.refs_0_, f32[768,1]{1,0:T(8,128)S(1)} %get-tuple-element.46.refs_1_, ...), custom_call_target="tpu_custom_call" | custom-call | flops 1610612736 | bytes 6815744 | tf_op jit(solution)/shard_map/pallas_call | solution.py:182
  48.6 0.0 collective-permute-done.10.refs_4_.refs_6_
  48.6 2.8 %shard_map.44 = (bf16[256,1024]{1,0:T(8,128)(2,1)S(1)}, bf16[256,1024]{1,0:T(8,128)(2,1)S(1)}, f32[1,256]{1,0:T(1,128)S(1)}, f32[1,256]{1,0:T(1,128)S(1)}) custom-call(s32[32,32]{1,0:T(8,128)S(1)} %copy-done.2, bf16[768,1024]{1,0:T(8,128)(2,1)S(1)} %get-tuple-element.33.query_ref, f32[512,1]{1,0:T(8,128)S(1)} %get-tuple-element.50.refs_0_, ...), custom_call_target="tpu_custom_call" | custom-call | flops 1610612736 | bytes 6815744 | tf_op jit(solution)/shard_map/pallas_call | solution.py:182
  51.4 1.4 %collective-permute-start.12 = (bf16[256,1024]{1,0:T(8,128)(2,1)S(1)}, bf16[256,1024]{1,0:T(8,128)(2,1)S(1)}, u32[]{:S(2)}, u32[]{:S(2)}) collective-permute-start(bf16[256,1024]{1,0:T(8,128)(2,1)S(1)} %get-tuple-element.58), channel_id=1, source_target_pairs={{0,128},{1,129},{2,130},{3,131},{4,132},{5,133},{6,134},{7,135},{8... | collective-permute-start | bytes 1572872 | tf_op jit(solution)/shard_map/ppermute | solution.py:29
  52.8 1.9 %collective-permute-start.14 = (bf16[256,1024]{1,0:T(8,128)(2,1)S(1)}, bf16[256,1024]{1,0:T(8,128)(2,1)S(1)}, u32[]{:S(2)}, u32[]{:S(2)}) collective-permute-start(bf16[256,1024]{1,0:T(8,128)(2,1)S(1)} %get-tuple-element.60), channel_id=1, source_target_pairs={{0,130},{1,131},{2,128},{3,129},{4,134},{5,135},{6,132},{7,133},{8... | collective-permute-start | bytes 1572872 | tf_op jit(solution)/shard_map/ppermute | solution.py:29
  54.7 0.0 copy-start.1
  54.7 3.1 %shard_map.45 = (bf16[144,1024]{1,0:T(8,128)(2,1)S(1)}, bf16[144,1024]{1,0:T(8,128)(2,1)S(1)}, f32[1,384]{1,0:T(1,128)S(1)}, f32[1,384]{1,0:T(1,128)S(1)}) custom-call(s32[32,32]{1,0:T(8,128)S(1)} %copy-done.2, bf16[768,1024]{1,0:T(8,128)(2,1)S(1)} %get-tuple-element.33.query_ref, f32[768,1]{1,0:T(8,128)S(1)} %get-tuple-element.45.refs_0_, ...), custom_call_target="tpu_custom_call" | custom-call | flops 1610612736 | bytes 5767168 | tf_op jit(solution)/shard_map/pallas_call | solution.py:182
  57.8 0.5 collective-permute-start.13
  58.3 0.6 collective-permute-start.15
  58.9 2.2 %collective-permute-start.11 = (f32[1,384]{1,0:T(1,128)S(1)}, f32[1,384]{1,0:T(1,128)S(1)}, u32[]{:S(2)}, u32[]{:S(2)}) collective-permute-start(f32[1,384]{1,0:T(1,128)S(1)} %get-tuple-element.56), channel_id=1, source_target_pairs={{0,2},{1,3},{2,0},{3,1},{4,6},{5,7},{6,4},{7,5},{8,10},{9,11},{10,... | collective-permute-start | bytes 4616 | tf_op jit(solution)/shard_map/ppermute | solution.py:29
  61.1 0.0 copy-done.1
  61.1 0.3 shard_map.46.pair_ref
  61.4 12.1 %collective-permute-done.11.half_log_ref = f32[1,384]{1,0:T(1,128)S(1)} collective-permute-done((f32[1,384]{1,0:T(1,128)S(1)}, f32[1,384]{1,0:T(1,128)S(1)}, u32[]{:S(2)}, u32[]{:S(2)}) %collective-permute-start.11) | collective-permute-done | bytes 1568 | tf_op jit(solution)/shard_map/ppermute | solution.py:29
  73.6 0.0 collective-permute-done.13.near_late_ref
  73.6 0.0 collective-permute-done.15.far_late_ref
  73.6 0.0 collective-permute-done.12.near_early_ref
  73.6 0.0 collective-permute-done.14.far_early_ref
  73.6 1.4 %shard_map.47 = (bf16[384,1024]{1,0:T(8,128)(2,1)}, f32[1,384]{1,0:T(1,128)}) custom-call(f32[1,384]{1,0:T(1,128)S(1)} %get-tuple-element.55.here_log_ref, f32[1,384]{1,0:T(1,128)S(1)} %collective-permute-done.11.half_log_ref, f32[1,384]{1,0:T(1,128)S(1)} %shard_map.46.pair_ref, bf16[256,1024]{1,0:T(8,128)(2,1)S(1)} %collective-permute-done.12.near_early_ref, ...), custom_call_target="tpu_custom_call" | custom-call | tf_op jit(solution)/shard_map/pallas_call | solution.py:182
Async XLA Ops:
  0.6 10.7 %collective-permute-start.2 = (bf16[384,1024]{1,0:T(8,128)(2,1)}, bf16[384,1024]{1,0:T(8,128)(2,1)S(1)}, u32[]{:S(2)}, u32[]{:S(2)}) collective-permute-start(bf16[384,1024]{1,0:T(8,128)(2,1)} %bitcast.2), channel_id=1, source_target_pairs={{0,1},{1,0},{2,3},{3,2},{4,5},{5,4},{6,7},{7,6},{8,9},{9,8},{10,11... | collective-permute-start | bytes 2359304 | tf_op jit(solution)/shard_map/ppermute | solution.py:29
  4.0 15.3 %collective-permute-start.5 = (bf16[384,1024]{1,0:T(8,128)(2,1)}, bf16[384,1024]{1,0:T(8,128)(2,1)S(1)}, u32[]{:S(2)}, u32[]{:S(2)}) collective-permute-start(bf16[384,1024]{1,0:T(8,128)(2,1)} %bitcast.3), channel_id=1, source_target_pairs={{0,4},{1,125},{2,6},{3,127},{4,8},{5,1},{6,10},{7,3},{8,12},{9,5},... | collective-permute-start | bytes 2359304 | tf_op jit(solution)/shard_map/ppermute | solution.py:29
  10.0 14.5 %collective-permute-start = (bf16[384,1024]{1,0:T(8,128)(2,1)}, bf16[384,1024]{1,0:T(8,128)(2,1)S(1)}, u32[]{:S(2)}, u32[]{:S(2)}) collective-permute-start(bf16[384,1024]{1,0:T(8,128)(2,1)} %bitcast.4), channel_id=1, source_target_pairs={{0,128},{1,129},{2,130},{3,131},{4,132},{5,133},{6,134},{7,135},{8... | collective-permute-start | bytes 2359304 | tf_op jit(solution)/shard_map/ppermute | solution.py:29
  11.3 16.3 %collective-permute-start.3 = (bf16[384,1024]{1,0:T(8,128)(2,1)S(1)}, bf16[384,1024]{1,0:T(8,128)(2,1)S(1)}, u32[]{:S(2)}, u32[]{:S(2)}) collective-permute-start(bf16[384,1024]{1,0:T(8,128)(2,1)S(1)} %collective-permute-done.2.sibling_ref), channel_id=1, source_target_pairs={{0,4},{1,125},{2,6},{3,127},{4,8},{5,1},{6,10},{7,3},{8,12},{9,5},... | collective-permute-start | bytes 2359304 | tf_op jit(solution)/shard_map/ppermute | solution.py:29
  12.1 20.7 %collective-permute-start.1 = (bf16[384,1024]{1,0:T(8,128)(2,1)}, bf16[384,1024]{1,0:T(8,128)(2,1)S(1)}, u32[]{:S(2)}, u32[]{:S(2)}) collective-permute-start(bf16[384,1024]{1,0:T(8,128)(2,1)} %bitcast.5), channel_id=1, source_target_pairs={{0,130},{1,131},{2,128},{3,129},{4,134},{5,135},{6,132},{7,133},{8... | collective-permute-start | bytes 2359304 | tf_op jit(solution)/shard_map/ppermute | solution.py:29
  19.2 17.5 %collective-permute-start.6 = (bf16[384,1024]{1,0:T(8,128)(2,1)S(1)}, bf16[384,1024]{1,0:T(8,128)(2,1)S(1)}, u32[]{:S(2)}, u32[]{:S(2)}) collective-permute-start(bf16[384,1024]{1,0:T(8,128)(2,1)S(1)} %collective-permute-done.5.refs_3_), channel_id=1, source_target_pairs={{0,4},{1,125},{2,6},{3,127},{4,8},{5,1},{6,10},{7,3},{8,12},{9,5},... | collective-permute-start | bytes 2359304 | tf_op jit(solution)/shard_map/ppermute | solution.py:29
  24.5 12.9 %collective-permute-start.7 = (bf16[384,1024]{1,0:T(8,128)(2,1)S(1)}, bf16[384,1024]{1,0:T(8,128)(2,1)S(1)}, u32[]{:S(2)}, u32[]{:S(2)}) collective-permute-start(bf16[384,1024]{1,0:T(8,128)(2,1)S(1)} %collective-permute-done.5.refs_3_), channel_id=1, source_target_pairs={{0,1},{1,0},{2,3},{3,2},{4,5},{5,4},{6,7},{7,6},{8,9},{9,8},{10,11... | collective-permute-start | bytes 2359304 | tf_op jit(solution)/shard_map/ppermute | solution.py:29
  27.6 9.8 %collective-permute-start.8 = (bf16[384,1024]{1,0:T(8,128)(2,1)S(1)}, bf16[384,1024]{1,0:T(8,128)(2,1)S(1)}, u32[]{:S(2)}, u32[]{:S(2)}) collective-permute-start(bf16[384,1024]{1,0:T(8,128)(2,1)S(1)} %collective-permute-done.3.refs_4_), channel_id=1, source_target_pairs={{0,1},{1,0},{2,3},{3,2},{4,5},{5,4},{6,7},{7,6},{8,9},{9,8},{10,11... | collective-permute-start | bytes 2359304 | tf_op jit(solution)/shard_map/ppermute | solution.py:29
  29.0 15.4 %collective-permute-start.4 = (bf16[384,1024]{1,0:T(8,128)(2,1)S(1)}, bf16[384,1024]{1,0:T(8,128)(2,1)S(1)}, u32[]{:S(2)}, u32[]{:S(2)}) collective-permute-start(bf16[384,1024]{1,0:T(8,128)(2,1)S(1)} %collective-permute-done.3.refs_4_), channel_id=1, source_target_pairs={{0,4},{1,125},{2,6},{3,127},{4,8},{5,1},{6,10},{7,3},{8,12},{9,5},... | collective-permute-start | bytes 2359304 | tf_op jit(solution)/shard_map/ppermute | solution.py:29
  32.8 1.1 %copy-start = (bf16[1,384,1024]{2,1,0:T(8,128)(2,1)S(1)}, bf16[1,384,1024]{2,1,0:T(8,128)(2,1)}, u32[]{:S(2)}) copy-start(bf16[1,384,1024]{2,1,0:T(8,128)(2,1)} %param.2) | copy-start | bytes 2359300
  33.9 3.5 %copy-start.2 = (s32[32,32]{1,0:T(8,128)S(1)}, s32[32,32]{1,0:T(8,128)}, u32[]{:S(2)}) copy-start(s32[32,32]{1,0:T(8,128)} %mask_ref.7) | copy-start | bytes 12292
  36.8 9.0 %collective-permute-start.9 = (bf16[384,1024]{1,0:T(8,128)(2,1)S(1)}, bf16[384,1024]{1,0:T(8,128)(2,1)S(1)}, u32[]{:S(2)}, u32[]{:S(2)}) collective-permute-start(bf16[384,1024]{1,0:T(8,128)(2,1)S(1)} %collective-permute-done.6.refs_3_), channel_id=1, source_target_pairs={{0,1},{1,0},{2,3},{3,2},{4,5},{5,4},{6,7},{7,6},{8,9},{9,8},{10,11... | collective-permute-start | bytes 2359304 | tf_op jit(solution)/shard_map/ppermute | solution.py:29
  44.4 4.2 %collective-permute-start.10 = (bf16[384,1024]{1,0:T(8,128)(2,1)S(1)}, bf16[384,1024]{1,0:T(8,128)(2,1)S(1)}, u32[]{:S(2)}, u32[]{:S(2)}) collective-permute-start(bf16[384,1024]{1,0:T(8,128)(2,1)S(1)} %collective-permute-done.4.refs_3_.refs_5_), channel_id=1, source_target_pairs={{0,1},{1,0},{2,3},{3,2},{4,5},{5,4},{6,7},{7,6},{8,9},{9,8},{10,11... | collective-permute-start | bytes 2359304 | tf_op jit(solution)/shard_map/ppermute | solution.py:29
  51.4 22.2 %collective-permute-start.12 = (bf16[256,1024]{1,0:T(8,128)(2,1)S(1)}, bf16[256,1024]{1,0:T(8,128)(2,1)S(1)}, u32[]{:S(2)}, u32[]{:S(2)}) collective-permute-start(bf16[256,1024]{1,0:T(8,128)(2,1)S(1)} %get-tuple-element.58), channel_id=1, source_target_pairs={{0,128},{1,129},{2,130},{3,131},{4,132},{5,133},{6,134},{7,135},{8... | collective-permute-start | bytes 1572872 | tf_op jit(solution)/shard_map/ppermute | solution.py:29
  52.8 20.8 %collective-permute-start.14 = (bf16[256,1024]{1,0:T(8,128)(2,1)S(1)}, bf16[256,1024]{1,0:T(8,128)(2,1)S(1)}, u32[]{:S(2)}, u32[]{:S(2)}) collective-permute-start(bf16[256,1024]{1,0:T(8,128)(2,1)S(1)} %get-tuple-element.60), channel_id=1, source_target_pairs={{0,130},{1,131},{2,128},{3,129},{4,134},{5,135},{6,132},{7,133},{8... | collective-permute-start | bytes 1572872 | tf_op jit(solution)/shard_map/ppermute | solution.py:29
  54.7 6.4 %copy-start.1 = (bf16[1,384,1024]{2,1,0:T(8,128)(2,1)S(1)}, bf16[1,384,1024]{2,1,0:T(8,128)(2,1)}, u32[]{:S(2)}) copy-start(bf16[1,384,1024]{2,1,0:T(8,128)(2,1)} %param.2) | copy-start | bytes 2359300
  57.8 15.8 %collective-permute-start.13 = (bf16[144,1024]{1,0:T(8,128)(2,1)S(1)}, bf16[144,1024]{1,0:T(8,128)(2,1)S(1)}, u32[]{:S(2)}, u32[]{:S(2)}) collective-permute-start(bf16[144,1024]{1,0:T(8,128)(2,1)S(1)} %get-tuple-element.59), channel_id=1, source_target_pairs={{0,128},{1,129},{2,130},{3,131},{4,132},{5,133},{6,134},{7,135},{8... | collective-permute-start | bytes 884744 | tf_op jit(solution)/shard_map/ppermute | solution.py:29
  58.3 15.3 %collective-permute-start.15 = (bf16[144,1024]{1,0:T(8,128)(2,1)S(1)}, bf16[144,1024]{1,0:T(8,128)(2,1)S(1)}, u32[]{:S(2)}, u32[]{:S(2)}) collective-permute-start(bf16[144,1024]{1,0:T(8,128)(2,1)S(1)} %get-tuple-element.61), channel_id=1, source_target_pairs={{0,130},{1,131},{2,128},{3,129},{4,134},{5,135},{6,132},{7,133},{8... | collective-permute-start | bytes 884744 | tf_op jit(solution)/shard_map/ppermute | solution.py:29
  58.9 14.7 %collective-permute-start.11 = (f32[1,384]{1,0:T(1,128)S(1)}, f32[1,384]{1,0:T(1,128)S(1)}, u32[]{:S(2)}, u32[]{:S(2)}) collective-permute-start(f32[1,384]{1,0:T(1,128)S(1)} %get-tuple-element.56), channel_id=1, source_target_pairs={{0,2},{1,3},{2,0},{3,1},{4,6},{5,7},{6,4},{7,5},{8,10},{9,11},{10,... | collective-permute-start | bytes 4616 | tf_op jit(solution)/shard_map/ppermute | solution.py:29

commit v6 on v5

--- a/solution.py
+++ b/solution.py
@@ -135,24 +135,31 @@
     flash(query_ref, key_refs, score_scale, bias, state, out, 0, out[0].shape[0] // 2, 2)
 
 
-def in_three(line):
-    high = line.astype(jnp.bfloat16).astype(jnp.float32)
-    middle = (line - high).astype(jnp.bfloat16).astype(jnp.float32)
-    low = line - high - middle
-    row = lax.broadcasted_iota(jnp.int32, (16, line.shape[1]), 0)
-    tile = jnp.where(row == 0, high, jnp.where(row == 1, middle, jnp.where(row == 2, low, 0.0)))
+def in_threes(lines):
+    row = lax.broadcasted_iota(jnp.int32, (16, lines.shape[1]), 0)
+    tile = jnp.zeros(row.shape, jnp.float32)
+    for index in range(lines.shape[0]):
+        line = lines[index : index + 1, :]
+        high = line.astype(jnp.bfloat16).astype(jnp.float32)
+        middle = (line - high).astype(jnp.bfloat16).astype(jnp.float32)
+        for place, piece in enumerate((high, middle, line - high - middle)):
+            tile = jnp.where(row == 3 * index + place, piece, tile)
     return tile.astype(jnp.bfloat16)
 
 
-def of_three(tile):
-    return jnp.sum(tile.astype(jnp.float32), axis=0, keepdims=True)
+def of_threes(tile, index):
+    high, middle, low = (
+        tile[3 * index + place : 3 * index + place + 1, :].astype(jnp.float32)
+        for place in range(3)
+    )
+    return low + middle + high
 
 
 def last_kernel(score_scale, late, offsets, mask_ref, query_ref, *refs):
     count = len(offsets)
     state, key_refs, refs = refs[:3], refs[3 : 3 + count], list(refs[3 + count :])
-    early_logs = [refs.pop(0), refs.pop(0)] if late else []
-    near_ref, far_ref, near_log_ref, far_log_ref = refs[:4]
+    early_stats = [refs.pop(0), refs.pop(0)] if late else []
+    near_ref, far_ref, near_stat_ref, far_stat_ref = refs[:4]
     out = refs[4:]
     rows = near_ref.shape[0] - (16 if late else 0)
     start = query_ref.shape[0] - 2 * rows if late else 0
@@ -160,21 +167,19 @@
     chunks = 1 if late else 2
     flash(query_ref, key_refs, score_scale, bias, state, out, start, 2 * rows // chunks, chunks)
     max_ref, total_ref, sum_ref = out
-    for index, (part_ref, log_ref) in enumerate(
-        ((near_ref, near_log_ref), (far_ref, far_log_ref))
+    for index, (part_ref, stat_ref) in enumerate(
+        ((near_ref, near_stat_ref), (far_ref, far_stat_ref))
     ):
         these = pl.ds(start + index * rows, rows)
         total = total_ref[these, :]
         part_ref[:rows, :] = (sum_ref[these, :] / total).astype(jnp.bfloat16)
-        log = (max_ref[these, :] * score_scale + jnp.log(total)).T
+        early = early_stats[index].shape[1] if late else 0
+        stat_ref[0:1, early:] = max_ref[these, :].T
+        stat_ref[1:2, early:] = total.T
         if late:
-            early = early_logs[index].shape[1]
-            log_ref[:, :early] = early_logs[index][...]
-            log_ref[:, early:] = log
+            stat_ref[:, :early] = early_stats[index][...]
             part_ref[rows:, :] = jnp.zeros((16, part_ref.shape[1]), jnp.bfloat16)
-            part_ref[rows:, : early + rows] = in_three(log_ref[...])
-        else:
-            log_ref[...] = log
+            part_ref[rows:, : early + rows] = in_threes(stat_ref[...])
 
 
 def call(kernel, out, operands, scratch=(), keys=0, query_rows=0, smem=False, left=()):
@@ -206,22 +211,30 @@
 
 
 def finish_kernel(
-    here_log_ref, half_log_ref, pair_ref,
+    score_scale, here_stat_ref, half_stat_ref, pair_ref,
     near_early_ref, near_late_ref, far_early_ref, far_late_ref, blended_ref, margin_ref,
 ):
-    def merged(one, two):
-        top = jnp.maximum(one, two)
-        return top + jnp.log(jnp.exp(one - top) + jnp.exp(two - top))
-
     rows, early = blended_ref.shape[0], near_early_ref.shape[0]
     late = rows - early
-    near_log = of_three(near_late_ref[late:, :rows])
-    far_log = of_three(far_late_ref[late:, :rows])
-    own_log = merged(near_log, far_log)
-    margin_ref[...] = pair_ref[...] - 0.5 * (
-        own_log + merged(here_log_ref[...], half_log_ref[...])
-    )
-    near_share, far_share = jnp.exp(near_log - own_log).T, jnp.exp(far_log - own_log).T
+
+    def merged(one, two):
+        top = jnp.maximum(one[0], two[0])
+        left = one[1] * jnp.exp2((one[0] - top) * (score_scale * LOG2_E))
+        right = two[1] * jnp.exp2((two[0] - top) * (score_scale * LOG2_E))
+        total = left + right
+        return left / total, right / total, top * score_scale + jnp.log(total)
+
+    near_tile, far_tile = near_late_ref[late:, :rows], far_late_ref[late:, :rows]
+    near_share, far_share, own_log = merged(
+        [of_threes(near_tile, index) for index in range(2)],
+        [of_threes(far_tile, index) for index in range(2)],
+    )
+    there_log = merged(
+        [here_stat_ref[index : index + 1, :] for index in range(2)],
+        [half_stat_ref[index : index + 1, :] for index in range(2)],
+    )[2]
+    margin_ref[...] = pair_ref[...] - 0.5 * (own_log + there_log)
+    near_share, far_share = near_share.T, far_share.T
     for here, count, near_ref, far_ref in (
         (slice(0, early), early, near_early_ref, far_early_ref),
         (slice(early, rows), late, near_late_ref, far_late_ref),
@@ -273,30 +286,30 @@
         [block_mask, queries, *state, *ring_2[:2]],
         keys=2 * rows, query_rows=2 * early, smem=True,
     )
-    logs, sent = [], []
+    stats, sent = [], []
     for size, offsets, keys, source in (
         (early, (2, -2), ring_2[2:], early_state),
         (late, (2, -2, 2, -2), ring_2, state),
     ):
-        near_part, far_part, *logs = call(
+        near_part, far_part, *stats = call(
             functools.partial(last_kernel, score_scale, bool(sent), offsets),
             [jax.ShapeDtypeStruct((size + (16 if sent else 0), width), jnp.bfloat16)] * 2
-            + [jax.ShapeDtypeStruct((1, rows if sent else size), jnp.float32)] * 2,
-            [block_mask, queries, *source, *keys, *logs],
+            + [jax.ShapeDtypeStruct((2, rows if sent else size), jnp.float32)] * 2,
+            [block_mask, queries, *source, *keys, *stats],
             scratch=[pltpu.VMEM(a.shape, a.dtype) for a in held(2 * rows, width)],
             keys=len(keys) * rows, query_rows=2 * size, smem=True,
         )
         sent.append((moved(near_part, across_near), moved(far_part, across_far)))
-    near_log, far_log = logs
+    near_stat, far_stat = stats
     pair_score = call(
-        functools.partial(pair_kernel, score_scale), [line], [after(near, near_log), own]
+        functools.partial(pair_kernel, score_scale), [line], [after(near, near_stat), own]
     )[0]
     blended, margin = call(
-        finish_kernel,
+        functools.partial(finish_kernel, score_scale),
         [jax.ShapeDtypeStruct((rows, width), jnp.bfloat16), line],
         [
-            near_log,
-            moved(far_log, other_half),
+            near_stat,
+            moved(far_stat, other_half),
             pair_score,
             sent[0][0], sent[1][0], sent[0][1], sent[1][1],
         ],

time: 75.2 us -> 75.3 us (level)
  no operation moved by 1% of the time
where the time goes in v6:
time: 75.3 us; the launch traced here: 75.1 us
  starting transfers between devices  33.2 us (44%)
  waiting for transfers between devices  20.6 us (27%)
  Pallas kernels  19.5 us (26%)
  local copies, waits for them, and re-layouts  1.14 us (2%)
    ppermute x16, starting transfers between devices, moved(): return lax.ppermute(value, AXES, pairs)  33.2 us
    ppermute x16, waiting for transfers between devices, moved(): return lax.ppermute(value, AXES, pairs)  20.6 us
    pallas_call x7, Pallas kernels, call(): pl.pallas_call(kernel, out_shape=out, in_specs=[SMEM if smem and index ==...  19.5 us
  transfers between devices with their start and end apart: 16, of which 5 were waited for; matrix products, arithmetic and copies ran while one was open for 0% of the time, Pallas kernels for 20%

profile of v6, /device:TPU:1, one launch (start us, length us, event | category | flops | bytes accessed | tf_op | source)
XLA Modules:
  0.0 75.1 jit_solution(1703077860379362200)
XLA Ops:
  0.6 3.3 %collective-permute-start.2 = (bf16[384,1024]{1,0:T(8,128)(2,1)}, bf16[384,1024]{1,0:T(8,128)(2,1)S(1)}, u32[]{:S(2)}, u32[]{:S(2)}) collective-permute-start(bf16[384,1024]{1,0:T(8,128)(2,1)} %bitcast.2), channel_id=1, source_target_pairs={{0,1},{1,0},{2,3},{3,2},{4,5},{5,4},{6,7},{7,6},{8,9},{9,8},{10,11... | collective-permute-start | bytes 2359304 | tf_op jit(solution)/shard_map/ppermute | solution.py:29
  4.0 6.0 %collective-permute-start.5 = (bf16[384,1024]{1,0:T(8,128)(2,1)}, bf16[384,1024]{1,0:T(8,128)(2,1)S(1)}, u32[]{:S(2)}, u32[]{:S(2)}) collective-permute-start(bf16[384,1024]{1,0:T(8,128)(2,1)} %bitcast.3), channel_id=1, source_target_pairs={{0,4},{1,125},{2,6},{3,127},{4,8},{5,1},{6,10},{7,3},{8,12},{9,5},... | collective-permute-start | bytes 2359304 | tf_op jit(solution)/shard_map/ppermute | solution.py:29
  10.0 1.3 %collective-permute-start = (bf16[384,1024]{1,0:T(8,128)(2,1)}, bf16[384,1024]{1,0:T(8,128)(2,1)S(1)}, u32[]{:S(2)}, u32[]{:S(2)}) collective-permute-start(bf16[384,1024]{1,0:T(8,128)(2,1)} %bitcast.4), channel_id=1, source_target_pairs={{0,128},{1,129},{2,130},{3,131},{4,132},{5,133},{6,134},{7,135},{8... | collective-permute-start | bytes 2359304 | tf_op jit(solution)/shard_map/ppermute | solution.py:29
  11.3 0.0 collective-permute-done.2.sibling_ref
  11.3 0.8 %collective-permute-start.3 = (bf16[384,1024]{1,0:T(8,128)(2,1)S(1)}, bf16[384,1024]{1,0:T(8,128)(2,1)S(1)}, u32[]{:S(2)}, u32[]{:S(2)}) collective-permute-start(bf16[384,1024]{1,0:T(8,128)(2,1)S(1)} %collective-permute-done.2.sibling_ref), channel_id=1, source_target_pairs={{0,4},{1,125},{2,6},{3,127},{4,8},{5,1},{6,10},{7,3},{8,12},{9,5},... | collective-permute-start | bytes 2359304 | tf_op jit(solution)/shard_map/ppermute | solution.py:29
  12.1 2.7 %collective-permute-start.1 = (bf16[384,1024]{1,0:T(8,128)(2,1)}, bf16[384,1024]{1,0:T(8,128)(2,1)S(1)}, u32[]{:S(2)}, u32[]{:S(2)}) collective-permute-start(bf16[384,1024]{1,0:T(8,128)(2,1)} %bitcast.5), channel_id=1, source_target_pairs={{0,130},{1,131},{2,128},{3,129},{4,134},{5,135},{6,132},{7,133},{8... | collective-permute-start | bytes 2359304 | tf_op jit(solution)/shard_map/ppermute | solution.py:29
  14.8 4.4 %collective-permute-done.5.refs_3_ = bf16[384,1024]{1,0:T(8,128)(2,1)S(1)} collective-permute-done((bf16[384,1024]{1,0:T(8,128)(2,1)}, bf16[384,1024]{1,0:T(8,128)(2,1)S(1)}, u32[]{:S(2)}, u32[]{:S(2)}) %collective-permute-start.5) | collective-permute-done | bytes 786464 | tf_op jit(solution)/shard_map/ppermute | solution.py:29
  19.2 5.1 %collective-permute-start.6 = (bf16[384,1024]{1,0:T(8,128)(2,1)S(1)}, bf16[384,1024]{1,0:T(8,128)(2,1)S(1)}, u32[]{:S(2)}, u32[]{:S(2)}) collective-permute-start(bf16[384,1024]{1,0:T(8,128)(2,1)S(1)} %collective-permute-done.5.refs_3_), channel_id=1, source_target_pairs={{0,4},{1,125},{2,6},{3,127},{4,8},{5,1},{6,10},{7,3},{8,12},{9,5},... | collective-permute-start | bytes 2359304 | tf_op jit(solution)/shard_map/ppermute | solution.py:29
  24.4 0.1 collective-permute-done.near_ref
  24.5 0.0 collective-permute-start.7
  24.5 3.1 %collective-permute-done.3.refs_4_ = bf16[384,1024]{1,0:T(8,128)(2,1)S(1)} collective-permute-done((bf16[384,1024]{1,0:T(8,128)(2,1)S(1)}, bf16[384,1024]{1,0:T(8,128)(2,1)S(1)}, u32[]{:S(2)}, u32[]{:S(2)}) %collective-permute-start.3) | collective-permute-done | bytes 786464 | tf_op jit(solution)/shard_map/ppermute | solution.py:29
  27.6 1.4 %collective-permute-start.8 = (bf16[384,1024]{1,0:T(8,128)(2,1)S(1)}, bf16[384,1024]{1,0:T(8,128)(2,1)S(1)}, u32[]{:S(2)}, u32[]{:S(2)}) collective-permute-start(bf16[384,1024]{1,0:T(8,128)(2,1)S(1)} %collective-permute-done.3.refs_4_), channel_id=1, source_target_pairs={{0,1},{1,0},{2,3},{3,2},{4,5},{5,4},{6,7},{7,6},{8,9},{9,8},{10,11... | collective-permute-start | bytes 2359304 | tf_op jit(solution)/shard_map/ppermute | solution.py:29
  29.0 3.8 %collective-permute-start.4 = (bf16[384,1024]{1,0:T(8,128)(2,1)S(1)}, bf16[384,1024]{1,0:T(8,128)(2,1)S(1)}, u32[]{:S(2)}, u32[]{:S(2)}) collective-permute-start(bf16[384,1024]{1,0:T(8,128)(2,1)S(1)} %collective-permute-done.3.refs_4_), channel_id=1, source_target_pairs={{0,4},{1,125},{2,6},{3,127},{4,8},{5,1},{6,10},{7,3},{8,12},{9,5},... | collective-permute-start | bytes 2359304 | tf_op jit(solution)/shard_map/ppermute | solution.py:29
  32.8 0.0 collective-permute-done.1.far_ref
  32.8 0.0 copy-start
  32.8 1.1 %copy-done = bf16[1,384,1024]{2,1,0:T(8,128)(2,1)S(1)} copy-done((bf16[1,384,1024]{2,1,0:T(8,128)(2,1)S(1)}, bf16[1,384,1024]{2,1,0:T(8,128)(2,1)}, u32[]{:S(2)}) %copy-start) | copy-done | bytes 786456
  33.9 0.0 copy-start.2
  33.9 2.8 %shard_map.41 = (f32[768,1]{1,0:T(8,128)S(1)}, f32[768,1]{1,0:T(8,128)S(1)}, f32[768,1024]{1,0:T(8,128)S(1)}, bf16[768,1024]{1,0:T(8,128)(2,1)S(1)}) custom-call(bf16[384,1024]{1,0:T(8,128)(2,1)S(1)} %collective-permute-done.near_ref, bf16[384,1024]{1,0:T(8,128)(2,1)S(1)} %collective-permute-done.1.far_ref, bf16[384,1024]{1,0:T(8,128)(2,1)S(1)} %bitcast.6, ...), custom_call_target="tpu_custom_call" | custom-call | tf_op jit(solution)/shard_map/pallas_call | solution.py:187
  36.8 0.0 collective-permute-done.6.refs_3_
  36.8 0.6 collective-permute-start.9
  37.4 0.0 collective-permute-done.7.refs_5_
  37.4 0.0 collective-permute-done.8.refs_6_
  37.4 0.0 copy-done.2
  37.4 6.2 %shard_map.42 = (f32[768,1]{1,0:T(8,128)S(1)}, f32[768,1]{1,0:T(8,128)S(1)}, f32[768,1024]{1,0:T(8,128)S(1)}) custom-call(s32[32,32]{1,0:T(8,128)S(1)} %copy-done.2, bf16[768,1024]{1,0:T(8,128)(2,1)S(1)} %get-tuple-element.33.query_ref, f32[768,1]{1,0:T(8,128)S(1)} %get-tuple-element.37.refs_0_, f32[768,1]{1,0:T(8,128)S(1)} %get-tuple-element.38.refs_1_, ...), custom_call_target="tpu_custom_call" | custom-call | tf_op jit(solution)/shard_map/pallas_call | solution.py:187
  43.7 0.8 %collective-permute-done.4.refs_3_.refs_5_ = bf16[384,1024]{1,0:T(8,128)(2,1)S(1)} collective-permute-done((bf16[384,1024]{1,0:T(8,128)(2,1)S(1)}, bf16[384,1024]{1,0:T(8,128)(2,1)S(1)}, u32[]{:S(2)}, u32[]{:S(2)}) %collective-permute-start.4) | collective-permute-done | bytes 786464 | tf_op jit(solution)/shard_map/ppermute | solution.py:29
  44.4 1.4 %collective-permute-start.10 = (bf16[384,1024]{1,0:T(8,128)(2,1)S(1)}, bf16[384,1024]{1,0:T(8,128)(2,1)S(1)}, u32[]{:S(2)}, u32[]{:S(2)}) collective-permute-start(bf16[384,1024]{1,0:T(8,128)(2,1)S(1)} %collective-permute-done.4.refs_3_.refs_5_), channel_id=1, source_target_pairs={{0,1},{1,0},{2,3},{3,2},{4,5},{5,4},{6,7},{7,6},{8,9},{9,8},{10,11... | collective-permute-start | bytes 2359304 | tf_op jit(solution)/shard_map/ppermute | solution.py:29
  45.8 0.0 collective-permute-done.9.refs_4_
  45.8 2.8 %shard_map.43 = (f32[512,1]{1,0:T(8,128)S(1)}, f32[512,1]{1,0:T(8,128)S(1)}, f32[512,1024]{1,0:T(8,128)S(1)}) custom-call(s32[32,32]{1,0:T(8,128)S(1)} %copy-done.2, bf16[768,1024]{1,0:T(8,128)(2,1)S(1)} %get-tuple-element.33.query_ref, f32[768,1]{1,0:T(8,128)S(1)} %get-tuple-element.45.refs_0_, f32[768,1]{1,0:T(8,128)S(1)} %get-tuple-element.46.refs_1_, ...), custom_call_target="tpu_custom_call" | custom-call | flops 1610612736 | bytes 6815744 | tf_op jit(solution)/shard_map/pallas_call | solution.py:187
  48.6 0.0 collective-permute-done.10.refs_4_.refs_6_
  48.6 2.9 %shard_map.44 = (bf16[256,1024]{1,0:T(8,128)(2,1)S(1)}, bf16[256,1024]{1,0:T(8,128)(2,1)S(1)}, f32[2,256]{1,0:T(2,128)S(1)}, f32[2,256]{1,0:T(2,128)S(1)}) custom-call(s32[32,32]{1,0:T(8,128)S(1)} %copy-done.2, bf16[768,1024]{1,0:T(8,128)(2,1)S(1)} %get-tuple-element.33.query_ref, f32[512,1]{1,0:T(8,128)S(1)} %get-tuple-element.50.refs_0_, ...), custom_call_target="tpu_custom_call" | custom-call | flops 1610612736 | bytes 6815744 | tf_op jit(solution)/shard_map/pallas_call | solution.py:187
  51.5 1.4 %collective-permute-start.12 = (bf16[256,1024]{1,0:T(8,128)(2,1)S(1)}, bf16[256,1024]{1,0:T(8,128)(2,1)S(1)}, u32[]{:S(2)}, u32[]{:S(2)}) collective-permute-start(bf16[256,1024]{1,0:T(8,128)(2,1)S(1)} %get-tuple-element.58), channel_id=1, source_target_pairs={{0,128},{1,129},{2,130},{3,131},{4,132},{5,133},{6,134},{7,135},{8... | collective-permute-start | bytes 1572872 | tf_op jit(solution)/shard_map/ppermute | solution.py:29
  52.9 1.9 %collective-permute-start.14 = (bf16[256,1024]{1,0:T(8,128)(2,1)S(1)}, bf16[256,1024]{1,0:T(8,128)(2,1)S(1)}, u32[]{:S(2)}, u32[]{:S(2)}) collective-permute-start(bf16[256,1024]{1,0:T(8,128)(2,1)S(1)} %get-tuple-element.60), channel_id=1, source_target_pairs={{0,130},{1,131},{2,128},{3,129},{4,134},{5,135},{6,132},{7,133},{8... | collective-permute-start | bytes 1572872 | tf_op jit(solution)/shard_map/ppermute | solution.py:29
  54.8 0.0 copy-start.1
  54.8 3.0 %shard_map.45 = (bf16[144,1024]{1,0:T(8,128)(2,1)S(1)}, bf16[144,1024]{1,0:T(8,128)(2,1)S(1)}, f32[2,384]{1,0:T(2,128)S(1)}, f32[2,384]{1,0:T(2,128)S(1)}) custom-call(s32[32,32]{1,0:T(8,128)S(1)} %copy-done.2, bf16[768,1024]{1,0:T(8,128)(2,1)S(1)} %get-tuple-element.33.query_ref, f32[768,1]{1,0:T(8,128)S(1)} %get-tuple-element.45.refs_0_, ...), custom_call_target="tpu_custom_call" | custom-call | flops 1610612736 | bytes 5767168 | tf_op jit(solution)/shard_map/pallas_call | solution.py:187
  57.8 0.5 collective-permute-start.13
  58.3 0.6 collective-permute-start.15
  58.9 2.2 %collective-permute-start.11 = (f32[2,384]{1,0:T(2,128)S(1)}, f32[2,384]{1,0:T(2,128)S(1)}, u32[]{:S(2)}, u32[]{:S(2)}) collective-permute-start(f32[2,384]{1,0:T(2,128)S(1)} %get-tuple-element.56), channel_id=1, source_target_pairs={{0,2},{1,3},{2,0},{3,1},{4,6},{5,7},{6,4},{7,5},{8,10},{9,11},{10,... | collective-permute-start | bytes 9224 | tf_op jit(solution)/shard_map/ppermute | solution.py:29
  61.2 0.0 copy-done.1
  61.2 0.3 shard_map.46.pair_ref
  61.5 12.2 %collective-permute-done.11.half_stat_ref = f32[2,384]{1,0:T(2,128)S(1)} collective-permute-done((f32[2,384]{1,0:T(2,128)S(1)}, f32[2,384]{1,0:T(2,128)S(1)}, u32[]{:S(2)}, u32[]{:S(2)}) %collective-permute-start.11) | collective-permute-done | bytes 3104 | tf_op jit(solution)/shard_map/ppermute | solution.py:29
  73.7 0.0 collective-permute-done.13.near_late_ref
  73.7 0.0 collective-permute-done.15.far_late_ref
  73.7 0.0 collective-permute-done.12.near_early_ref
  73.7 0.0 collective-permute-done.14.far_early_ref
  73.7 1.4 %shard_map.47 = (bf16[384,1024]{1,0:T(8,128)(2,1)}, f32[1,384]{1,0:T(1,128)}) custom-call(f32[2,384]{1,0:T(2,128)S(1)} %get-tuple-element.55.here_stat_ref, f32[2,384]{1,0:T(2,128)S(1)} %collective-permute-done.11.half_stat_ref, f32[1,384]{1,0:T(1,128)S(1)} %shard_map.46.pair_ref, bf16[256,1024]{1,0:T(8,128)(2,1)S(1)} %collective-permute-done.12.near_early_ref, ...), custom_call_target="tpu_custom_call" | custom-call | tf_op jit(solution)/shard_map/pallas_call | solution.py:187
Async XLA Ops:
  0.6 10.7 %collective-permute-start.2 = (bf16[384,1024]{1,0:T(8,128)(2,1)}, bf16[384,1024]{1,0:T(8,128)(2,1)S(1)}, u32[]{:S(2)}, u32[]{:S(2)}) collective-permute-start(bf16[384,1024]{1,0:T(8,128)(2,1)} %bitcast.2), channel_id=1, source_target_pairs={{0,1},{1,0},{2,3},{3,2},{4,5},{5,4},{6,7},{7,6},{8,9},{9,8},{10,11... | collective-permute-start | bytes 2359304 | tf_op jit(solution)/shard_map/ppermute | solution.py:29
  4.0 15.3 %collective-permute-start.5 = (bf16[384,1024]{1,0:T(8,128)(2,1)}, bf16[384,1024]{1,0:T(8,128)(2,1)S(1)}, u32[]{:S(2)}, u32[]{:S(2)}) collective-permute-start(bf16[384,1024]{1,0:T(8,128)(2,1)} %bitcast.3), channel_id=1, source_target_pairs={{0,4},{1,125},{2,6},{3,127},{4,8},{5,1},{6,10},{7,3},{8,12},{9,5},... | collective-permute-start | bytes 2359304 | tf_op jit(solution)/shard_map/ppermute | solution.py:29
  10.0 14.5 %collective-permute-start = (bf16[384,1024]{1,0:T(8,128)(2,1)}, bf16[384,1024]{1,0:T(8,128)(2,1)S(1)}, u32[]{:S(2)}, u32[]{:S(2)}) collective-permute-start(bf16[384,1024]{1,0:T(8,128)(2,1)} %bitcast.4), channel_id=1, source_target_pairs={{0,128},{1,129},{2,130},{3,131},{4,132},{5,133},{6,134},{7,135},{8... | collective-permute-start | bytes 2359304 | tf_op jit(solution)/shard_map/ppermute | solution.py:29
  11.3 16.3 %collective-permute-start.3 = (bf16[384,1024]{1,0:T(8,128)(2,1)S(1)}, bf16[384,1024]{1,0:T(8,128)(2,1)S(1)}, u32[]{:S(2)}, u32[]{:S(2)}) collective-permute-start(bf16[384,1024]{1,0:T(8,128)(2,1)S(1)} %collective-permute-done.2.sibling_ref), channel_id=1, source_target_pairs={{0,4},{1,125},{2,6},{3,127},{4,8},{5,1},{6,10},{7,3},{8,12},{9,5},... | collective-permute-start | bytes 2359304 | tf_op jit(solution)/shard_map/ppermute | solution.py:29
  12.1 20.7 %collective-permute-start.1 = (bf16[384,1024]{1,0:T(8,128)(2,1)}, bf16[384,1024]{1,0:T(8,128)(2,1)S(1)}, u32[]{:S(2)}, u32[]{:S(2)}) collective-permute-start(bf16[384,1024]{1,0:T(8,128)(2,1)} %bitcast.5), channel_id=1, source_target_pairs={{0,130},{1,131},{2,128},{3,129},{4,134},{5,135},{6,132},{7,133},{8... | collective-permute-start | bytes 2359304 | tf_op jit(solution)/shard_map/ppermute | solution.py:29
  19.2 17.5 %collective-permute-start.6 = (bf16[384,1024]{1,0:T(8,128)(2,1)S(1)}, bf16[384,1024]{1,0:T(8,128)(2,1)S(1)}, u32[]{:S(2)}, u32[]{:S(2)}) collective-permute-start(bf16[384,1024]{1,0:T(8,128)(2,1)S(1)} %collective-permute-done.5.refs_3_), channel_id=1, source_target_pairs={{0,4},{1,125},{2,6},{3,127},{4,8},{5,1},{6,10},{7,3},{8,12},{9,5},... | collective-permute-start | bytes 2359304 | tf_op jit(solution)/shard_map/ppermute | solution.py:29
  24.5 12.9 %collective-permute-start.7 = (bf16[384,1024]{1,0:T(8,128)(2,1)S(1)}, bf16[384,1024]{1,0:T(8,128)(2,1)S(1)}, u32[]{:S(2)}, u32[]{:S(2)}) collective-permute-start(bf16[384,1024]{1,0:T(8,128)(2,1)S(1)} %collective-permute-done.5.refs_3_), channel_id=1, source_target_pairs={{0,1},{1,0},{2,3},{3,2},{4,5},{5,4},{6,7},{7,6},{8,9},{9,8},{10,11... | collective-permute-start | bytes 2359304 | tf_op jit(solution)/shard_map/ppermute | solution.py:29
  27.6 9.8 %collective-permute-start.8 = (bf16[384,1024]{1,0:T(8,128)(2,1)S(1)}, bf16[384,1024]{1,0:T(8,128)(2,1)S(1)}, u32[]{:S(2)}, u32[]{:S(2)}) collective-permute-start(bf16[384,1024]{1,0:T(8,128)(2,1)S(1)} %collective-permute-done.3.refs_4_), channel_id=1, source_target_pairs={{0,1},{1,0},{2,3},{3,2},{4,5},{5,4},{6,7},{7,6},{8,9},{9,8},{10,11... | collective-permute-start | bytes 2359304 | tf_op jit(solution)/shard_map/ppermute | solution.py:29
  29.0 15.4 %collective-permute-start.4 = (bf16[384,1024]{1,0:T(8,128)(2,1)S(1)}, bf16[384,1024]{1,0:T(8,128)(2,1)S(1)}, u32[]{:S(2)}, u32[]{:S(2)}) collective-permute-start(bf16[384,1024]{1,0:T(8,128)(2,1)S(1)} %collective-permute-done.3.refs_4_), channel_id=1, source_target_pairs={{0,4},{1,125},{2,6},{3,127},{4,8},{5,1},{6,10},{7,3},{8,12},{9,5},... | collective-permute-start | bytes 2359304 | tf_op jit(solution)/shard_map/ppermute | solution.py:29
  32.8 1.1 %copy-start = (bf16[1,384,1024]{2,1,0:T(8,128)(2,1)S(1)}, bf16[1,384,1024]{2,1,0:T(8,128)(2,1)}, u32[]{:S(2)}) copy-start(bf16[1,384,1024]{2,1,0:T(8,128)(2,1)} %param.2) | copy-start | bytes 2359300
  33.9 3.5 %copy-start.2 = (s32[32,32]{1,0:T(8,128)S(1)}, s32[32,32]{1,0:T(8,128)}, u32[]{:S(2)}) copy-start(s32[32,32]{1,0:T(8,128)} %mask_ref.7) | copy-start | bytes 12292
  36.8 9.0 %collective-permute-start.9 = (bf16[384,1024]{1,0:T(8,128)(2,1)S(1)}, bf16[384,1024]{1,0:T(8,128)(2,1)S(1)}, u32[]{:S(2)}, u32[]{:S(2)}) collective-permute-start(bf16[384,1024]{1,0:T(8,128)(2,1)S(1)} %collective-permute-done.6.refs_3_), channel_id=1, source_target_pairs={{0,1},{1,0},{2,3},{3,2},{4,5},{5,4},{6,7},{7,6},{8,9},{9,8},{10,11... | collective-permute-start | bytes 2359304 | tf_op jit(solution)/shard_map/ppermute | solution.py:29
  44.4 4.2 %collective-permute-start.10 = (bf16[384,1024]{1,0:T(8,128)(2,1)S(1)}, bf16[384,1024]{1,0:T(8,128)(2,1)S(1)}, u32[]{:S(2)}, u32[]{:S(2)}) collective-permute-start(bf16[384,1024]{1,0:T(8,128)(2,1)S(1)} %collective-permute-done.4.refs_3_.refs_5_), channel_id=1, source_target_pairs={{0,1},{1,0},{2,3},{3,2},{4,5},{5,4},{6,7},{7,6},{8,9},{9,8},{10,11... | collective-permute-start | bytes 2359304 | tf_op jit(solution)/shard_map/ppermute | solution.py:29
  51.5 22.2 %collective-permute-start.12 = (bf16[256,1024]{1,0:T(8,128)(2,1)S(1)}, bf16[256,1024]{1,0:T(8,128)(2,1)S(1)}, u32[]{:S(2)}, u32[]{:S(2)}) collective-permute-start(bf16[256,1024]{1,0:T(8,128)(2,1)S(1)} %get-tuple-element.58), channel_id=1, source_target_pairs={{0,128},{1,129},{2,130},{3,131},{4,132},{5,133},{6,134},{7,135},{8... | collective-permute-start | bytes 1572872 | tf_op jit(solution)/shard_map/ppermute | solution.py:29
  52.9 20.8 %collective-permute-start.14 = (bf16[256,1024]{1,0:T(8,128)(2,1)S(1)}, bf16[256,1024]{1,0:T(8,128)(2,1)S(1)}, u32[]{:S(2)}, u32[]{:S(2)}) collective-permute-start(bf16[256,1024]{1,0:T(8,128)(2,1)S(1)} %get-tuple-element.60), channel_id=1, source_target_pairs={{0,130},{1,131},{2,128},{3,129},{4,134},{5,135},{6,132},{7,133},{8... | collective-permute-start | bytes 1572872 | tf_op jit(solution)/shard_map/ppermute | solution.py:29
  54.8 6.4 %copy-start.1 = (bf16[1,384,1024]{2,1,0:T(8,128)(2,1)S(1)}, bf16[1,384,1024]{2,1,0:T(8,128)(2,1)}, u32[]{:S(2)}) copy-start(bf16[1,384,1024]{2,1,0:T(8,128)(2,1)} %param.2) | copy-start | bytes 2359300
  57.8 15.9 %collective-permute-start.13 = (bf16[144,1024]{1,0:T(8,128)(2,1)S(1)}, bf16[144,1024]{1,0:T(8,128)(2,1)S(1)}, u32[]{:S(2)}, u32[]{:S(2)}) collective-permute-start(bf16[144,1024]{1,0:T(8,128)(2,1)S(1)} %get-tuple-element.59), channel_id=1, source_target_pairs={{0,128},{1,129},{2,130},{3,131},{4,132},{5,133},{6,134},{7,135},{8... | collective-permute-start | bytes 884744 | tf_op jit(solution)/shard_map/ppermute | solution.py:29
  58.3 15.4 %collective-permute-start.15 = (bf16[144,1024]{1,0:T(8,128)(2,1)S(1)}, bf16[144,1024]{1,0:T(8,128)(2,1)S(1)}, u32[]{:S(2)}, u32[]{:S(2)}) collective-permute-start(bf16[144,1024]{1,0:T(8,128)(2,1)S(1)} %get-tuple-element.61), channel_id=1, source_target_pairs={{0,130},{1,131},{2,128},{3,129},{4,134},{5,135},{6,132},{7,133},{8... | collective-permute-start | bytes 884744 | tf_op jit(solution)/shard_map/ppermute | solution.py:29
  58.9 14.8 %collective-permute-start.11 = (f32[2,384]{1,0:T(2,128)S(1)}, f32[2,384]{1,0:T(2,128)S(1)}, u32[]{:S(2)}, u32[]{:S(2)}) collective-permute-start(f32[2,384]{1,0:T(2,128)S(1)} %get-tuple-element.56), channel_id=1, source_target_pairs={{0,2},{1,3},{2,0},{3,1},{4,6},{5,7},{6,4},{7,5},{8,10},{9,11},{10,... | collective-permute-start | bytes 9224 | tf_op jit(solution)/shard_map/ppermute | solution.py:29

commit v7 on v6

--- a/solution.py
+++ b/solution.py
@@ -269,15 +269,14 @@
         scratch=[pltpu.VMEM(own.shape, own.dtype), pltpu.SemaphoreType.DMA(())],
         left=(2,),
     )
-    first_2, state = lax.optimization_barrier((first_2, state))
-    first_2_sib = moved(first_2, sibling)
     state = call(
         functools.partial(middle_kernel, score_scale, (1, 1, -1, -1)),
         held(2 * rows, width),
         [block_mask, queries, *state, first_1, second_1, first_1_sib, second_1_sib],
         smem=True,
     )
-    second_2, state = lax.optimization_barrier((second_2, state))
+    first_2, second_2 = after(first_2, state[0]), after(second_2, state[0])
+    first_2_sib = moved(first_2, sibling)
     second_2_sib = moved(second_2, sibling)
     ring_2 = [first_2, first_2_sib, second_2, second_2_sib]
     early_state = call(

time: 75.3 us -> 83.2 us (1.10)
  waiting for transfers between devices: 20.6 us -> 30.4 us
  starting transfers between devices: 33.2 us -> 31.2 us
    ppermute x16, waiting for transfers between devices: 20.6 us -> 30.4 us  [moved(): return lax.ppermute(value, AXES, pairs)]
    ppermute x16, starting transfers between devices: 33.2 us -> 31.2 us  [moved(): return lax.ppermute(value, AXES, pairs)]
  transfers between devices with their start and end apart: 16 -> 16, of which waited for: 5 -> 4; matrix products, arithmetic and copies ran while one was open for 0% -> 0% of each run, Pallas kernels for 20% -> 18%
where the time goes in v7:
time: 83.2 us; the launch traced here: 83 us
  starting transfers between devices  31.2 us (38%)
  waiting for transfers between devices  30.4 us (37%)
  Pallas kernels  19.5 us (23%)
  local copies, waits for them, and re-layouts  1.14 us (1%)
    ppermute x16, starting transfers between devices, moved(): return lax.ppermute(value, AXES, pairs)  31.2 us
    ppermute x16, waiting for transfers between devices, moved(): return lax.ppermute(value, AXES, pairs)  30.4 us
    pallas_call x7, Pallas kernels, call(): pl.pallas_call(kernel, out_shape=out, in_specs=[SMEM if smem and index ==...  19.5 us
  transfers between devices with their start and end apart: 16, of which 4 were waited for; matrix products, arithmetic and copies ran while one was open for 0% of the time, Pallas kernels for 18%

profile of v7, /device:TPU:1, one launch (start us, length us, event | category | flops | bytes accessed | tf_op | source)
XLA Modules:
  0.0 83.0 jit_solution(1461000053069536815)
XLA Ops:
  0.6 3.3 %collective-permute-start.2 = (bf16[384,1024]{1,0:T(8,128)(2,1)}, bf16[384,1024]{1,0:T(8,128)(2,1)S(1)}, u32[]{:S(2)}, u32[]{:S(2)}) collective-permute-start(bf16[384,1024]{1,0:T(8,128)(2,1)} %bitcast.2), channel_id=1, source_target_pairs={{0,1},{1,0},{2,3},{3,2},{4,5},{5,4},{6,7},{7,6},{8,9},{9,8},{10,11... | collective-permute-start | bytes 2359304 | tf_op jit(solution)/shard_map/ppermute | solution.py:29
  4.0 0.0 collective-permute-start
  4.0 7.3 %collective-permute-start.3 = (bf16[384,1024]{1,0:T(8,128)(2,1)}, bf16[384,1024]{1,0:T(8,128)(2,1)S(1)}, u32[]{:S(2)}, u32[]{:S(2)}) collective-permute-start(bf16[384,1024]{1,0:T(8,128)(2,1)} %bitcast.4), channel_id=1, source_target_pairs={{0,4},{1,125},{2,6},{3,127},{4,8},{5,1},{6,10},{7,3},{8,12},{9,5},... | collective-permute-start | bytes 2359304 | tf_op jit(solution)/shard_map/ppermute | solution.py:29
  11.3 0.0 collective-permute-done.2.sibling_ref
  11.3 0.8 collective-permute-start.4
  12.1 2.7 %collective-permute-start.1 = (bf16[384,1024]{1,0:T(8,128)(2,1)}, bf16[384,1024]{1,0:T(8,128)(2,1)S(1)}, u32[]{:S(2)}, u32[]{:S(2)}) collective-permute-start(bf16[384,1024]{1,0:T(8,128)(2,1)} %bitcast.5), channel_id=1, source_target_pairs={{0,130},{1,131},{2,128},{3,129},{4,134},{5,135},{6,132},{7,133},{8... | collective-permute-start | bytes 2359304 | tf_op jit(solution)/shard_map/ppermute | solution.py:29
  14.8 8.4 %collective-permute-done.near_ref = bf16[384,1024]{1,0:T(8,128)(2,1)S(1)} collective-permute-done((bf16[384,1024]{1,0:T(8,128)(2,1)}, bf16[384,1024]{1,0:T(8,128)(2,1)S(1)}, u32[]{:S(2)}, u32[]{:S(2)}) %collective-permute-start) | collective-permute-done | bytes 786464 | tf_op jit(solution)/shard_map/ppermute | solution.py:29
  23.3 0.0 collective-permute-done.3.refs_3_
  23.3 0.9 %collective-permute-start.5 = (bf16[384,1024]{1,0:T(8,128)(2,1)S(1)}, bf16[384,1024]{1,0:T(8,128)(2,1)S(1)}, u32[]{:S(2)}, u32[]{:S(2)}) collective-permute-start(bf16[384,1024]{1,0:T(8,128)(2,1)S(1)} %collective-permute-done.3.refs_3_), channel_id=1, source_target_pairs={{0,1},{1,0},{2,3},{3,2},{4,5},{5,4},{6,7},{7,6},{8,9},{9,8},{10,11... | collective-permute-start | bytes 2359304 | tf_op jit(solution)/shard_map/ppermute | solution.py:29
  24.1 4.7 %collective-permute-done.4.refs_4_ = bf16[384,1024]{1,0:T(8,128)(2,1)S(1)} collective-permute-done((bf16[384,1024]{1,0:T(8,128)(2,1)S(1)}, bf16[384,1024]{1,0:T(8,128)(2,1)S(1)}, u32[]{:S(2)}, u32[]{:S(2)}) %collective-permute-start.4) | collective-permute-done | bytes 786464 | tf_op jit(solution)/shard_map/ppermute | solution.py:29
  28.9 1.7 %collective-permute-start.6 = (bf16[384,1024]{1,0:T(8,128)(2,1)S(1)}, bf16[384,1024]{1,0:T(8,128)(2,1)S(1)}, u32[]{:S(2)}, u32[]{:S(2)}) collective-permute-start(bf16[384,1024]{1,0:T(8,128)(2,1)S(1)} %collective-permute-done.4.refs_4_), channel_id=1, source_target_pairs={{0,1},{1,0},{2,3},{3,2},{4,5},{5,4},{6,7},{7,6},{8,9},{9,8},{10,11... | collective-permute-start | bytes 2359304 | tf_op jit(solution)/shard_map/ppermute | solution.py:29
  30.6 3.5 %collective-permute-start.7 = (bf16[384,1024]{1,0:T(8,128)(2,1)S(1)}, bf16[384,1024]{1,0:T(8,128)(2,1)S(1)}, u32[]{:S(2)}, u32[]{:S(2)}) collective-permute-start(bf16[384,1024]{1,0:T(8,128)(2,1)S(1)} %collective-permute-done.3.refs_3_), channel_id=1, source_target_pairs={{0,4},{1,125},{2,6},{3,127},{4,8},{5,1},{6,10},{7,3},{8,12},{9,5},... | collective-permute-start | bytes 2359304 | tf_op jit(solution)/shard_map/ppermute | solution.py:29
  34.1 0.0 collective-permute-start.9
  34.1 0.0 collective-permute-done.1.far_ref
  34.1 0.0 copy-start
  34.1 1.1 %copy-done = bf16[1,384,1024]{2,1,0:T(8,128)(2,1)S(1)} copy-done((bf16[1,384,1024]{2,1,0:T(8,128)(2,1)S(1)}, bf16[1,384,1024]{2,1,0:T(8,128)(2,1)}, u32[]{:S(2)}) %copy-start) | copy-done | bytes 786456
  35.3 0.0 copy-start.2
  35.3 2.8 %shard_map.41 = (f32[768,1]{1,0:T(8,128)S(1)}, f32[768,1]{1,0:T(8,128)S(1)}, f32[768,1024]{1,0:T(8,128)S(1)}, bf16[768,1024]{1,0:T(8,128)(2,1)S(1)}) custom-call(bf16[384,1024]{1,0:T(8,128)(2,1)S(1)} %collective-permute-done.near_ref, bf16[384,1024]{1,0:T(8,128)(2,1)S(1)} %collective-permute-done.1.far_ref, bf16[384,1024]{1,0:T(8,128)(2,1)S(1)} %bitcast.6, ...), custom_call_target="tpu_custom_call" | custom-call | tf_op jit(solution)/shard_map/pallas_call | solution.py:187
  38.1 0.0 collective-permute-done.5.refs_5_
  38.1 0.0 collective-permute-done.6.refs_6_
  38.1 0.0 copy-done.2
  38.2 6.2 %shard_map.42 = (f32[768,1]{1,0:T(8,128)S(1)}, f32[768,1]{1,0:T(8,128)S(1)}, f32[768,1024]{1,0:T(8,128)S(1)}) custom-call(s32[32,32]{1,0:T(8,128)S(1)} %copy-done.2, bf16[768,1024]{1,0:T(8,128)(2,1)S(1)} %get-tuple-element.27.query_ref, f32[768,1]{1,0:T(8,128)S(1)} %get-tuple-element.28.refs_0_, f32[768,1]{1,0:T(8,128)S(1)} %get-tuple-element.29.refs_1_, ...), custom_call_target="tpu_custom_call" | custom-call | tf_op jit(solution)/shard_map/pallas_call | solution.py:187
  44.4 0.0 collective-permute-done.7.refs_3_
  44.4 1.5 %collective-permute-start.8 = (bf16[384,1024]{1,0:T(8,128)(2,1)S(1)}, bf16[384,1024]{1,0:T(8,128)(2,1)S(1)}, u32[]{:S(2)}, u32[]{:S(2)}) collective-permute-start(bf16[384,1024]{1,0:T(8,128)(2,1)S(1)} %collective-permute-done.7.refs_3_), channel_id=1, source_target_pairs={{0,1},{1,0},{2,3},{3,2},{4,5},{5,4},{6,7},{7,6},{8,9},{9,8},{10,11... | collective-permute-start | bytes 2359304 | tf_op jit(solution)/shard_map/ppermute | solution.py:29
  45.9 5.6 %collective-permute-done.9.refs_3_.refs_5_ = bf16[384,1024]{1,0:T(8,128)(2,1)S(1)} collective-permute-done((bf16[384,1024]{1,0:T(8,128)(2,1)S(1)}, bf16[384,1024]{1,0:T(8,128)(2,1)S(1)}, u32[]{:S(2)}, u32[]{:S(2)}) %collective-permute-start.9) | collective-permute-done | bytes 786464 | tf_op jit(solution)/shard_map/ppermute | solution.py:29
  51.5 2.9 %collective-permute-start.10 = (bf16[384,1024]{1,0:T(8,128)(2,1)S(1)}, bf16[384,1024]{1,0:T(8,128)(2,1)S(1)}, u32[]{:S(2)}, u32[]{:S(2)}) collective-permute-start(bf16[384,1024]{1,0:T(8,128)(2,1)S(1)} %collective-permute-done.9.refs_3_.refs_5_), channel_id=1, source_target_pairs={{0,1},{1,0},{2,3},{3,2},{4,5},{5,4},{6,7},{7,6},{8,9},{9,8},{10,11... | collective-permute-start | bytes 2359304 | tf_op jit(solution)/shard_map/ppermute | solution.py:29
  54.3 0.0 collective-permute-done.8.refs_4_
  54.3 2.8 %shard_map.43 = (f32[512,1]{1,0:T(8,128)S(1)}, f32[512,1]{1,0:T(8,128)S(1)}, f32[512,1024]{1,0:T(8,128)S(1)}) custom-call(s32[32,32]{1,0:T(8,128)S(1)} %copy-done.2, bf16[768,1024]{1,0:T(8,128)(2,1)S(1)} %get-tuple-element.27.query_ref, f32[768,1]{1,0:T(8,128)S(1)} %get-tuple-element.33.refs_0_, f32[768,1]{1,0:T(8,128)S(1)} %get-tuple-element.34.refs_1_, ...), custom_call_target="tpu_custom_call" | custom-call | flops 1610612736 | bytes 6815744 | tf_op jit(solution)/shard_map/pallas_call | solution.py:187
  57.1 0.0 collective-permute-done.10.refs_4_.refs_6_
  57.1 2.9 %shard_map.44 = (bf16[256,1024]{1,0:T(8,128)(2,1)S(1)}, bf16[256,1024]{1,0:T(8,128)(2,1)S(1)}, f32[2,256]{1,0:T(2,128)S(1)}, f32[2,256]{1,0:T(2,128)S(1)}) custom-call(s32[32,32]{1,0:T(8,128)S(1)} %copy-done.2, bf16[768,1024]{1,0:T(8,128)(2,1)S(1)} %get-tuple-element.27.query_ref, f32[512,1]{1,0:T(8,128)S(1)} %get-tuple-element.38.refs_0_, ...), custom_call_target="tpu_custom_call" | custom-call | flops 1610612736 | bytes 6815744 | tf_op jit(solution)/shard_map/pallas_call | solution.py:187
  60.0 0.5 collective-permute-start.12
  60.5 2.7 %collective-permute-start.14 = (bf16[256,1024]{1,0:T(8,128)(2,1)S(1)}, bf16[256,1024]{1,0:T(8,128)(2,1)S(1)}, u32[]{:S(2)}, u32[]{:S(2)}) collective-permute-start(bf16[256,1024]{1,0:T(8,128)(2,1)S(1)} %get-tuple-element.48), channel_id=1, source_target_pairs={{0,130},{1,131},{2,128},{3,129},{4,134},{5,135},{6,132},{7,133},{8... | collective-permute-start | bytes 1572872 | tf_op jit(solution)/shard_map/ppermute | solution.py:29
  63.2 0.0 copy-start.1
  63.2 3.0 %shard_map.45 = (bf16[144,1024]{1,0:T(8,128)(2,1)S(1)}, bf16[144,1024]{1,0:T(8,128)(2,1)S(1)}, f32[2,384]{1,0:T(2,128)S(1)}, f32[2,384]{1,0:T(2,128)S(1)}) custom-call(s32[32,32]{1,0:T(8,128)S(1)} %copy-done.2, bf16[768,1024]{1,0:T(8,128)(2,1)S(1)} %get-tuple-element.27.query_ref, f32[768,1]{1,0:T(8,128)S(1)} %get-tuple-element.33.refs_0_, ...), custom_call_target="tpu_custom_call" | custom-call | flops 1610612736 | bytes 5767168 | tf_op jit(solution)/shard_map/pallas_call | solution.py:187
  66.3 0.1 collective-permute-start.13
  66.4 0.6 collective-permute-start.15
  67.0 2.6 %collective-permute-start.11 = (f32[2,384]{1,0:T(2,128)S(1)}, f32[2,384]{1,0:T(2,128)S(1)}, u32[]{:S(2)}, u32[]{:S(2)}) collective-permute-start(f32[2,384]{1,0:T(2,128)S(1)} %get-tuple-element.44), channel_id=1, source_target_pairs={{0,2},{1,3},{2,0},{3,1},{4,6},{5,7},{6,4},{7,5},{8,10},{9,11},{10,... | collective-permute-start | bytes 9224 | tf_op jit(solution)/shard_map/ppermute | solution.py:29
  69.6 0.0 copy-done.1
  69.6 0.3 shard_map.46.pair_ref
  69.9 11.7 %collective-permute-done.11.half_stat_ref = f32[2,384]{1,0:T(2,128)S(1)} collective-permute-done((f32[2,384]{1,0:T(2,128)S(1)}, f32[2,384]{1,0:T(2,128)S(1)}, u32[]{:S(2)}, u32[]{:S(2)}) %collective-permute-start.11) | collective-permute-done | bytes 3104 | tf_op jit(solution)/shard_map/ppermute | solution.py:29
  81.6 0.0 collective-permute-done.13.near_late_ref
  81.6 0.0 collective-permute-done.15.far_late_ref
  81.6 0.0 collective-permute-done.12.near_early_ref
  81.6 0.0 collective-permute-done.14.far_early_ref
  81.6 1.4 %shard_map.47 = (bf16[384,1024]{1,0:T(8,128)(2,1)}, f32[1,384]{1,0:T(1,128)}) custom-call(f32[2,384]{1,0:T(2,128)S(1)} %get-tuple-element.43.here_stat_ref, f32[2,384]{1,0:T(2,128)S(1)} %collective-permute-done.11.half_stat_ref, f32[1,384]{1,0:T(1,128)S(1)} %shard_map.46.pair_ref, bf16[256,1024]{1,0:T(8,128)(2,1)S(1)} %collective-permute-done.12.near_early_ref, ...), custom_call_target="tpu_custom_call" | custom-call | tf_op jit(solution)/shard_map/pallas_call | solution.py:187
Async XLA Ops:
  0.6 10.7 %collective-permute-start.2 = (bf16[384,1024]{1,0:T(8,128)(2,1)}, bf16[384,1024]{1,0:T(8,128)(2,1)S(1)}, u32[]{:S(2)}, u32[]{:S(2)}) collective-permute-start(bf16[384,1024]{1,0:T(8,128)(2,1)} %bitcast.2), channel_id=1, source_target_pairs={{0,1},{1,0},{2,3},{3,2},{4,5},{5,4},{6,7},{7,6},{8,9},{9,8},{10,11... | collective-permute-start | bytes 2359304 | tf_op jit(solution)/shard_map/ppermute | solution.py:29
  4.0 19.3 %collective-permute-start = (bf16[384,1024]{1,0:T(8,128)(2,1)}, bf16[384,1024]{1,0:T(8,128)(2,1)S(1)}, u32[]{:S(2)}, u32[]{:S(2)}) collective-permute-start(bf16[384,1024]{1,0:T(8,128)(2,1)} %bitcast.3), channel_id=1, source_target_pairs={{0,128},{1,129},{2,130},{3,131},{4,132},{5,133},{6,134},{7,135},{8... | collective-permute-start | bytes 2359304 | tf_op jit(solution)/shard_map/ppermute | solution.py:29
  4.0 19.3 %collective-permute-start.3 = (bf16[384,1024]{1,0:T(8,128)(2,1)}, bf16[384,1024]{1,0:T(8,128)(2,1)S(1)}, u32[]{:S(2)}, u32[]{:S(2)}) collective-permute-start(bf16[384,1024]{1,0:T(8,128)(2,1)} %bitcast.4), channel_id=1, source_target_pairs={{0,4},{1,125},{2,6},{3,127},{4,8},{5,1},{6,10},{7,3},{8,12},{9,5},... | collective-permute-start | bytes 2359304 | tf_op jit(solution)/shard_map/ppermute | solution.py:29
  11.3 17.6 %collective-permute-start.4 = (bf16[384,1024]{1,0:T(8,128)(2,1)S(1)}, bf16[384,1024]{1,0:T(8,128)(2,1)S(1)}, u32[]{:S(2)}, u32[]{:S(2)}) collective-permute-start(bf16[384,1024]{1,0:T(8,128)(2,1)S(1)} %collective-permute-done.2.sibling_ref), channel_id=1, source_target_pairs={{0,4},{1,125},{2,6},{3,127},{4,8},{5,1},{6,10},{7,3},{8,12},{9,5},... | collective-permute-start | bytes 2359304 | tf_op jit(solution)/shard_map/ppermute | solution.py:29
  12.1 22.0 %collective-permute-start.1 = (bf16[384,1024]{1,0:T(8,128)(2,1)}, bf16[384,1024]{1,0:T(8,128)(2,1)S(1)}, u32[]{:S(2)}, u32[]{:S(2)}) collective-permute-start(bf16[384,1024]{1,0:T(8,128)(2,1)} %bitcast.5), channel_id=1, source_target_pairs={{0,130},{1,131},{2,128},{3,129},{4,134},{5,135},{6,132},{7,133},{8... | collective-permute-start | bytes 2359304 | tf_op jit(solution)/shard_map/ppermute | solution.py:29
  23.3 14.9 %collective-permute-start.5 = (bf16[384,1024]{1,0:T(8,128)(2,1)S(1)}, bf16[384,1024]{1,0:T(8,128)(2,1)S(1)}, u32[]{:S(2)}, u32[]{:S(2)}) collective-permute-start(bf16[384,1024]{1,0:T(8,128)(2,1)S(1)} %collective-permute-done.3.refs_3_), channel_id=1, source_target_pairs={{0,1},{1,0},{2,3},{3,2},{4,5},{5,4},{6,7},{7,6},{8,9},{9,8},{10,11... | collective-permute-start | bytes 2359304 | tf_op jit(solution)/shard_map/ppermute | solution.py:29
  28.9 9.3 %collective-permute-start.6 = (bf16[384,1024]{1,0:T(8,128)(2,1)S(1)}, bf16[384,1024]{1,0:T(8,128)(2,1)S(1)}, u32[]{:S(2)}, u32[]{:S(2)}) collective-permute-start(bf16[384,1024]{1,0:T(8,128)(2,1)S(1)} %collective-permute-done.4.refs_4_), channel_id=1, source_target_pairs={{0,1},{1,0},{2,3},{3,2},{4,5},{5,4},{6,7},{7,6},{8,9},{9,8},{10,11... | collective-permute-start | bytes 2359304 | tf_op jit(solution)/shard_map/ppermute | solution.py:29
  30.6 13.8 %collective-permute-start.7 = (bf16[384,1024]{1,0:T(8,128)(2,1)S(1)}, bf16[384,1024]{1,0:T(8,128)(2,1)S(1)}, u32[]{:S(2)}, u32[]{:S(2)}) collective-permute-start(bf16[384,1024]{1,0:T(8,128)(2,1)S(1)} %collective-permute-done.3.refs_3_), channel_id=1, source_target_pairs={{0,4},{1,125},{2,6},{3,127},{4,8},{5,1},{6,10},{7,3},{8,12},{9,5},... | collective-permute-start | bytes 2359304 | tf_op jit(solution)/shard_map/ppermute | solution.py:29
  34.1 17.4 %collective-permute-start.9 = (bf16[384,1024]{1,0:T(8,128)(2,1)S(1)}, bf16[384,1024]{1,0:T(8,128)(2,1)S(1)}, u32[]{:S(2)}, u32[]{:S(2)}) collective-permute-start(bf16[384,1024]{1,0:T(8,128)(2,1)S(1)} %collective-permute-done.4.refs_4_), channel_id=1, source_target_pairs={{0,4},{1,125},{2,6},{3,127},{4,8},{5,1},{6,10},{7,3},{8,12},{9,5},... | collective-permute-start | bytes 2359304 | tf_op jit(solution)/shard_map/ppermute | solution.py:29
  34.1 1.1 %copy-start = (bf16[1,384,1024]{2,1,0:T(8,128)(2,1)S(1)}, bf16[1,384,1024]{2,1,0:T(8,128)(2,1)}, u32[]{:S(2)}) copy-start(bf16[1,384,1024]{2,1,0:T(8,128)(2,1)} %param.2) | copy-start | bytes 2359300
  35.3 2.9 %copy-start.2 = (s32[32,32]{1,0:T(8,128)S(1)}, s32[32,32]{1,0:T(8,128)}, u32[]{:S(2)}) copy-start(s32[32,32]{1,0:T(8,128)} %mask_ref.7) | copy-start | bytes 12292
  44.4 9.9 %collective-permute-start.8 = (bf16[384,1024]{1,0:T(8,128)(2,1)S(1)}, bf16[384,1024]{1,0:T(8,128)(2,1)S(1)}, u32[]{:S(2)}, u32[]{:S(2)}) collective-permute-start(bf16[384,1024]{1,0:T(8,128)(2,1)S(1)} %collective-permute-done.7.refs_3_), channel_id=1, source_target_pairs={{0,1},{1,0},{2,3},{3,2},{4,5},{5,4},{6,7},{7,6},{8,9},{9,8},{10,11... | collective-permute-start | bytes 2359304 | tf_op jit(solution)/shard_map/ppermute | solution.py:29
  51.5 5.7 %collective-permute-start.10 = (bf16[384,1024]{1,0:T(8,128)(2,1)S(1)}, bf16[384,1024]{1,0:T(8,128)(2,1)S(1)}, u32[]{:S(2)}, u32[]{:S(2)}) collective-permute-start(bf16[384,1024]{1,0:T(8,128)(2,1)S(1)} %collective-permute-done.9.refs_3_.refs_5_), channel_id=1, source_target_pairs={{0,1},{1,0},{2,3},{3,2},{4,5},{5,4},{6,7},{7,6},{8,9},{9,8},{10,11... | collective-permute-start | bytes 2359304 | tf_op jit(solution)/shard_map/ppermute | solution.py:29
  60.0 21.6 %collective-permute-start.12 = (bf16[256,1024]{1,0:T(8,128)(2,1)S(1)}, bf16[256,1024]{1,0:T(8,128)(2,1)S(1)}, u32[]{:S(2)}, u32[]{:S(2)}) collective-permute-start(bf16[256,1024]{1,0:T(8,128)(2,1)S(1)} %get-tuple-element.46), channel_id=1, source_target_pairs={{0,128},{1,129},{2,130},{3,131},{4,132},{5,133},{6,134},{7,135},{8... | collective-permute-start | bytes 1572872 | tf_op jit(solution)/shard_map/ppermute | solution.py:29
  60.5 21.1 %collective-permute-start.14 = (bf16[256,1024]{1,0:T(8,128)(2,1)S(1)}, bf16[256,1024]{1,0:T(8,128)(2,1)S(1)}, u32[]{:S(2)}, u32[]{:S(2)}) collective-permute-start(bf16[256,1024]{1,0:T(8,128)(2,1)S(1)} %get-tuple-element.48), channel_id=1, source_target_pairs={{0,130},{1,131},{2,128},{3,129},{4,134},{5,135},{6,132},{7,133},{8... | collective-permute-start | bytes 1572872 | tf_op jit(solution)/shard_map/ppermute | solution.py:29
  63.2 6.4 %copy-start.1 = (bf16[1,384,1024]{2,1,0:T(8,128)(2,1)S(1)}, bf16[1,384,1024]{2,1,0:T(8,128)(2,1)}, u32[]{:S(2)}) copy-start(bf16[1,384,1024]{2,1,0:T(8,128)(2,1)} %param.2) | copy-start | bytes 2359300
  66.3 15.3 %collective-permute-start.13 = (bf16[144,1024]{1,0:T(8,128)(2,1)S(1)}, bf16[144,1024]{1,0:T(8,128)(2,1)S(1)}, u32[]{:S(2)}, u32[]{:S(2)}) collective-permute-start(bf16[144,1024]{1,0:T(8,128)(2,1)S(1)} %get-tuple-element.47), channel_id=1, source_target_pairs={{0,128},{1,129},{2,130},{3,131},{4,132},{5,133},{6,134},{7,135},{8... | collective-permute-start | bytes 884744 | tf_op jit(solution)/shard_map/ppermute | solution.py:29
  66.4 15.2 %collective-permute-start.15 = (bf16[144,1024]{1,0:T(8,128)(2,1)S(1)}, bf16[144,1024]{1,0:T(8,128)(2,1)S(1)}, u32[]{:S(2)}, u32[]{:S(2)}) collective-permute-start(bf16[144,1024]{1,0:T(8,128)(2,1)S(1)} %get-tuple-element.49), channel_id=1, source_target_pairs={{0,130},{1,131},{2,128},{3,129},{4,134},{5,135},{6,132},{7,133},{8... | collective-permute-start | bytes 884744 | tf_op jit(solution)/shard_map/ppermute | solution.py:29
  67.0 14.6 %collective-permute-start.11 = (f32[2,384]{1,0:T(2,128)S(1)}, f32[2,384]{1,0:T(2,128)S(1)}, u32[]{:S(2)}, u32[]{:S(2)}) collective-permute-start(f32[2,384]{1,0:T(2,128)S(1)} %get-tuple-element.44), channel_id=1, source_target_pairs={{0,2},{1,3},{2,0},{3,1},{4,6},{5,7},{6,4},{7,5},{8,10},{9,11},{10,... | collective-permute-start | bytes 9224 | tf_op jit(solution)/shard_map/ppermute | solution.py:29
